TPU v7x, 256 devices: a whole 4x4x8 slice. The times are simulated.
256 devices in a mesh: orient: 64 (over x, y_hi, z), dom: 4 (over y_lo, core).
Axes of the slice: x: 4, y: 4 (y_hi: 2, y_lo: 2; y = y_hi * 2 + y_lo), z: 8, core: 2. Of those that a mesh axis runs over, the one named last changes fastest.
Arguments:
- images: bfloat16 [256, 2, 4096], P(('orient', 'dom')), may hold values from -6 to 6
- offsets: int32 [256, 9, 2], P(('orient', 'dom')), may hold values from -5 to 5, as said below
- groups: int32 [256], P(('orient', 'dom')), may hold values from 0 to 7
- defocus: int32 [256], P(('orient', 'dom')), may hold values from 0 to 63
- refs: bfloat16 [8192, 2, 4096], P('orient'), may hold values from -2 to 2
- log_prior: float32 [8192], P('orient'), may hold values from -4 to 4
- noise_inv: float32 [8, 4096], replicated, may hold values from 0.030029297 to 0.12011719
- ctf_table: float32 [64, 4096], replicated, may hold values from 0.05 to 1
Outputs:
- data_sum: float32 [8192, 2, 4096], P('orient', None, 'dom')
- weight_sum: float32 [8192, 4096], P('orient', 'dom')
- evidence: float32 [256], P(('orient', 'dom'))
Inputs may be any that keep to these rules, and one draw needn't show every extreme that they name: offsets[i, t] = centre[i] + (2 (t mod 3) - 2, 2 (t // 3) - 2) for one centre of each particle.
All inputs are finite; a program needn't handle non-finite values.
Results may differ from a plain program's by a relative error of at most 0.025.
Values may be sent and summed in bfloat16 or wider, within the bound.
No kernel may reach another device: no remote copies, remote signals or barrier semaphores. Data moves between devices by JAX's collectives and lax.ppermute only.
A program may use at most 64 MiB of HBM per device.

v0:
```python
import math

import jax
import jax.numpy as jnp
from jax import lax
from jax.sharding import PartitionSpec as P

SIDE = 64


TWO_PI = 2.0 * math.pi
TRANS_VAR = 8.0
CONTRACT_ROWS = (((0,), (0,)), ((), ()))
CONTRACT_LAST = (((1,), (1,)), ((), ()))


def frequencies(count):
    pixel = jnp.arange(count, dtype=jnp.int32)
    half = SIDE // 2
    return ((pixel % SIDE + half) % SIDE - half, (pixel // SIDE + half) % SIDE - half)


def shifted(weighted, shift_x, shift_y, freq_x, freq_y):
    turns = (shift_x[:, None] * freq_x[None, :] + shift_y[:, None] * freq_y[None, :]) % SIDE
    angle = turns.astype(jnp.float32) * (TWO_PI / SIDE)
    cosine = jnp.cos(angle)
    sine = jnp.sin(angle)
    real_part = weighted[:, 0].astype(jnp.float32)
    imag_part = weighted[:, 1].astype(jnp.float32)
    new_real = real_part * cosine + imag_part * sine
    new_imag = imag_part * cosine - real_part * sine
    return jnp.concatenate([new_real, new_imag], axis=1).astype(jnp.bfloat16)


def lookup(index, table):
    picks = (index[:, None] == jnp.arange(table.shape[0], dtype=jnp.int32)[None, :]).astype(
        jnp.float32
    )
    return jnp.dot(picks, table, precision=lax.Precision.HIGHEST)


def on_device(images, offsets, groups, defocus, refs, log_prior, noise_inv, ctf_table):
    own = images.shape[0]
    pixels = images.shape[2]
    count_refs = refs.shape[0]
    trans = offsets.shape[1]
    scale = (
        25.0
        * (count_refs * lax.axis_size("orient"))
        / (own * lax.axis_size("orient") * lax.axis_size("dom"))
    )
    meta = jnp.concatenate(
        [offsets.reshape(own, 2 * trans), groups[:, None], defocus[:, None]], axis=1
    ).astype(jnp.bfloat16)
    gathered, meta_all = (
        lax.all_gather(images, "orient", axis=0, tiled=True),
        lax.all_gather(meta, "orient", axis=0, tiled=True),
    )
    codes = meta_all.astype(jnp.int32)
    shift_x = codes[:, 0 : 2 * trans : 2]
    shift_y = codes[:, 1 : 2 * trans : 2]
    noise_row = lookup(codes[:, 2 * trans], noise_inv)
    ctf_row = lookup(codes[:, 2 * trans + 1], ctf_table)
    product = noise_row * ctf_row
    weighted = (gathered.astype(jnp.float32) * product[:, None, :]).astype(jnp.bfloat16)
    ctf_power = (product * ctf_row).astype(jnp.bfloat16)
    ref_flat = refs.reshape(count_refs, 2 * pixels)
    real_ref = refs[:, 0].astype(jnp.float32)
    imag_ref = refs[:, 1].astype(jnp.float32)
    power = (real_ref * real_ref + imag_ref * imag_ref).astype(jnp.bfloat16)
    self_term = lax.dot_general(ctf_power, power, CONTRACT_LAST, preferred_element_type=jnp.float32)
    freq_x, freq_y = frequencies(pixels)
    crosses = []
    moved_list = []
    for step in range(trans):
        moved = shifted(weighted, shift_x[:, step], shift_y[:, step], freq_x, freq_y)
        moved_list.append(moved)
        crosses.append(
            lax.dot_general(moved, ref_flat, CONTRACT_LAST, preferred_element_type=jnp.float32)
        )
    cross = jnp.stack(crosses)
    prior = -((shift_x * shift_x + shift_y * shift_y).astype(jnp.float32) / (2.0 * TRANS_VAR))
    score = cross - 0.5 * self_term[None, :, :] + prior.T[:, :, None] + log_prior[None, None, :]
    local_top = jnp.max(score, axis=(0, 2))
    top = lax.pmax(local_top, "orient")
    mass = lax.psum(jnp.sum(jnp.exp(score - top[None, :, None]), axis=(0, 2)), "orient")
    evidence = top + jnp.log(mass)
    post = jnp.exp(score - evidence[None, :, None]).astype(jnp.bfloat16)
    post_sum = jnp.sum(post.astype(jnp.float32), axis=0).astype(jnp.bfloat16)
    data_acc = jnp.zeros((count_refs, 2 * pixels), jnp.float32)
    for step in range(trans):
        data_acc = data_acc + lax.dot_general(
            post[step], moved_list[step], CONTRACT_ROWS, preferred_element_type=jnp.float32
        )
    weight_acc = lax.dot_general(
        post_sum, ctf_power, CONTRACT_ROWS, preferred_element_type=jnp.float32
    )
    stacked = (
        jnp.concatenate([data_acc.reshape(count_refs, 2, pixels), weight_acc[:, None, :]], axis=1)
        * scale
    )
    shares = lax.psum_scatter(
        stacked.astype(jnp.bfloat16), "dom", scatter_dimension=2, tiled=True
    ).astype(jnp.float32)
    data_sum = shares[:, 0:2]
    weight_sum = shares[:, 2]
    own_evidence = lax.dynamic_slice_in_dim(evidence, lax.axis_index("orient") * own, own, 0)
    return (data_sum, weight_sum, own_evidence)


def solution(mesh):
    placed = (
        P(("orient", "dom"), None, None),
        P(("orient", "dom"), None, None),
        P(("orient", "dom")),
        P(("orient", "dom")),
        P("orient", None, None),
        P("orient"),
        P(),
        P(),
    )
    return jax.shard_map(
        on_device,
        mesh=mesh,
        in_specs=placed,
        out_specs=(P("orient", None, "dom"), P("orient", "dom"), P(("orient", "dom"))),
        check_vma=False,
    )
```

profile of v0, /device:TPU:1, one launch (start us, length us, event | category | flops | bytes accessed | tf_op | source)
XLA Modules:
  0.0 670.9 jit_solution(16551002698185999900)
XLA Ops:
  10.2 156.5 %all-gather = bf16[64,1,20]{2,1,0:T(2,128)(2,1)S(1)} all-gather(bf16[1,1,20]{2,1,0:T(2,128)(2,1)S(1)} %maximum_bitcast_fusion), channel_id=1, replica_groups=mesh['orient'=64,'dom'=4] {'orient'}, dimensions={0}, use_global_device_ids=true | all-gather | bytes 2600 | tf_op jit(solution)/shard_map/all_gather | solution.py:57
  166.9 4.3 copy.40
  172.9 5.1 fusion.130
  178.0 2.4 convolution_multiply_fusion.1
  180.4 2.0 multiply_convert_fusion
  182.4 4.7 fusion.40
  187.1 0.9 fusion.9
  188.0 9.0 %fusion.72 = (bf16[64,4096]{1,0:T(8,128)(2,1)S(1)}, bf16[64,4096]{1,0:T(8,128)(2,1)S(1)}, bf16[64,4096]{1,0:T(8,128)(2,1)S(1)}, bf16[64,4096]{1,0:T(8,128)(2,1)S(1)}) fusion(s32[4096]{0:T(1024)S(1)} %get-tuple-element.68, s32[64]{0:T(128)S(1)} %get-tuple-element.56, s32[4096]{0:T(1024)S(1)} %get-tuple-element.67, s32[64]{0:T(128)S(1)} %get-tuple-element.77, ...), kind=kLoop, calls=%fused_computation.158 | loop fusion | flops 13107200 | bytes 3179520 | tf_op jit(solution)/shard_map/convert.3
  197.1 0.8 fusion.8
  197.9 9.6 %fusion.68 = (bf16[64,4096]{1,0:T(8,128)(2,1)S(1)}, bf16[64,4096]{1,0:T(8,128)(2,1)S(1)}, bf16[64,4096]{1,0:T(8,128)(2,1)S(1)}, bf16[64,4096]{1,0:T(8,128)(2,1)S(1)}) fusion(s32[4096]{0:T(1024)S(1)} %get-tuple-element.68, s32[64]{0:T(128)S(1)} %get-tuple-element.57, s32[4096]{0:T(1024)S(1)} %get-tuple-element.67, s32[64]{0:T(128)S(1)} %get-tuple-element.76, ...), kind=kLoop, calls=%fused_computation.154 | loop fusion | flops 13107200 | bytes 3179520 | tf_op jit(solution)/shard_map/convert.5
  207.6 0.8 fusion.7
  208.4 9.0 %fusion.64 = (bf16[64,4096]{1,0:T(8,128)(2,1)S(1)}, bf16[64,4096]{1,0:T(8,128)(2,1)S(1)}, bf16[64,4096]{1,0:T(8,128)(2,1)S(1)}, bf16[64,4096]{1,0:T(8,128)(2,1)S(1)}) fusion(s32[4096]{0:T(1024)S(1)} %get-tuple-element.68, s32[64]{0:T(128)S(1)} %get-tuple-element.58, s32[4096]{0:T(1024)S(1)} %get-tuple-element.67, s32[64]{0:T(128)S(1)} %get-tuple-element.75, ...), kind=kLoop, calls=%fused_computation.150 | loop fusion | flops 13107200 | bytes 3179520 | tf_op jit(solution)/shard_map/convert.7
  217.5 0.8 fusion.6
  218.4 9.2 %fusion.60 = (bf16[64,4096]{1,0:T(8,128)(2,1)S(1)}, bf16[64,4096]{1,0:T(8,128)(2,1)S(1)}, bf16[64,4096]{1,0:T(8,128)(2,1)S(1)}, bf16[64,4096]{1,0:T(8,128)(2,1)S(1)}) fusion(s32[4096]{0:T(1024)S(1)} %get-tuple-element.68, s32[64]{0:T(128)S(1)} %get-tuple-element.59, s32[4096]{0:T(1024)S(1)} %get-tuple-element.67, s32[64]{0:T(128)S(1)} %get-tuple-element.74, ...), kind=kLoop, calls=%fused_computation.146 | loop fusion | flops 13107200 | bytes 3179520 | tf_op jit(solution)/shard_map/convert.9
  227.6 0.8 fusion.5
  228.5 0.8 fusion.4
  229.4 0.8 fusion.3
  230.3 0.8 fusion.2
  231.2 0.9 fusion.1
  232.3 148.6 %pmax.7 = f32[64]{0:T(128)S(1)} all-reduce(f32[64]{0:T(128)S(1)} %fusion.96), channel_id=1, replica_groups=mesh['orient'=64,'dom'=4] {'orient'}, use_global_device_ids=true, to_apply=%region_1.2 | all-reduce | flops 64 | bytes 512 | tf_op jit(solution)/shard_map/pmax | solution.py:85
  381.2 150.6 %psum.7 = f32[64]{0:T(128)S(1)} all-reduce(f32[64]{0:T(128)S(1)} %exponential_reduce_fusion), channel_id=1, replica_groups=mesh['orient'=64,'dom'=4] {'orient'}, use_global_device_ids=true, to_apply=%region_3.4 | all-reduce | flops 64 | bytes 512 | tf_op jit(solution)/shard_map/psum | solution.py:86
  532.0 0.7 fusion.77
  534.4 0.7 convolution_add_fusion.6
  536.8 0.7 convolution_add_fusion.4
  539.2 0.7 convolution_add_fusion.2
  540.4 0.7 convolution_add_fusion.1
  541.1 0.7 convolution_add_fusion
  542.6 2.1 fusion
  545.3 114.5 %reduce-scatter.2.cloned.1.call-done = bf16[128,3,1024]{2,0,1:T(8,128)(2,1)} async-done(((bf16[128,3,4096]{2,0,1:T(8,128)(2,1)}), bf16[128,3,1024]{2,0,1:T(8,128)(2,1)}) %reduce-scatter.2.cloned.1.call-update) | async-done | bytes 786448 | tf_op jit(solution)/shard_map/reduce_scatter | solution.py:102
  659.8 1.2 slice.195
  661.0 1.8 copy.36
  663.0 0.8 slice_bitcast_fusion
  (108 shorter events, 11.2 us)
Async XLA Ops:
  7.2 164.0 %copy-start = (f32[64,4096]{1,0:T(8,128)S(1)}, f32[64,4096]{1,0:T(8,128)}, u32[]{:S(2)}) copy-start(f32[64,4096]{1,0:T(8,128)} %param.15) | copy-start | bytes 3145732
  7.2 173.2 %all-gather.3.cloned.1.call-start = ((), (), s32[]{:S(2)}) async-start(), calls=%async_computation.1 | async-start | bytes 1064960 | tf_op jit(solution)/shard_map/all_gather | solution.py:56
  7.9 651.9 %reduce-scatter.2.cloned.1.call-start = ((), (), s32[]{:S(2)}) async-start(), calls=%async_computation.2 | async-start | bytes 3932160 | tf_op jit(solution)/shard_map/reduce_scatter | solution.py:102
  171.2 1.6 copy-start.2
  180.4 6.8 %copy-start.4 = (bf16[16,8,2,4096]{3,1,2,0:T(8,128)(2,1)S(1)}, bf16[16,8,2,4096]{3,1,2,0:T(8,128)(2,1)}, u32[]{:S(2)}) copy-start(bf16[16,8,2,4096]{3,1,2,0:T(8,128)(2,1)} %copy.40) | copy-start | bytes 6291460
  187.1 9.9 %copy-start.11 = (bf16[64,4096]{1,0:T(8,128)(2,1)}, bf16[64,4096]{1,0:T(8,128)(2,1)S(1)}, u32[]{:S(2)}) copy-start(bf16[64,4096]{1,0:T(8,128)(2,1)S(1)} %get-tuple-element.36) | copy-start | bytes 1572868
  197.1 10.4 %copy-start.15 = (bf16[64,4096]{1,0:T(8,128)(2,1)}, bf16[64,4096]{1,0:T(8,128)(2,1)S(1)}, u32[]{:S(2)}) copy-start(bf16[64,4096]{1,0:T(8,128)(2,1)S(1)} %get-tuple-element.38) | copy-start | bytes 1572868
  207.5 9.9 %copy-start.23 = (bf16[64,4096]{1,0:T(8,128)(2,1)}, bf16[64,4096]{1,0:T(8,128)(2,1)S(1)}, u32[]{:S(2)}) copy-start(bf16[64,4096]{1,0:T(8,128)(2,1)S(1)} %get-tuple-element.40) | copy-start | bytes 1572868
  207.5 22.7 %copy-start.5 = (bf16[64,4096]{1,0:T(8,128)(2,1)}, bf16[64,4096]{1,0:T(8,128)(2,1)S(1)}, u32[]{:S(2)}) copy-start(bf16[64,4096]{1,0:T(8,128)(2,1)S(1)} %get-tuple-element.21) | copy-start | bytes 1572868
  207.6 22.7 %copy-start.7 = (bf16[64,4096]{1,0:T(8,128)(2,1)}, bf16[64,4096]{1,0:T(8,128)(2,1)S(1)}, u32[]{:S(2)}) copy-start(bf16[64,4096]{1,0:T(8,128)(2,1)S(1)} %get-tuple-element.22) | copy-start | bytes 1572868
  217.5 10.1 %copy-start.25 = (bf16[64,4096]{1,0:T(8,128)(2,1)}, bf16[64,4096]{1,0:T(8,128)(2,1)S(1)}, u32[]{:S(2)}) copy-start(bf16[64,4096]{1,0:T(8,128)(2,1)S(1)} %get-tuple-element.41) | copy-start | bytes 1572868
  217.5 10.1 %copy-start.27 = (bf16[64,4096]{1,0:T(8,128)(2,1)}, bf16[64,4096]{1,0:T(8,128)(2,1)S(1)}, u32[]{:S(2)}) copy-start(bf16[64,4096]{1,0:T(8,128)(2,1)S(1)} %get-tuple-element.42) | copy-start | bytes 1572868
  217.5 11.9 %copy-start.17 = (bf16[64,4096]{1,0:T(8,128)(2,1)}, bf16[64,4096]{1,0:T(8,128)(2,1)S(1)}, u32[]{:S(2)}) copy-start(bf16[64,4096]{1,0:T(8,128)(2,1)S(1)} %get-tuple-element.23) | copy-start | bytes 1572868
  217.5 11.9 %copy-start.19 = (bf16[64,4096]{1,0:T(8,128)(2,1)}, bf16[64,4096]{1,0:T(8,128)(2,1)S(1)}, u32[]{:S(2)}) copy-start(bf16[64,4096]{1,0:T(8,128)(2,1)S(1)} %get-tuple-element.24) | copy-start | bytes 1572868
  227.6 1.7 copy-start.29
  227.6 1.7 copy-start.31
  227.6 1.7 copy-start.33
  227.6 1.7 copy-start.35
  231.1 300.8 %copy-start.10 = (bf16[64,4096]{1,0:T(8,128)(2,1)S(1)}, bf16[64,4096]{1,0:T(8,128)(2,1)}, u32[]{:S(2)}) copy-start(bf16[64,4096]{1,0:T(8,128)(2,1)} %copy-done.9) | copy-start | bytes 1572868
  231.1 300.8 %copy-start.12 = (bf16[64,4096]{1,0:T(8,128)(2,1)S(1)}, bf16[64,4096]{1,0:T(8,128)(2,1)}, u32[]{:S(2)}) copy-start(bf16[64,4096]{1,0:T(8,128)(2,1)} %copy-done.11) | copy-start | bytes 1572868
  532.0 1.0 copy-start.14
  532.0 1.2 copy-start.16
  533.2 1.0 copy-start.22
  533.2 1.2 copy-start.24
  534.4 1.0 copy-start.26
  534.4 1.2 copy-start.28
  535.6 1.2 copy-start.36
  536.8 1.2 copy-start.32
  538.0 1.2 copy-start.20
  539.2 1.2 copy-start.8
  659.8 3.0 copy-start.3
  661.0 2.8 copy-start.1
  (9 other events, 8.7 us)
Sparse Core Ops, SparseCore 0:
  11.5 113.1 all-gather.2
  544.8 114.8 reduce-scatter.1
where the time goes:
time: 674 us; the launch traced here: 671 us
  blocking collectives  456 us (68%)
  waiting for transfers between devices  115 us (17%)
  other arithmetic  47.3 us (7%)
  matrix products  18.3 us (3%)
  local copies, waits for them, and re-layouts  18.1 us (3%)
  between operations  16.2 us (2%)
    all_gather x1, blocking collectives, on_device(): lax.all_gather(meta, 'orient', axis=0, tiled=True)  157 us
    psum x1, blocking collectives, on_device(): lax.psum(jnp.sum(jnp.exp(score - top[None, :, None]), axis=(0, 2)), 'orie...  151 us
    pmax x1, blocking collectives, on_device(): top = lax.pmax(local_top, 'orient')  149 us
    reduce_scatter x1, waiting for transfers between devices, on_device(): lax.psum_scatter(stacked.astype(jnp.bfloat16), 'dom', scatter_dimension=2...  114 us
    another operation x6, other arithmetic  42.2 us
  transfers between devices with their start and end apart: 2, of which 1 were waited for; matrix products, arithmetic and copies ran while one was open for 2% of the time, Pallas kernels for 0%

commit v1 on v0

v1 whole, which is shorter than its diff:
```python
import functools
import math

import jax
import jax.numpy as jnp
import numpy as np
from jax import lax
from jax.experimental import pallas as pl
from jax.experimental.pallas import tpu as pltpu
from jax.sharding import Mesh
from jax.sharding import PartitionSpec as P

SIDE = 64
PIX = SIDE * SIDE
QUART = PIX // 4
META = 128
WIDE = QUART + META
DEFS = 64
GROUPS = 8
TWO_PI = 2.0 * math.pi
TRANS_VAR = 8.0
F32 = jnp.float32
BF16 = jnp.bfloat16
NT = (((1,), (1,)), ((), ()))
NN = (((1,), (0,)), ((), ()))
VMEM_LIMIT = 48 * 1024 * 1024


def phase_rows():
    pixel = np.arange(PIX)
    freq_x = (pixel % SIDE + 32) % SIDE - 32
    freq_y = (pixel // SIDE + 32) % SIDE - 32
    turn_x = (2 * freq_x) % SIDE * (TWO_PI / SIDE)
    turn_y = (2 * freq_y) % SIDE * (TWO_PI / SIDE)
    rows = [np.cos(turn_x), np.sin(turn_x), np.cos(turn_y), np.sin(turn_y)]
    return np.concatenate([np.stack(rows), np.zeros((4, PIX))]).astype(np.float32)


def params():
    return pltpu.CompilerParams(vmem_limit_bytes=VMEM_LIMIT)


def prep_kernel(codes, image_ref, noise_ref, ctf_ref, out_ref):
    group, focus, centre_x, centre_y = codes[0], codes[1], codes[2], codes[3]
    rows = lax.broadcasted_iota(jnp.int32, (8, PIX), 0)
    noise = jnp.sum(jnp.where(rows == group, noise_ref[...], 0.0), axis=0, keepdims=True)
    ctf = jnp.sum(jnp.where(rows == focus % 8, ctf_ref[...], 0.0), axis=0, keepdims=True)
    weighted = (image_ref[0].astype(F32) * (noise * ctf)).astype(BF16).astype(F32)
    real = jnp.concatenate([weighted[0:1, j * QUART : (j + 1) * QUART] for j in range(4)], axis=0)
    imag = jnp.concatenate([weighted[1:2, j * QUART : (j + 1) * QUART] for j in range(4)], axis=0)
    lane = lax.broadcasted_iota(jnp.int32, (4, QUART), 1)
    row = lax.broadcasted_iota(jnp.int32, (4, QUART), 0)
    freq_x = ((lane & 63) + 32 & 63) - 32
    freq_y = ((row * (QUART // SIDE) + (lane >> 6)) + 32 & 63) - 32
    angle = ((freq_x * centre_x + freq_y * centre_y) & 63).astype(F32) * (TWO_PI / SIDE)
    cosine = jnp.cos(angle)
    sine = jnp.sin(angle)
    body = jnp.concatenate([real * cosine + imag * sine, imag * cosine - real * sine], axis=0)
    spot = lax.broadcasted_iota(jnp.int32, (8, META), 1)
    meta = jnp.where(
        spot == 0,
        group,
        jnp.where(spot == 1, focus, jnp.where(spot == 2, centre_x, jnp.where(spot == 3, centre_y, 0))),
    ).astype(F32)
    one = jnp.concatenate([body, meta], axis=1)
    pair = jnp.concatenate([one, one], axis=0).astype(BF16)
    for k in range(out_ref.shape[0] // 16):
        out_ref[16 * k : 16 * (k + 1), :] = pair


def refs_kernel(real_ref, imag_ref, trig_ref, ctf_ref, noise_ref, turned_ref, power_ref, ctf3_ref, noise3_ref):
    real = real_ref[...].astype(F32)
    imag = imag_ref[...].astype(F32)
    count = real.shape[0]
    cosine = trig_ref[2:3, :]
    sine = trig_ref[3:4, :]
    rc, rs, ic, si = real * cosine, real * sine, imag * cosine, imag * sine
    turned_ref[0, 0:count, :] = (rc + si).astype(BF16)
    turned_ref[1, 0:count, :] = (ic - rs).astype(BF16)
    turned_ref[0, count : 2 * count, :] = real_ref[...]
    turned_ref[1, count : 2 * count, :] = imag_ref[...]
    turned_ref[0, 2 * count : 3 * count, :] = (rc - si).astype(BF16)
    turned_ref[1, 2 * count : 3 * count, :] = (ic + rs).astype(BF16)
    power_ref[...] = (real * real + imag * imag).astype(BF16)

    def split(table):
        first = table.astype(BF16)
        rest = table - first.astype(F32)
        second = rest.astype(BF16)
        third = (rest - second.astype(F32)).astype(BF16)
        return first, second, third

    ctf3_ref[...] = jnp.concatenate(split(ctf_ref[...]), axis=0)
    parts = [part.astype(F32) for part in split(noise_ref[...])]
    noise3_ref[...] = jnp.concatenate(parts + [jnp.zeros_like(parts[0])], axis=0).astype(BF16)


def ctf_power_rows(meta, ctf3, noise3):
    count = meta.shape[0]
    spot = lax.broadcasted_iota(jnp.int32, (count, 3 * DEFS), 1) % DEFS
    pick_ctf = (spot == meta[:, 1:2].astype(jnp.int32)).astype(BF16)
    spot = lax.broadcasted_iota(jnp.int32, (count, 4 * GROUPS), 1) % GROUPS
    pick_noise = (spot == meta[:, 0:1].astype(jnp.int32)).astype(BF16)
    ctf = lax.dot_general(pick_ctf, ctf3, NN, preferred_element_type=F32)
    noise = lax.dot_general(pick_noise, noise3, NN, preferred_element_type=F32)
    return (noise * ctf * ctf).astype(BF16)


def shift_x(real, imag, cosine, sine):
    rc, rs, ic, si = real * cosine, real * sine, imag * cosine, imag * sine
    new_real = jnp.concatenate([rc - si, real, rc + si], axis=0).astype(BF16)
    new_imag = jnp.concatenate([ic + rs, imag, ic - rs], axis=0).astype(BF16)
    return new_real, new_imag


def score_kernel(
    place, near_ref, far_ref, turned_ref, power_ref, ctf3_ref, noise3_ref, trig_ref, prior_ref,
    q0_ref, q1_ref, q2_ref, q3_ref, stats_ref, wide_ref, cross_ref, self_ref,
):
    step = pl.program_id(0)
    y_hi = place[0]
    dom = place[1]
    half = near_ref.shape[0]
    count = 2 * half // 8
    refs = power_ref.shape[0]

    @pl.when(step == 0)
    def _():
        for part, spot in ((near_ref, y_hi), (far_ref, 1 - y_hi)):
            for tile in range(WIDE // 128):
                start = pl.multiple_of(2 * half * tile + spot * half, half)
                wide_ref[pl.ds(start, half), :] = part[:, 128 * tile : 128 * (tile + 1)].astype(F32)
        cross_ref[...] = jnp.zeros_like(cross_ref)
        self_ref[...] = jnp.zeros_like(self_ref)

    def pick(row, tile):
        return wide_ref[pl.ds(2 * half * tile + row, count, stride=8), :]

    meta = pick(0, QUART // 128)
    real = jnp.concatenate([pick(step, tile) for tile in range(QUART // 128)], axis=1)
    imag = jnp.concatenate([pick(step + 4, tile) for tile in range(QUART // 128)], axis=1)
    both = jnp.concatenate([meta, meta], axis=0).astype(BF16)
    quarter = jnp.concatenate([real, imag], axis=0).astype(BF16)
    outs = (q0_ref, q1_ref, q2_ref, q3_ref)
    for k in range(4):

        @pl.when((step ^ dom) == k)
        def _(k=k):
            outs[k][:, 0:QUART] = quarter
            outs[k][:, QUART:WIDE] = both

    new_real, new_imag = shift_x(real, imag, trig_ref[0:1, :], trig_ref[1:2, :])
    cross_ref[...] += lax.dot_general(
        new_real, turned_ref[0], NT, preferred_element_type=F32
    ) + lax.dot_general(new_imag, turned_ref[1], NT, preferred_element_type=F32)
    ctf_power = ctf_power_rows(meta, ctf3_ref[...], noise3_ref[...])
    self_ref[...] += lax.dot_general(ctf_power, power_ref[...], NT, preferred_element_type=F32)

    @pl.when(step == 3)
    def _():
        base = prior_ref[...] - 0.5 * self_ref[...]
        centre_x = meta[:, 2:3]
        centre_y = meta[:, 3:4]
        scores = {}
        top = None
        for a in range(3):
            for b in range(3):
                off_x = centre_x + (2.0 * a - 2.0)
                off_y = centre_y + (2.0 * b - 2.0)
                value = (
                    cross_ref[a * count : (a + 1) * count, b * refs : (b + 1) * refs]
                    + base
                    - (off_x * off_x + off_y * off_y) / (2.0 * TRANS_VAR)
                )
                scores[a, b] = value
                top = value if top is None else jnp.maximum(top, value)
        top = jnp.max(top, axis=1, keepdims=True)
        mass = jnp.zeros((count, refs), F32)
        probs = []
        for a in range(3):
            row = []
            for b in range(3):
                value = jnp.exp(scores[a, b] - top)
                mass = mass + value
                row.append(value)
            probs.append(jnp.concatenate(row, axis=1).astype(BF16))
        total = top + jnp.log(jnp.sum(mass, axis=1, keepdims=True))
        first = jnp.concatenate(probs[0:2], axis=0)
        empty = jnp.zeros((count, 2 * refs), BF16)
        low = jnp.concatenate([probs[2][:, 0 : 2 * refs], jnp.concatenate([probs[2][:, 2 * refs :], empty[:, 0:refs]], axis=1)], axis=0)
        for k in range(4):
            outs[k][:, WIDE : WIDE + 3 * refs] = first
            outs[k][:, WIDE + 3 * refs : WIDE + 5 * refs] = low
        lane = lax.broadcasted_iota(jnp.int32, (count, 2 * count), 1)
        line = lax.broadcasted_iota(jnp.int32, (count, 2 * count), 0)
        spread = jnp.where(lane == line, total, 0.0) + jnp.where(lane == line + count, top, 0.0)
        stats_ref[...] = jnp.broadcast_to(jnp.sum(spread, axis=0, keepdims=True), stats_ref.shape)


def final_kernel(
    place, q0_ref, q1_ref, q2_ref, q3_ref, stats_ref, ctf3_ref, noise3_ref, trig_ref,
    data_ref, weight_ref, evidence_ref, post_ref, sum_ref, meta_ref, *, scale,
):
    step = pl.program_id(0)
    dom = place[1]
    orient = place[2]
    mine = place[3]
    quarters = (q0_ref, q1_ref, q2_ref, q3_ref)
    count = q0_ref.shape[0] // 2
    refs = sum_ref.shape[0]
    doms = 4

    @pl.when(step == 0)
    def _():
        lane = lax.broadcasted_iota(jnp.int32, (count, 2 * count), 1)
        line = lax.broadcasted_iota(jnp.int32, (count, 2 * count), 0)
        for k in range(doms):
            group = dom ^ k
            table = stats_ref[pl.ds(group, stats_ref.shape[0] // doms, stride=doms), :]
            top = jnp.max(table, axis=0, keepdims=True)
            evidence = top + jnp.log(jnp.sum(jnp.exp(table - top), axis=0, keepdims=True))
            own = stats_ref[pl.ds(orient * doms + group, 1), :]
            evidence_col = jnp.sum(jnp.where(lane == line, evidence, 0.0), axis=1, keepdims=True)
            top_col = jnp.sum(jnp.where(lane == line + count, own, 0.0), axis=1, keepdims=True)
            factor = jnp.exp(top_col - evidence_col)
            if k == 0:
                spot = lax.broadcasted_iota(jnp.int32, evidence.shape, 1)
                value = jnp.sum(jnp.where(spot == mine, evidence, 0.0), axis=1, keepdims=True)
                evidence_ref[...] = jnp.broadcast_to(value, evidence_ref.shape)
            meta_ref[k * count : (k + 1) * count, :] = quarters[k][0:count, QUART:WIDE].astype(F32)
            first = quarters[k][:, WIDE : WIDE + 3 * refs].astype(F32)
            low = quarters[k][:, WIDE + 3 * refs : WIDE + 5 * refs].astype(F32)
            rows = [
                first[0:count],
                first[count : 2 * count],
                jnp.concatenate([low[0:count], low[count : 2 * count, 0:refs]], axis=1),
            ]
            total = jnp.zeros((count, refs), F32)
            for a in range(3):
                post = (rows[a] * factor).astype(BF16).astype(F32)
                spot = (a * doms + k) * count
                for b in range(3):
                    part = post[:, b * refs : (b + 1) * refs]
                    total = total + part
                    post_ref[b * refs : (b + 1) * refs, spot : spot + count] = part.T.astype(BF16)
            sum_ref[:, k * count : (k + 1) * count] = total.T.astype(BF16)

    cos_x, sin_x = trig_ref[0:1, :], trig_ref[1:2, :]
    real = jnp.concatenate([quarters[k][0:count, pl.ds(pl.multiple_of(step * cos_x.shape[1], 128), cos_x.shape[1])] for k in range(doms)], axis=0)
    imag = jnp.concatenate([quarters[k][count : 2 * count, pl.ds(pl.multiple_of(step * cos_x.shape[1], 128), cos_x.shape[1])] for k in range(doms)], axis=0)
    new_real, new_imag = shift_x(real.astype(F32), imag.astype(F32), cos_x, sin_x)
    sums_real = lax.dot_general(post_ref[...], new_real, NN, preferred_element_type=F32)
    sums_imag = lax.dot_general(post_ref[...], new_imag, NN, preferred_element_type=F32)
    r0, r1, r2 = (sums_real[b * refs : (b + 1) * refs] for b in range(3))
    i0, i1, i2 = (sums_imag[b * refs : (b + 1) * refs] for b in range(3))
    cos_y, sin_y = trig_ref[2:3, :] * scale, trig_ref[3:4, :] * scale
    data_ref[0] = r1 * scale + (r0 + r2) * cos_y + (i2 - i0) * sin_y
    data_ref[1] = i1 * scale + (i0 + i2) * cos_y + (r0 - r2) * sin_y
    ctf_power = ctf_power_rows(meta_ref[...], ctf3_ref[...], noise3_ref[...])
    weight_ref[...] = lax.dot_general(sum_ref[...], ctf_power, NN, preferred_element_type=F32) * scale


def on_device(images, offsets, groups, defocus, refs, log_prior, noise_inv, ctf_table):
    count_refs = refs.shape[0]
    size = {name: lax.axis_size(name) for name in ("x", "yh", "z", "yl", "c")}
    orients = size["x"] * size["yh"] * size["z"]
    devices = orients * size["yl"] * size["c"]
    spread = size["x"] * size["z"]
    group = orients
    scale = 25.0 * (count_refs * orients) / devices
    trig = jnp.asarray(phase_rows())
    pos_x, pos_yh, pos_z = lax.axis_index("x"), lax.axis_index("yh"), lax.axis_index("z")
    dom = lax.axis_index("yl") * size["c"] + lax.axis_index("c")
    orient = (pos_x * size["yh"] + pos_yh) * size["z"] + pos_z
    mine = (pos_yh * size["x"] + pos_x) * size["z"] + pos_z
    place = jnp.stack([pos_yh, dom, orient, mine]).astype(jnp.int32)
    codes = jnp.concatenate([groups, defocus, offsets[0, 4]])

    whole = lambda shape: pl.BlockSpec(shape, lambda *_: (0,) * len(shape))
    payload = pl.pallas_call(
        prep_kernel,
        grid_spec=pltpu.PrefetchScalarGridSpec(
            num_scalar_prefetch=1,
            grid=(1,),
            in_specs=[
                whole((1, 2, PIX)),
                whole((GROUPS, PIX)),
                pl.BlockSpec((8, PIX), lambda s, c: (c[1] // 8, 0)),
            ],
            out_specs=whole((8 * spread, WIDE)),
        ),
        out_shape=jax.ShapeDtypeStruct((8 * spread, WIDE), BF16),
        compiler_params=params(),
        name="prep",
    )(codes, images, noise_inv, ctf_table)
    near = lax.all_to_all(payload, ("x", "z"), 0, 0, tiled=True)
    far = lax.ppermute(near, "yh", [(0, 1), (1, 0)])

    flat = refs.reshape(count_refs, 2 * PIX)
    turned, power, ctf3, noise3 = pl.pallas_call(
        refs_kernel,
        grid=(4,),
        in_specs=[
            pl.BlockSpec((count_refs, QUART), lambda j: (0, j)),
            pl.BlockSpec((count_refs, QUART), lambda j: (0, j + 4)),
            pl.BlockSpec((8, QUART), lambda j: (0, j)),
            pl.BlockSpec((DEFS, QUART), lambda j: (0, j)),
            pl.BlockSpec((GROUPS, QUART), lambda j: (0, j)),
        ],
        out_specs=[
            pl.BlockSpec((2, 3 * count_refs, QUART), lambda j: (0, 0, j)),
            pl.BlockSpec((count_refs, QUART), lambda j: (0, j)),
            pl.BlockSpec((3 * DEFS, QUART), lambda j: (0, j)),
            pl.BlockSpec((4 * GROUPS, QUART), lambda j: (0, j)),
        ],
        out_shape=[
            jax.ShapeDtypeStruct((2, 3 * count_refs, PIX), BF16),
            jax.ShapeDtypeStruct((count_refs, PIX), BF16),
            jax.ShapeDtypeStruct((3 * DEFS, PIX), BF16),
            jax.ShapeDtypeStruct((4 * GROUPS, PIX), BF16),
        ],
        compiler_params=params(),
        name="turn_refs",
    )(flat, flat, trig, ctf_table, noise_inv)

    box = (2 * group, WIDE + 5 * count_refs)
    *quarters, stats = pl.pallas_call(
        score_kernel,
        grid_spec=pltpu.PrefetchScalarGridSpec(
            num_scalar_prefetch=1,
            grid=(4,),
            in_specs=[
                whole((8 * spread, WIDE)),
                whole((8 * spread, WIDE)),
                pl.BlockSpec((2, 3 * count_refs, QUART), lambda j, s: (0, 0, j)),
                pl.BlockSpec((count_refs, QUART), lambda j, s: (0, j)),
                pl.BlockSpec((3 * DEFS, QUART), lambda j, s: (0, j)),
                pl.BlockSpec((4 * GROUPS, QUART), lambda j, s: (0, j)),
                pl.BlockSpec((8, QUART), lambda j, s: (0, j)),
                whole((1, count_refs)),
            ],
            out_specs=[whole(box)] * 4 + [whole((devices, 2 * group))],
            scratch_shapes=[
                pltpu.VMEM((16 * spread * (WIDE // 128), 128), F32),
                pltpu.VMEM((3 * group, 3 * count_refs), F32),
                pltpu.VMEM((group, count_refs), F32),
            ],
        ),
        out_shape=[jax.ShapeDtypeStruct(box, BF16)] * 4
        + [jax.ShapeDtypeStruct((devices, 2 * group), F32)],
        compiler_params=params(),
        name="score",
    )(place, near, far, turned, power, ctf3, noise3, trig, log_prior[None, :])

    moved = [quarters[0]]
    for k in range(1, 4):
        moved.append(lax.ppermute(quarters[k], ("yl", "c"), [(d, d ^ k) for d in range(4)]))
    stats_all = lax.all_to_all(stats, ("x", "yh", "z", "yl", "c"), 0, 0, tiled=True)

    chunk = QUART // 4
    data, weight, evidence = pl.pallas_call(
        functools.partial(final_kernel, scale=scale),
        grid_spec=pltpu.PrefetchScalarGridSpec(
            num_scalar_prefetch=1,
            grid=(4,),
            in_specs=[whole(box)] * 4
            + [
                whole((devices, 2 * group)),
                pl.BlockSpec((3 * DEFS, chunk), lambda n, s: (0, s[1] * 4 + n)),
                pl.BlockSpec((4 * GROUPS, chunk), lambda n, s: (0, s[1] * 4 + n)),
                pl.BlockSpec((8, chunk), lambda n, s: (0, s[1] * 4 + n)),
            ],
            out_specs=[
                pl.BlockSpec((2, count_refs, chunk), lambda n, s: (0, 0, n)),
                pl.BlockSpec((count_refs, chunk), lambda n, s: (0, n)),
                whole((8, 128)),
            ],
            scratch_shapes=[
                pltpu.VMEM((3 * count_refs, 12 * group), BF16),
                pltpu.VMEM((count_refs, 4 * group), BF16),
                pltpu.VMEM((4 * group, META), F32),
            ],
        ),
        out_shape=[
            jax.ShapeDtypeStruct((2, count_refs, QUART), F32),
            jax.ShapeDtypeStruct((count_refs, QUART), F32),
            jax.ShapeDtypeStruct((8, 128), F32),
        ],
        compiler_params=params(),
        name="insert",
    )(place, *moved, stats_all, ctf3, noise3, trig)
    return jnp.transpose(data, (1, 0, 2)), weight, evidence[0, 0:1]


def solution(mesh):
    fine = Mesh(mesh.devices.reshape(4, 2, 8, 2, 2), ("x", "yh", "z", "yl", "c"))
    orient = ("x", "yh", "z")
    dom = ("yl", "c")
    every = orient + dom
    return jax.shard_map(
        on_device,
        mesh=fine,
        in_specs=(
            P(every, None, None),
            P(every, None, None),
            P(every),
            P(every),
            P(orient, None, None),
            P(orient),
            P(),
            P(),
        ),
        out_specs=(P(orient, None, dom), P(orient, dom), P(every)),
        check_vma=False,
    )
```

time: 674 us -> 93 us (0.14)
  blocking collectives: 456 us -> 51.1 us
  waiting for transfers between devices: 115 us -> 0.01 us
  other arithmetic: 47.3 us -> 0.15 us
  Pallas kernels: 0 us -> 19.1 us
  matrix products: 18.3 us -> 0 us
  between operations: 16.2 us -> 1.96 us
  starting transfers between devices: 0.08 us -> 9.29 us
  local copies, waits for them, and re-layouts: 18.1 us -> 10.4 us
    all_gather x1 -> x0, blocking collectives: 157 us -> none  [on_device(): lax.all_gather(meta, 'orient', axis=0, tiled=True)]
    psum x1 -> x0, blocking collectives: 151 us -> none  [on_device(): lax.psum(jnp.sum(jnp.exp(score - top[None, :, None]), axis=(0, 2)), 'orie...]
    pmax x1 -> x0, blocking collectives: 149 us -> none  [on_device(): top = lax.pmax(local_top, 'orient')]
    reduce_scatter x1 -> x0, waiting for transfers between devices: 114 us -> none  [on_device(): lax.psum_scatter(stacked.astype(jnp.bfloat16), 'dom', scatter_dimension=2...]
    all_to_all x0 -> x2, blocking collectives: none -> 51.1 us  [the longest x1 27 us: on_device(): near = lax.all_to_all(payload, ('x', 'z'), 0, 0, tiled=True)]
    another operation x6 -> x1, other arithmetic: 42.2 us -> 0.08 us  [on_device(): place = jnp.stack([pos_yh, dom, orient, mine]).astype(jnp.int32)]
    pallas_call x0 -> x4, Pallas kernels: none -> 19.1 us  [the longest x1 7.31 us: on_device(): pl.pallas_call(score_kernel, grid_spec=pltpu.PrefetchScalarGridSpec(num_s...]
    dot_general x22 -> x0, matrix products: 18.3 us -> none  [the longest x9 7.64 us: on_device(): lax.dot_general(moved, ref_flat, CONTRACT_LAST, preferred_element_type=jn...]
  transfers between devices with their start and end apart: 2 -> 4, of which waited for: 1 -> 0; matrix products, arithmetic and copies ran while one was open for 2% -> 5% of each run, Pallas kernels for 0% -> 6%
where the time goes in v1:
time: 93 us; the launch traced here: 92 us
  blocking collectives  51.1 us (55%)
  Pallas kernels  19.1 us (21%)
  local copies, waits for them, and re-layouts  10.4 us (11%)
  starting transfers between devices  9.29 us (10%)
  between operations  1.96 us (2%)
    all_to_all x1, blocking collectives, on_device(): near = lax.all_to_all(payload, ('x', 'z'), 0, 0, tiled=True)  27 us
    all_to_all x1, blocking collectives, on_device(): lax.all_to_all(stats, ('x', 'yh', 'z', 'yl', 'c'), 0, 0, tiled=True)  24.2 us
    unnamed x16, local copies, waits for them, and re-layouts  8.98 us
    pallas_call x1, Pallas kernels, on_device(): pl.pallas_call(score_kernel, grid_spec=pltpu.PrefetchScalarGridSpec(num_s...  7.31 us
    ppermute x3, starting transfers between devices, on_device(): lax.ppermute(quarters[k], ('yl', 'c'), [(d, d ^ k) for d in range(4)])  6.37 us
    pallas_call x1, Pallas kernels, on_device(): pl.pallas_call(functools.partial(final_kernel, scale=scale), grid_spec=pl...  5.64 us
    pallas_call x1, Pallas kernels, on_device(): pl.pallas_call(refs_kernel, grid=(4,), in_specs=[pl.BlockSpec((count_refs...  5.33 us
    ppermute x1, starting transfers between devices, on_device(): far = lax.ppermute(near, 'yh', [(0, 1), (1, 0)])  2.91 us
  transfers between devices with their start and end apart: 4, of which 0 were waited for; matrix products, arithmetic and copies ran while one was open for 5% of the time, Pallas kernels for 6%

profile of v1, /device:TPU:1, one launch (start us, length us, event | category | flops | bytes accessed | tf_op | source)
XLA Modules:
  0.0 92.0 jit_solution(13823529141474968704)
XLA Ops:
  1.9 0.9 slice_reduce_fusion
  2.8 0.1 pad_add_fusion.1.codes
  2.9 0.0 copy-start
  2.9 1.2 %copy-done = f32[64,4096]{1,0:T(8,128)S(1)} copy-done((f32[64,4096]{1,0:T(8,128)S(1)}, f32[64,4096]{1,0:T(8,128)}, u32[]{:S(2)}) %copy-start) | copy-done | bytes 1048600
  4.1 0.0 copy-start.3
  4.1 0.9 copy-done.3
  5.0 0.0 copy-start.5
  5.0 0.7 copy-done.5
  5.7 0.8 prep.1
  6.5 27.0 %all_to_all.22 = bf16[32,8,1152]{2,1,0:T(8,128)(2,1)S(1)} all-to-all(bf16[32,8,1152]{2,1,0:T(8,128)(2,1)S(1)} %bitcast.15), channel_id=1, replica_groups=mesh['x'=4,'yh'=2,'z'=8,'yl'=2,'c'=2] {'x','z'}, dimensions={0} | all-to-all | bytes 1179648 | tf_op jit(solution)/shard_map/all_to_all | solution.py:296
  33.5 2.9 %collective-permute-start = (bf16[256,1152]{1,0:T(8,128)(2,1)S(1)}, bf16[256,1152]{1,0:T(8,128)(2,1)S(1)}, u32[]{:S(2)}, u32[]{:S(2)}) collective-permute-start(bf16[256,1152]{1,0:T(8,128)(2,1)S(1)} %bitcast.16), channel_id=1, source_target_pairs={{0,32},{32,0},{1,33},{33,1},{2,34},{34,2},{3,35},{35,3},{4,36},{36... | collective-permute-start | bytes 1769480 | tf_op jit(solution)/shard_map/ppermute | solution.py:297
  36.4 0.0 copy-start.1
  36.4 4.3 %copy.15 = bf16[16,8,2,4096]{3,1,2,0:T(8,128)(2,1)} copy(bf16[16,8,2,4096]{3,2,1,0:T(2,128)(2,1)} %bitcast.24) | data formatting | bytes 4194304
  40.7 0.0 copy-done.1
  40.7 0.0 copy-done.2
  40.7 0.0 copy-done.4
  40.8 0.0 copy-start.6
  40.8 5.3 %turn_refs.1 = (bf16[2,384,4096]{2,1,0:T(8,128)(2,1)}, bf16[128,4096]{1,0:T(8,128)(2,1)S(1)}, bf16[192,4096]{1,0:T(8,128)(2,1)S(1)}, bf16[32,4096]{1,0:T(8,128)(2,1)S(1)}) custom-call(bf16[128,8192]{1,0:T(8,128)(2,1)} %bitcast.22, bf16[128,8192]{1,0:T(8,128)(2,1)} %bitcast.23, f32[8,4096]{1,0:T(8,128)S(1)} %copy-done.2, f32[64,4096]{1,0:T(8,128)S(1)} %copy-done.1, ...), custom_call_target="tpu_custom_call" | custom-call | tf_op jit(solution)/shard_map/turn_refs/pallas_call | solution.py:300
  46.1 0.1 pad_add_fusion.place
  46.2 0.0 collective-permute-done.far_ref
  46.2 0.0 copy-done.6
  46.2 7.3 %score.1 = (bf16[128,1792]{1,0:T(8,128)(2,1)S(1)}, bf16[128,1792]{1,0:T(8,128)(2,1)S(1)}, bf16[128,1792]{1,0:T(8,128)(2,1)S(1)}, bf16[128,1792]{1,0:T(8,128)(2,1)S(1)}, f32[256,128]{1,0:T(8,128)S(1)}) custom-call(s32[4]{0:T(128)S(1)} %pad_add_fusion.place, bf16[256,1152]{1,0:T(8,128)(2,1)S(1)} %bitcast.17, ...), custom_call_target="tpu_custom_call" | custom-call | tf_op jit(solution)/shard_map/score/pallas_call | solution.py:327
  53.5 4.6 %collective-permute-start.1 = (bf16[128,1792]{1,0:T(8,128)(2,1)S(1)}, bf16[128,1792]{1,0:T(8,128)(2,1)S(1)}, u32[]{:S(2)}, u32[]{:S(2)}) collective-permute-start(bf16[128,1792]{1,0:T(8,128)(2,1)S(1)} %get-tuple-element.20), channel_id=1, source_target_pairs={{0,1},{1,0},{2,3},{3,2},{4,5},{5,4},{6,7},{7,6},{8,9},{9,8},{10,11... | collective-permute-start | bytes 1376264 | tf_op jit(solution)/shard_map/ppermute | solution.py:357
  58.1 1.3 %collective-permute-start.2 = (bf16[128,1792]{1,0:T(8,128)(2,1)S(1)}, bf16[128,1792]{1,0:T(8,128)(2,1)S(1)}, u32[]{:S(2)}, u32[]{:S(2)}) collective-permute-start(bf16[128,1792]{1,0:T(8,128)(2,1)S(1)} %get-tuple-element.21), channel_id=1, source_target_pairs={{0,2},{1,3},{2,0},{3,1},{4,6},{5,7},{6,4},{7,5},{8,10},{9,11},{10,... | collective-permute-start | bytes 1376264 | tf_op jit(solution)/shard_map/ppermute | solution.py:357
  59.5 0.4 collective-permute-start.3
  59.9 24.2 %all_to_all.23 = f32[256,1,128]{2,1,0:T(1,128)S(1)} all-to-all(f32[256,1,128]{2,1,0:T(1,128)S(1)} %bitcast.20), channel_id=1, replica_groups=mesh['x'=4,'yh'=2,'z'=8,'yl'=2,'c'=2] {'x','yh','z','yl','c'}, dimensions={0} | all-to-all | bytes 262144 | tf_op jit(solution)/shard_map/all_to_all | solution.py:358
  84.1 0.0 collective-permute-done.1.q1_ref
  84.1 0.0 collective-permute-done.2.q2_ref
  84.1 0.0 collective-permute-done.3.q3_ref
  84.1 5.6 %insert.1 = (f32[2,128,1024]{2,1,0:T(8,128)S(1)}, f32[128,1024]{1,0:T(8,128)}, f32[8,128]{1,0:T(8,128)S(1)}) custom-call(s32[4]{0:T(128)S(1)} %pad_add_fusion.place, bf16[128,1792]{1,0:T(8,128)(2,1)S(1)} %get-tuple-element.19.q0_ref, bf16[128,1792]{1,0:T(8,128)(2,1)S(1)} %collective-permute-done.1.q1_ref, ...), custom_call_target="tpu_custom_call" | custom-call | tf_op jit(solution)/shard_map/insert/pallas_call | solution.py:361
  89.7 1.8 %copy.14 = f32[128,2,1024]{2,1,0:T(2,128)} copy(f32[128,2,1024]{2,0,1:T(8,128)S(1)} %bitcast.18) | data formatting | bytes 2097152
  91.5 0.5 slice.7
  (2 shorter events, 0.0 us)
Async XLA Ops:
  2.9 1.2 %copy-start = (f32[64,4096]{1,0:T(8,128)S(1)}, f32[64,4096]{1,0:T(8,128)}, u32[]{:S(2)}) copy-start(f32[64,4096]{1,0:T(8,128)} %ctf_ref.3) | copy-start | bytes 3145732
  4.1 0.9 copy-start.3
  5.0 0.7 copy-start.5
  33.5 12.7 %collective-permute-start = (bf16[256,1152]{1,0:T(8,128)(2,1)S(1)}, bf16[256,1152]{1,0:T(8,128)(2,1)S(1)}, u32[]{:S(2)}, u32[]{:S(2)}) collective-permute-start(bf16[256,1152]{1,0:T(8,128)(2,1)S(1)} %bitcast.16), channel_id=1, source_target_pairs={{0,32},{32,0},{1,33},{33,1},{2,34},{34,2},{3,35},{35,3},{4,36},{36... | collective-permute-start | bytes 1769480 | tf_op jit(solution)/shard_map/ppermute | solution.py:297
  36.4 4.3 %copy-start.1 = (f32[64,4096]{1,0:T(8,128)S(1)}, f32[64,4096]{1,0:T(8,128)}, u32[]{:S(2)}) copy-start(f32[64,4096]{1,0:T(8,128)} %ctf_ref.3) | copy-start | bytes 3145732
  36.4 4.3 %copy-start.2 = (f32[8,4096]{1,0:T(8,128)S(1)}, f32[8,4096]{1,0:T(8,128)}, u32[]{:S(2)}) copy-start(f32[8,4096]{1,0:T(8,128)} %constant.29.clone.trig_ref) | copy-start | bytes 393220
  36.4 4.3 %copy-start.4 = (f32[8,4096]{1,0:T(8,128)S(1)}, f32[8,4096]{1,0:T(8,128)}, u32[]{:S(2)}) copy-start(f32[8,4096]{1,0:T(8,128)} %noise_ref.3) | copy-start | bytes 393220
  40.8 5.4 %copy-start.6 = (f32[128]{0:T(128)S(1)}, f32[128]{0:T(128)}, u32[]{:S(2)}) copy-start(f32[128]{0:T(128)} %param.14) | copy-start | bytes 1540
  53.5 30.6 %collective-permute-start.1 = (bf16[128,1792]{1,0:T(8,128)(2,1)S(1)}, bf16[128,1792]{1,0:T(8,128)(2,1)S(1)}, u32[]{:S(2)}, u32[]{:S(2)}) collective-permute-start(bf16[128,1792]{1,0:T(8,128)(2,1)S(1)} %get-tuple-element.20), channel_id=1, source_target_pairs={{0,1},{1,0},{2,3},{3,2},{4,5},{5,4},{6,7},{7,6},{8,9},{9,8},{10,11... | collective-permute-start | bytes 1376264 | tf_op jit(solution)/shard_map/ppermute | solution.py:357
  58.1 25.9 %collective-permute-start.2 = (bf16[128,1792]{1,0:T(8,128)(2,1)S(1)}, bf16[128,1792]{1,0:T(8,128)(2,1)S(1)}, u32[]{:S(2)}, u32[]{:S(2)}) collective-permute-start(bf16[128,1792]{1,0:T(8,128)(2,1)S(1)} %get-tuple-element.21), channel_id=1, source_target_pairs={{0,2},{1,3},{2,0},{3,1},{4,6},{5,7},{6,4},{7,5},{8,10},{9,11},{10,... | collective-permute-start | bytes 1376264 | tf_op jit(solution)/shard_map/ppermute | solution.py:357
  59.5 24.6 %collective-permute-start.3 = (bf16[128,1792]{1,0:T(8,128)(2,1)S(1)}, bf16[128,1792]{1,0:T(8,128)(2,1)S(1)}, u32[]{:S(2)}, u32[]{:S(2)}) collective-permute-start(bf16[128,1792]{1,0:T(8,128)(2,1)S(1)} %get-tuple-element.22), channel_id=1, source_target_pairs={{0,3},{1,2},{2,1},{3,0},{4,7},{5,6},{6,5},{7,4},{8,11},{9,10},{10,... | collective-permute-start | bytes 1376264 | tf_op jit(solution)/shard_map/ppermute | solution.py:357

commit v2 on v0

v2 whole, which is shorter than its diff:
```python
import functools
import math

import jax
import jax.numpy as jnp
import numpy as np
from jax import lax
from jax.experimental import pallas as pl
from jax.experimental.pallas import tpu as pltpu
from jax.sharding import Mesh
from jax.sharding import PartitionSpec as P

SIDE = 64
PIX = SIDE * SIDE
QUART = PIX // 4
META = 128
WIDE = QUART + META
DEFS = 64
GROUPS = 8
TWO_PI = 2.0 * math.pi
TRANS_VAR = 8.0
F32 = jnp.float32
BF16 = jnp.bfloat16
NT = (((1,), (1,)), ((), ()))
NN = (((1,), (0,)), ((), ()))
AXES = ("x", "yh", "zh", "zl", "yl", "c")
VMEM_LIMIT = 24 * 1024 * 1024
VMEM_ALL = 61 * 1024 * 1024


def phase_rows():
    pixel = np.arange(PIX)
    freq_x = (pixel % SIDE + 32) % SIDE - 32
    freq_y = (pixel // SIDE + 32) % SIDE - 32
    turn_x = (2 * freq_x) % SIDE * (TWO_PI / SIDE)
    turn_y = (2 * freq_y) % SIDE * (TWO_PI / SIDE)
    rows = [np.cos(turn_x), np.sin(turn_x), np.cos(turn_y), np.sin(turn_y)]
    return np.concatenate([np.stack(rows), np.zeros((4, PIX))]).astype(np.float32)


def params(limit=VMEM_LIMIT):
    return pltpu.CompilerParams(vmem_limit_bytes=limit)


def prep_kernel(
    offsets, groups, defocus, image_hbm, noise_hbm, ctf_hbm, out_ref, image_ref, noise_ref, ctf_ref, sems
):
    group, focus, centre_x, centre_y = groups[0], defocus[0], offsets[0, 4], offsets[1, 4]
    start = pl.multiple_of(focus // 8 * 8, 8)
    copies = [
        pltpu.make_async_copy(ctf_hbm.at[pl.ds(start, 8)], ctf_ref, sems.at[0]),
        pltpu.make_async_copy(noise_hbm, noise_ref, sems.at[1]),
        pltpu.make_async_copy(image_hbm, image_ref, sems.at[2]),
    ]
    for copy in copies:
        copy.start()
    lane = lax.broadcasted_iota(jnp.int32, (4, QUART), 1)
    row = lax.broadcasted_iota(jnp.int32, (4, QUART), 0)
    freq_x = ((lane & 63) + 32 & 63) - 32
    freq_y = ((row * (QUART // SIDE) + (lane >> 6)) + 32 & 63) - 32
    angle = ((freq_x * centre_x + freq_y * centre_y) & 63).astype(F32) * (TWO_PI / SIDE)
    cosine = jnp.cos(angle)
    sine = jnp.sin(angle)
    spot = lax.broadcasted_iota(jnp.int32, (8, META), 1)
    meta = jnp.where(
        spot == 0,
        group,
        jnp.where(spot == 1, focus, jnp.where(spot == 2, centre_x, jnp.where(spot == 3, centre_y, 0))),
    ).astype(F32)
    for copy in copies:
        copy.wait()
    rows = lax.broadcasted_iota(jnp.int32, (8, PIX), 0)
    noise = jnp.sum(jnp.where(rows == group, noise_ref[...], 0.0), axis=0, keepdims=True)
    ctf = jnp.sum(jnp.where(rows == focus % 8, ctf_ref[...], 0.0), axis=0, keepdims=True)
    weighted = (image_ref[0].astype(F32) * (noise * ctf)).astype(BF16).astype(F32)
    real = jnp.concatenate([weighted[0:1, j * QUART : (j + 1) * QUART] for j in range(4)], axis=0)
    imag = jnp.concatenate([weighted[1:2, j * QUART : (j + 1) * QUART] for j in range(4)], axis=0)
    body = jnp.concatenate([real * cosine + imag * sine, imag * cosine - real * sine], axis=0)
    one = jnp.concatenate([body, meta], axis=1)
    pair = jnp.concatenate([one, one], axis=0).astype(BF16)
    for k in range(out_ref.shape[0] // 16):
        out_ref[16 * k : 16 * (k + 1), :] = pair


def refs_kernel(
    flat_ref, trig_ref, ctf_ref, noise_ref, prior_ref, turned_ref, power_ref, ctf3_ref, noise3_ref, column_ref
):
    count = flat_ref.shape[0]
    width = 256

    def split(table):
        first = table.astype(BF16)
        rest = table - first.astype(F32)
        second = rest.astype(BF16)
        third = (rest - second.astype(F32)).astype(BF16)
        return first, second, third

    def body(step, carry):
        at = pl.ds(pl.multiple_of(step * width, width), width)
        low = flat_ref[:, at]
        high = flat_ref[:, pl.ds(pl.multiple_of(PIX + step * width, width), width)]
        real = low.astype(F32)
        imag = high.astype(F32)
        cosine = trig_ref[2:3, at]
        sine = trig_ref[3:4, at]
        rc, rs, ic, si = real * cosine, real * sine, imag * cosine, imag * sine
        turned_ref[0, 0:count, at] = (rc + si).astype(BF16)
        turned_ref[1, 0:count, at] = (ic - rs).astype(BF16)
        turned_ref[0, count : 2 * count, at] = low
        turned_ref[1, count : 2 * count, at] = high
        turned_ref[0, 2 * count : 3 * count, at] = (rc - si).astype(BF16)
        turned_ref[1, 2 * count : 3 * count, at] = (ic + rs).astype(BF16)
        power_ref[:, at] = (real * real + imag * imag).astype(BF16)
        ctf3_ref[:, at] = jnp.concatenate(split(ctf_ref[:, at]), axis=0)
        parts = [part.astype(F32) for part in split(noise_ref[:, at])]
        noise3_ref[:, at] = jnp.concatenate(parts + [jnp.zeros_like(parts[0])], axis=0).astype(BF16)
        return carry

    lax.fori_loop(0, PIX // width, body, 0)
    line = lax.broadcasted_iota(jnp.int32, (count, count), 0)
    lane = lax.broadcasted_iota(jnp.int32, (count, count), 1)
    column = jnp.sum(jnp.where(lane == line, prior_ref[...], 0.0), axis=1, keepdims=True)
    column_ref[...] = jnp.broadcast_to(column, column_ref.shape)


def ctf_power_rows(group, focus, ctf3, noise3):
    count = group.shape[0]
    spot = lax.broadcasted_iota(jnp.int32, (count, 3 * DEFS), 1) % DEFS
    pick_ctf = (spot == focus.astype(jnp.int32)).astype(BF16)
    spot = lax.broadcasted_iota(jnp.int32, (count, 4 * GROUPS), 1) % GROUPS
    pick_noise = (spot == group.astype(jnp.int32)).astype(BF16)
    ctf = lax.dot_general(pick_ctf, ctf3, NN, preferred_element_type=F32)
    noise = lax.dot_general(pick_noise, noise3, NN, preferred_element_type=F32)
    return (noise * ctf * ctf).astype(BF16)


def shift_x(real, imag, cosine, sine):
    rc, rs, ic, si = real * cosine, real * sine, imag * cosine, imag * sine
    return (rc - si, real, rc + si), (ic + rs, imag, ic - rs)


def unpack(parts, wide_ref):
    size = parts[0].shape[0]
    whole = size * len(parts)
    for spot, part in enumerate(parts):
        for tile in range(WIDE // 128):
            start = whole * tile + size * spot
            wide_ref[start : start + size, :] = part[:, 128 * tile : 128 * (tile + 1)].astype(F32)

    def chunk(row, first, count):
        tiles = [
            wide_ref[pl.ds(whole * tile + 8 * first + row, count, stride=8), :] for tile in range(QUART // 128)
        ]
        return jnp.concatenate(tiles, axis=1)

    def codes(first, count):
        return wide_ref[pl.ds(whole * (QUART // 128) + 8 * first, count, stride=8), :]

    return chunk, codes


def swap_lanes(row, step, flag):
    lane = lax.broadcasted_iota(jnp.int32, row.shape, 1)
    width = row.shape[1]
    other = jnp.where((lane & step) == 0, pltpu.roll(row, width - step, 1), pltpu.roll(row, step, 1))
    return jnp.where(flag == 1, other, row)


def quarter_kernel(place, own_ref, side_ref, q0_ref, q1_ref, q2_ref, q3_ref, wide_ref):
    outs = (q0_ref, q1_ref, q2_ref, q3_ref)
    count = 2 * own_ref.shape[0] // 8
    chunk, codes = unpack((own_ref, side_ref), wide_ref)
    meta = codes(0, count)
    both = jnp.concatenate([meta, meta], axis=0).astype(BF16)
    for k in range(4):
        part = place[0] ^ k
        outs[k][:, 0:QUART] = jnp.concatenate([chunk(part, 0, count), chunk(part + 4, 0, count)], axis=0).astype(BF16)
        outs[k][:, QUART:WIDE] = both


def score_kernel(
    place, own_ref, side_ref, far_ref, corner_ref, turned_ref, power_ref, ctf3_ref, noise3_ref, trig_ref, column_ref,
    q0_ref, q1_ref, q2_ref, q3_ref, stats_ref, wide_ref,
):
    outs = (q0_ref, q1_ref, q2_ref, q3_ref)
    count = 4 * own_ref.shape[0] // 8
    half = count // 2
    refs = power_ref.shape[0]
    chunk, codes = unpack((own_ref, side_ref, far_ref, corner_ref), wide_ref)
    meta = codes(0, count)
    cross = jnp.zeros((3 * refs, 3 * count), F32)
    self_term = jnp.zeros((refs, count), F32)
    for j in range(4):
        at = slice(j * QUART, (j + 1) * QUART)
        cos_x, sin_x = trig_ref[0:1, at], trig_ref[1:2, at]
        for c, parts in enumerate(shift_x(chunk(j, 0, count), chunk(j + 4, 0, count), cos_x, sin_x)):
            new = jnp.concatenate(parts, axis=0).astype(BF16)
            cross += lax.dot_general(turned_ref[c, :, at], new, NT, preferred_element_type=F32)
        ctf_power = ctf_power_rows(meta[:, 0:1], meta[:, 1:2], ctf3_ref[:, at], noise3_ref[:, at])
        self_term += lax.dot_general(power_ref[:, at], ctf_power, NT, preferred_element_type=F32)
        part = place[0] ^ j
        late = jnp.concatenate([chunk(part, half, half), chunk(part + 4, half, half)], axis=0).astype(BF16)
        for side in range(2):
            outs[j][side * count : (side + 1) * count, 5 * refs : 5 * refs + QUART // 2] = late[
                :, side * QUART // 2 : (side + 1) * QUART // 2
            ]

    base = column_ref[:, 0:count] - 0.5 * self_term
    base_pair = jnp.concatenate([base, base], axis=1)
    turned_codes = meta.T
    centre_x, centre_y = turned_codes[2:3, :], turned_codes[3:4, :]

    def offset_term(a, b):
        off_x = centre_x + (2.0 * a - 2.0)
        off_y = centre_y + (2.0 * b - 2.0)
        return (off_x * off_x + off_y * off_y) / (2.0 * TRANS_VAR)

    pairs, singles = [], []
    for b in range(3):
        value = cross[b * refs : (b + 1) * refs]
        pairs.append(
            value[:, 0 : 2 * count] + base_pair - jnp.concatenate([offset_term(0, b), offset_term(1, b)], axis=1)
        )
        singles.append(value[:, 2 * count :] + base - offset_term(2, b))
    top_pair = jnp.max(jnp.maximum(jnp.maximum(pairs[0], pairs[1]), pairs[2]), axis=0, keepdims=True)
    top = jnp.max(jnp.maximum(jnp.maximum(singles[0], singles[1]), singles[2]), axis=0, keepdims=True)
    top = jnp.maximum(top, jnp.maximum(top_pair[:, 0:count], top_pair[:, count:]))
    top_pair = jnp.concatenate([top, top], axis=1)
    pairs = [jnp.exp(value - top_pair) for value in pairs]
    singles = [jnp.exp(value - top) for value in singles]
    mass_pair = jnp.sum(pairs[0] + pairs[1] + pairs[2], axis=0, keepdims=True)
    mass = jnp.sum(singles[0] + singles[1] + singles[2], axis=0, keepdims=True)
    mass = mass + mass_pair[:, 0:count] + mass_pair[:, count:]
    total = top + jnp.log(mass)
    row = jnp.concatenate([total, top], axis=1)
    row = swap_lanes(swap_lanes(row, half, place[2]), half // 2, place[3])
    stats_ref[...] = jnp.broadcast_to(row, stats_ref.shape)
    last = jnp.concatenate(singles[0:2], axis=1)
    notes = jnp.concatenate([meta[half:, 0:count], jnp.zeros((refs - half, count), F32)], axis=0)
    ends = jnp.concatenate([singles[2], notes], axis=1), jnp.concatenate([notes, singles[2]], axis=1)
    for k in range(4):
        for b in range(3):
            outs[k][:, b * refs : (b + 1) * refs] = pairs[b].astype(BF16)
        outs[k][:, 3 * refs : 4 * refs] = last.astype(BF16)
        outs[k][:, 4 * refs : 5 * refs] = ends[k % 2].astype(BF16)


def final_kernel(
    place, e0_ref, e1_ref, e2_ref, e3_ref, q0_ref, q1_ref, q2_ref, q3_ref, stats_ref, ctf3_ref, noise3_ref, trig_ref,
    data_ref, weight_ref, evidence_ref, post_ref, sum_ref, *, scale,
):
    dom, orient, y_hi, z_lo, mine = place[0], place[1], place[2], place[3], place[4]
    early = (e0_ref, e1_ref, e2_ref, e3_ref)
    boxes = (q0_ref, q1_ref, q2_ref, q3_ref)
    doms = 4
    count = q0_ref.shape[0] // 2
    half = count // 2
    refs = sum_ref.shape[0]
    pair = 2 * count
    orients = stats_ref.shape[0] // doms
    lane = lax.broadcasted_iota(jnp.int32, (1, pair), 1)
    left = lane < count
    upper = (lax.broadcasted_iota(jnp.int32, (orients, pair), 0) & 8) != 0
    factors, groups, foci = [], [], []
    for k in range(doms):
        start = dom ^ k ^ (2 * y_hi)
        table = jnp.where(
            upper,
            stats_ref[pl.ds(start ^ 2, orients, stride=doms), :],
            stats_ref[pl.ds(start, orients, stride=doms), :],
        )
        top = jnp.max(table, axis=0, keepdims=True)
        evidence = top + jnp.log(jnp.sum(jnp.exp(table - top), axis=0, keepdims=True))
        own = stats_ref[pl.ds(orient * doms + (dom ^ k), 1), :]
        factor = jnp.exp(pltpu.roll(own, count, 1) - evidence)
        factor = swap_lanes(swap_lanes(factor, half, y_hi), half // 2, z_lo)
        factors.append(jnp.where(left, factor, pltpu.roll(factor, count, 1)))
        if k == 0:
            evidence_ref[0] = jnp.sum(jnp.where(lane == mine, evidence, 0.0))
        notes = boxes[k][0:half, 4 * refs : 5 * refs].astype(F32)
        first = early[k][0:half, QUART:WIDE].astype(F32)
        spot = count if k % 2 == 0 else 0
        groups += [first[:, 0:1], notes[:, spot : spot + 1]]
        foci += [first[:, 1:2], notes[:, spot + 1 : spot + 2]]

    def fill(pieces, spot):
        total = jnp.zeros((refs, pair), F32)
        for b in range(3):
            post = pieces[b].astype(BF16)
            post_ref[b * refs : (b + 1) * refs, spot : spot + pair] = post
            total = total + post.astype(F32)
        sum_ref[:, spot : spot + pair] = total.astype(BF16)

    def block(k, number):
        return boxes[k][:, number * refs : (number + 1) * refs].astype(F32) * factors[k]

    for k in range(doms):
        fill([block(k, b) for b in range(3)], k * pair)
    for k in range(0, doms, 2):
        even, odd = block(k, 3), block(k + 1, 3)
        pieces = [
            jnp.where(left, even, pltpu.roll(odd, count, 1)),
            jnp.where(left, pltpu.roll(even, count, 1), odd),
            jnp.where(left, block(k, 4), block(k + 1, 4)),
        ]
        fill(pieces, (doms + k // 2) * pair)

    width = 256
    group = jnp.concatenate(groups, axis=0)
    focus = jnp.concatenate(foci, axis=0)
    for n in range(QUART // width):
        at = slice(n * width, (n + 1) * width)
        wide_at = pl.ds(pl.multiple_of(dom * QUART + n * width, width), width)
        cos_x, sin_x = trig_ref[0:1, wide_at], trig_ref[1:2, wide_at]
        reals, imags = [], []
        side = 2 * n * width // QUART
        late_at = slice(5 * refs + n * width - side * QUART // 2, 5 * refs + (n + 1) * width - side * QUART // 2)
        for k in range(doms):
            late = boxes[k][side * count : (side + 1) * count, late_at].astype(F32)
            soon = early[k][:, at].astype(F32)
            real = jnp.concatenate([soon[0:half], late[0:half]], axis=0)
            imag = jnp.concatenate([soon[half:], late[half:]], axis=0)
            new_real, new_imag = shift_x(real, imag, cos_x, sin_x)
            reals.append([part.astype(BF16) for part in new_real])
            imags.append([part.astype(BF16) for part in new_imag])

        def stack(parts):
            first = [parts[k][a] for k in range(doms) for a in range(2)]
            return jnp.concatenate(first + [parts[k][2] for k in range(doms)], axis=0)

        sums_real = lax.dot_general(post_ref[...], stack(reals), NN, preferred_element_type=F32)
        sums_imag = lax.dot_general(post_ref[...], stack(imags), NN, preferred_element_type=F32)
        r0, r1, r2 = (sums_real[b * refs : (b + 1) * refs] for b in range(3))
        i0, i1, i2 = (sums_imag[b * refs : (b + 1) * refs] for b in range(3))
        cos_y, sin_y = trig_ref[2:3, wide_at] * scale, trig_ref[3:4, wide_at] * scale
        both = (
            r1 * scale + (r0 + r2) * cos_y + (i2 - i0) * sin_y,
            i1 * scale + (i0 + i2) * cos_y + (r0 - r2) * sin_y,
        )
        for tile in range(width // 128):
            for c in range(2):
                first = 2 * (n * (width // 128) + tile) + c
                data_ref[pl.ds(first, refs, stride=2 * (QUART // 128)), :] = both[c][:, 128 * tile : 128 * (tile + 1)]
        ctf_power = ctf_power_rows(group, focus, ctf3_ref[:, wide_at], noise3_ref[:, wide_at])
        owns = [ctf_power[k * count : (k + 1) * count] for k in range(doms)]
        spread = jnp.concatenate([own for own in owns for _ in range(2)] + owns, axis=0)
        weight_ref[:, at] = lax.dot_general(sum_ref[...], spread, NN, preferred_element_type=F32) * scale


def on_device(images, offsets, groups, defocus, refs, log_prior, noise_inv, ctf_table):
    count_refs = refs.shape[0]
    size = {name: lax.axis_size(name) for name in AXES}
    orients = size["x"] * size["yh"] * size["zh"] * size["zl"]
    devices = orients * size["yl"] * size["c"]
    scale = 25.0 * (count_refs * orients) / devices
    trig = jnp.asarray(phase_rows())
    at = {name: lax.axis_index(name) for name in AXES}
    dom = at["yl"] * size["c"] + at["c"]
    orient = ((at["x"] * size["yh"] + at["yh"]) * size["zh"] + at["zh"]) * size["zl"] + at["zl"]
    mine = ((at["yh"] * size["zl"] + at["zl"]) * size["x"] + at["x"]) * size["zh"] + at["zh"]
    place = jnp.stack([dom, orient, at["yh"], at["zl"], mine]).astype(jnp.int32)

    smem = pl.BlockSpec(memory_space=pltpu.SMEM)
    vmem = pl.BlockSpec(memory_space=pltpu.VMEM)
    hbm = pl.BlockSpec(memory_space=pltpu.HBM)
    shape = jax.ShapeDtypeStruct
    line = 8 * size["x"] * size["zh"]
    payload = pl.pallas_call(
        prep_kernel,
        in_specs=[smem] * 3 + [hbm] * 3,
        out_specs=vmem,
        out_shape=shape((line, WIDE), BF16),
        scratch_shapes=[
            pltpu.VMEM((1, 2, PIX), BF16),
            pltpu.VMEM((GROUPS, PIX), F32),
            pltpu.VMEM((8, PIX), F32),
            pltpu.SemaphoreType.DMA((3,)),
        ],
        compiler_params=params(VMEM_ALL),
        name="prep",
    )(jnp.transpose(offsets, (0, 2, 1))[0], groups, defocus, images, noise_inv, ctf_table)
    flip = [(i, 3 - i) for i in range(4)]
    own = lax.all_to_all(payload, ("x", "zh"), 0, 0, tiled=True)
    side = lax.ppermute(own, "zl", [(0, 1), (1, 0)])
    far = lax.ppermute(own, ("yh", "yl"), flip)

    flat = refs.reshape(count_refs, 2 * PIX)
    side, flat = lax.optimization_barrier((side, flat))
    corner = lax.ppermute(side, ("yh", "yl"), flip)

    early = pl.pallas_call(
        quarter_kernel,
        in_specs=[smem] + [vmem] * 2,
        out_specs=[vmem] * 4,
        out_shape=[shape((orients, WIDE), BF16)] * 4,
        scratch_shapes=[pltpu.VMEM((4 * orients * (WIDE // 128), 128), F32)],
        compiler_params=params(),
        name="quarters",
    )(place, own, side)

    def share(parts):
        moves = [[(d, d ^ k) for d in range(4)] for k in range(4)]
        return parts[0:1] + [lax.ppermute(parts[k], ("yl", "c"), moves[k]) for k in range(1, 4)]

    early = list(early)
    flat, early[0] = lax.optimization_barrier((flat, early[0]))
    turned, power, ctf3, noise3, column = pl.pallas_call(
        refs_kernel,
        in_specs=[vmem] * 5,
        out_specs=[vmem] * 5,
        out_shape=[
            shape((2, 3 * count_refs, PIX), BF16),
            shape((count_refs, PIX), BF16),
            shape((3 * DEFS, PIX), BF16),
            shape((4 * GROUPS, PIX), BF16),
            shape((count_refs, 128), F32),
        ],
        compiler_params=params(),
        cost_estimate=pl.CostEstimate(flops=8 * count_refs * PIX, bytes_accessed=10 << 20, transcendentals=0),
        name="turn_refs",
    )(flat, trig, ctf_table, noise_inv, log_prior[None, :])

    early = share(early)
    early, far, corner = lax.optimization_barrier((early, far, corner))

    box = (2 * orients, 5 * count_refs + QUART // 2)
    *boxes, stats = pl.pallas_call(
        score_kernel,
        in_specs=[smem] + [vmem] * 10,
        out_specs=[vmem] * 5,
        out_shape=[shape(box, BF16)] * 4 + [shape((devices, 2 * orients), F32)],
        scratch_shapes=[pltpu.VMEM((8 * orients * (WIDE // 128), 128), F32)],
        compiler_params=params(),
        cost_estimate=pl.CostEstimate(
            flops=18 * orients * count_refs * 2 * PIX, bytes_accessed=10 << 20, transcendentals=0
        ),
        name="score",
    )(place, own, side, far, corner, turned, power, ctf3, noise3, trig, column)

    boxes = share(list(boxes))
    stats_all = lax.all_to_all(stats, AXES, 0, 0, tiled=True)

    data, weight, evidence = pl.pallas_call(
        functools.partial(final_kernel, scale=scale),
        in_specs=[smem] + [vmem] * 12,
        out_specs=[vmem, vmem, smem],
        scratch_shapes=[
            pltpu.VMEM((3 * count_refs, 12 * orients), BF16),
            pltpu.VMEM((count_refs, 12 * orients), BF16),
        ],
        out_shape=[
            shape((2 * count_refs * (QUART // 128), 128), F32),
            shape((count_refs, QUART), F32),
            shape((1,), F32),
        ],
        compiler_params=params(),
        name="insert",
    )(place, *early, *boxes, stats_all, ctf3, noise3, trig)
    data = jnp.transpose(data.reshape(count_refs, QUART // 128, 2, 128), (0, 2, 1, 3))
    return data.reshape(count_refs, 2, QUART), weight, evidence


def solution(mesh):
    fine = Mesh(mesh.devices.reshape(4, 2, 4, 2, 2, 2), AXES)
    orient = AXES[0:4]
    dom = AXES[4:6]
    return jax.shard_map(
        on_device,
        mesh=fine,
        in_specs=(
            P(AXES, None, None),
            P(AXES, None, None),
            P(AXES),
            P(AXES),
            P(orient, None, None),
            P(orient),
            P(),
            P(),
        ),
        out_specs=(P(orient, None, dom), P(orient, dom), P(AXES)),
        check_vma=False,
    )
```

time: 674 us -> 81.4 us (0.12)
  blocking collectives: 456 us -> 42.1 us
  waiting for transfers between devices: 115 us -> 3.03 us
  other arithmetic: 47.3 us -> 0 us
  matrix products: 18.3 us -> 0 us
  Pallas kernels: 0 us -> 15.3 us
  between operations: 16.2 us -> 2.16 us
  starting transfers between devices: 0.08 us -> 13.6 us
  local copies, waits for them, and re-layouts: 18.1 us -> 4.88 us
    all_gather x1 -> x0, blocking collectives: 157 us -> none  [on_device(): lax.all_gather(meta, 'orient', axis=0, tiled=True)]
    psum x1 -> x0, blocking collectives: 151 us -> none  [on_device(): lax.psum(jnp.sum(jnp.exp(score - top[None, :, None]), axis=(0, 2)), 'orie...]
    pmax x1 -> x0, blocking collectives: 149 us -> none  [on_device(): top = lax.pmax(local_top, 'orient')]
    reduce_scatter x1 -> x0, waiting for transfers between devices: 114 us -> none  [on_device(): lax.psum_scatter(stacked.astype(jnp.bfloat16), 'dom', scatter_dimension=2...]
    another operation x6 -> x0, other arithmetic: 42.2 us -> none
    all_to_all x0 -> x2, blocking collectives: none -> 42.1 us  [the longest x1 24.4 us: on_device(): own = lax.all_to_all(payload, ('x', 'zh'), 0, 0, tiled=True)]
    dot_general x22 -> x0, matrix products: 18.3 us -> none  [the longest x9 7.64 us: on_device(): lax.dot_general(moved, ref_flat, CONTRACT_LAST, preferred_element_type=jn...]
    pallas_call x0 -> x5, Pallas kernels: none -> 15.3 us  [the longest x1 4.75 us: on_device(): pl.pallas_call(score_kernel, in_specs=[smem] + [vmem] * 10, out_specs=[vm...]
  transfers between devices with their start and end apart: 2 -> 9, of which waited for: 1 -> 1; matrix products, arithmetic and copies ran while one was open for 2% -> 4% of each run, Pallas kernels for 0% -> 4%
where the time goes in v2:
time: 81.4 us; the launch traced here: 81 us
  blocking collectives  42.1 us (52%)
  Pallas kernels  15.3 us (19%)
  starting transfers between devices  13.6 us (17%)
  local copies, waits for them, and re-layouts  4.88 us (6%)
  waiting for transfers between devices  3.03 us (4%)
  between operations  2.16 us (3%)
    all_to_all x1, blocking collectives, on_device(): own = lax.all_to_all(payload, ('x', 'zh'), 0, 0, tiled=True)  24.4 us
    all_to_all x1, blocking collectives, on_device(): stats_all = lax.all_to_all(stats, AXES, 0, 0, tiled=True)  17.6 us
    ppermute x6, starting transfers between devices, share(): lax.ppermute(parts[k], ('yl', 'c'), moves[k])  7.35 us
    unnamed x11, local copies, waits for them, and re-layouts  4.79 us
    pallas_call x1, Pallas kernels, on_device(): pl.pallas_call(score_kernel, in_specs=[smem] + [vmem] * 10, out_specs=[vm...  4.75 us
    pallas_call x1, Pallas kernels, on_device(): pl.pallas_call(functools.partial(final_kernel, scale=scale), in_specs=[sm...  4.57 us
    ppermute x6, waiting for transfers between devices, share(): lax.ppermute(parts[k], ('yl', 'c'), moves[k])  3.02 us
    ppermute x1, starting transfers between devices, on_device(): far = lax.ppermute(own, ('yh', 'yl'), flip)  2.82 us
  transfers between devices with their start and end apart: 9, of which 1 were waited for; matrix products, arithmetic and copies ran while one was open for 4% of the time, Pallas kernels for 4%

profile of v2, /device:TPU:1, one launch (start us, length us, event | category | flops | bytes accessed | tf_op | source)
XLA Modules:
  0.0 81.0 jit_solution(4453252832123101787)
XLA Ops:
  1.9 2.5 %prep.1 = bf16[128,1152]{1,0:T(8,128)(2,1)} custom-call(s32[2,9]{1,0:T(2,128)} %bitcast.32, s32[1]{0:T(128)S(6)} %copy.16.groups, s32[1]{0:T(128)S(6)} %copy.17.defocus, bf16[1,2,4096]{2,1,0:T(2,128)(2,1)} %image_hbm.1, f32[8,4096]{1,0:T(8,128)} %noise_ref.1, f32[64,4096]{1,0:T(8,128)} %ctf_ref.1), custom_call_target="tpu_custom_call" | custom-call | tf_op jit(solution)/shard_map/prep/pallas_call | solution.py:368
  4.4 24.4 %all_to_all.22 = bf16[16,8,1152]{2,1,0:T(8,128)(2,1)S(1)} all-to-all(bf16[16,8,1152]{2,1,0:T(8,128)(2,1)} %bitcast.31), channel_id=1, replica_groups=mesh['x'=4,'yh'=2,'zh'=4,'zl'=2,'yl'=2,'c'=2] {'x','zh'}, dimensions={0} | all-to-all | bytes 589824 | tf_op jit(solution)/shard_map/all_to_all | solution.py:383
  28.9 0.9 %collective-permute-start = (bf16[128,1152]{1,0:T(8,128)(2,1)S(1)}, bf16[128,1152]{1,0:T(8,128)(2,1)}, u32[]{:S(2)}, u32[]{:S(2)}) collective-permute-start(bf16[128,1152]{1,0:T(8,128)(2,1)S(1)} %bitcast.23), channel_id=1, source_target_pairs={{0,4},{4,0},{1,5},{5,1},{2,6},{6,2},{3,7},{7,3},{8,12},{12,8},{9,1... | collective-permute-start | bytes 884744 | tf_op jit(solution)/shard_map/ppermute | solution.py:384
  29.8 3.0 %copy.15 = bf16[16,8,2,4096]{3,1,2,0:T(8,128)(2,1)S(1)} copy(bf16[16,8,2,4096]{3,2,1,0:T(2,128)(2,1)} %bitcast.30) | data formatting | bytes 4194304
  32.8 2.8 %collective-permute-start.4 = (bf16[128,1152]{1,0:T(8,128)(2,1)S(1)}, bf16[128,1152]{1,0:T(8,128)(2,1)}, u32[]{:S(2)}, u32[]{:S(2)}) collective-permute-start(bf16[128,1152]{1,0:T(8,128)(2,1)S(1)} %bitcast.24), channel_id=1, source_target_pairs={{0,34},{2,32},{32,2},{34,0},{1,35},{3,33},{33,3},{35,1},{4,38},{6,... | collective-permute-start | bytes 884744 | tf_op jit(solution)/shard_map/ppermute | solution.py:385
  35.6 0.0 collective-permute-done.side_ref
  35.6 2.6 %collective-permute-start.5 = (bf16[128,1152]{1,0:T(8,128)(2,1)}, bf16[128,1152]{1,0:T(8,128)(2,1)}, u32[]{:S(2)}, u32[]{:S(2)}) collective-permute-start(bf16[128,1152]{1,0:T(8,128)(2,1)} %collective-permute-done.side_ref), channel_id=1, source_target_pairs={{0,34},{2,32},{32,2},{34,0},{1,35},{3,33},{33,3},{35,1},{4,38},{6,... | collective-permute-start | bytes 884744 | tf_op jit(solution)/shard_map/ppermute | solution.py:389
  38.1 0.1 stack.23.place
  38.2 1.3 %quarters.1 = (bf16[64,1152]{1,0:T(8,128)(2,1)S(1)}, bf16[64,1152]{1,0:T(8,128)(2,1)S(1)}, bf16[64,1152]{1,0:T(8,128)(2,1)S(1)}, bf16[64,1152]{1,0:T(8,128)(2,1)S(1)}) custom-call(s32[5]{0:T(128)S(1)} %stack.23.place, bf16[128,1152]{1,0:T(8,128)(2,1)S(1)} %bitcast.25, bf16[128,1152]{1,0:T(8,128)(2,1)} %collective-permute-done.side_ref), custom_call_target="tpu_custom_call" | custom-call | tf_op jit(solution)/shard_map/quarters/pallas_call | solution.py:391
  39.5 3.4 %collective-permute-start.1 = (bf16[64,1152]{1,0:T(8,128)(2,1)S(1)}, bf16[64,1152]{1,0:T(8,128)(2,1)S(1)}, u32[]{:S(2)}, u32[]{:S(2)}) collective-permute-start(bf16[64,1152]{1,0:T(8,128)(2,1)S(1)} %get-tuple-element.34), channel_id=1, source_target_pairs={{0,1},{1,0},{2,3},{3,2},{4,5},{5,4},{6,7},{7,6},{8,9},{9,8},{10,11... | collective-permute-start | bytes 442376 | tf_op jit(solution)/shard_map/ppermute | solution.py:403
  42.9 0.0 collective-permute-start.2
  42.9 1.7 %collective-permute-start.3 = (bf16[64,1152]{1,0:T(8,128)(2,1)S(1)}, bf16[64,1152]{1,0:T(8,128)(2,1)S(1)}, u32[]{:S(2)}, u32[]{:S(2)}) collective-permute-start(bf16[64,1152]{1,0:T(8,128)(2,1)S(1)} %get-tuple-element.36), channel_id=1, source_target_pairs={{0,3},{1,2},{2,1},{3,0},{4,7},{5,6},{6,5},{7,4},{8,11},{9,10},{10,... | collective-permute-start | bytes 442376 | tf_op jit(solution)/shard_map/ppermute | solution.py:403
  44.6 0.0 copy-done
  44.6 0.0 copy-done.4
  44.6 0.9 %copy-done.1 = f32[8,4096]{1,0:T(8,128)S(1)} copy-done((f32[8,4096]{1,0:T(8,128)S(1)}, f32[8,4096]{1,0:T(8,128)}, u32[]{:S(2)}) %copy-start.1) | copy-done | bytes 131096
  45.5 0.9 %copy-done.3 = f32[8,4096]{1,0:T(8,128)S(1)} copy-done((f32[8,4096]{1,0:T(8,128)S(1)}, f32[8,4096]{1,0:T(8,128)}, u32[]{:S(2)}) %copy-start.3) | copy-done | bytes 131096
  46.4 2.2 %turn_refs.1 = (bf16[2,384,4096]{2,1,0:T(8,128)(2,1)S(1)}, bf16[128,4096]{1,0:T(8,128)(2,1)S(1)}, bf16[192,4096]{1,0:T(8,128)(2,1)S(1)}, bf16[32,4096]{1,0:T(8,128)(2,1)S(1)}, f32[128,128]{1,0:T(8,128)S(1)}) custom-call(bf16[128,8192]{1,0:T(8,128)(2,1)S(1)} %bitcast.22, f32[8,4096]{1,0:T(8,128)S(1)} %copy-done.1, f32[64,4096]{1,0:T(8,128)S(1)} %copy-done, ...), custom_call_target="tpu_custom_call" | custom-call | flops 4194304 | bytes 10485760 | tf_op jit(solution)/shard_map/turn_refs/pallas_call | solution.py:407
  48.6 0.0 collective-permute-done.4.far_ref
  48.6 0.0 collective-permute-done.1.e1_ref
  48.6 0.0 collective-permute-done.2.e2_ref
  48.6 3.0 %collective-permute-done.3.e3_ref = bf16[64,1152]{1,0:T(8,128)(2,1)S(1)} collective-permute-done((bf16[64,1152]{1,0:T(8,128)(2,1)S(1)}, bf16[64,1152]{1,0:T(8,128)(2,1)S(1)}, u32[]{:S(2)}, u32[]{:S(2)}) %collective-permute-start.3) | collective-permute-done | bytes 147488 | tf_op jit(solution)/shard_map/ppermute | solution.py:403
  51.6 0.0 collective-permute-done.5.corner_ref
  51.6 0.0 copy-done.2
  51.6 4.8 %score.1 = (bf16[128,1152]{1,0:T(8,128)(2,1)S(1)}, bf16[128,1152]{1,0:T(8,128)(2,1)S(1)}, bf16[128,1152]{1,0:T(8,128)(2,1)S(1)}, bf16[128,1152]{1,0:T(8,128)(2,1)S(1)}, f32[256,128]{1,0:T(8,128)S(1)}) custom-call(s32[5]{0:T(128)S(1)} %stack.23.place, bf16[128,1152]{1,0:T(8,128)(2,1)S(1)} %bitcast.26, bf16[128,1152]{1,0:T(8,128)(2,1)} %collective-permute-done.side_ref, ...), custom_call_target="tpu_custom_call" | custom-call | flops 1207959552 | bytes 10485760 | tf_op jit(solution)/shard_map/score/pallas_call | solution.py:427
  56.4 0.3 collective-permute-start.6
  56.7 0.1 collective-permute-start.7
  56.8 1.8 %collective-permute-start.8 = (bf16[128,1152]{1,0:T(8,128)(2,1)S(1)}, bf16[128,1152]{1,0:T(8,128)(2,1)S(1)}, u32[]{:S(2)}, u32[]{:S(2)}) collective-permute-start(bf16[128,1152]{1,0:T(8,128)(2,1)S(1)} %get-tuple-element.52), channel_id=1, source_target_pairs={{0,3},{1,2},{2,1},{3,0},{4,7},{5,6},{6,5},{7,4},{8,11},{9,10},{10,... | collective-permute-start | bytes 884744 | tf_op jit(solution)/shard_map/ppermute | solution.py:403
  58.7 17.6 %all_to_all.23 = f32[256,1,128]{2,1,0:T(1,128)S(1)} all-to-all(f32[256,1,128]{2,1,0:T(1,128)S(1)} %bitcast.28), channel_id=1, replica_groups=mesh['x'=4,'yh'=2,'zh'=4,'zl'=2,'yl'=2,'c'=2] {'x','yh','zh','zl','yl','c'}, dimensions={0} | all-to-all | bytes 262144 | tf_op jit(solution)/shard_map/all_to_all | solution.py:441
  76.3 0.0 collective-permute-done.6.q1_ref
  76.3 0.0 collective-permute-done.7.q2_ref
  76.3 0.0 collective-permute-done.8.q3_ref
  76.3 4.6 %insert.1 = (f32[2048,128]{1,0:T(8,128)}, f32[128,1024]{1,0:T(8,128)}, f32[1]{0:T(128)}) custom-call(s32[5]{0:T(128)S(1)} %stack.23.place, bf16[64,1152]{1,0:T(8,128)(2,1)S(1)} %get-tuple-element.37.e0_ref, bf16[64,1152]{1,0:T(8,128)(2,1)S(1)} %collective-permute-done.1.e1_ref, bf16[64,1152]{1,0:T(8,128)(2,1)S(1)} %collective-permute-done.2.e2_ref, ...), custom_call_target="tpu_custom_call" | custom-call | tf_op jit(solution)/shard_map/insert/pallas_call | solution.py:443
  (5 shorter events, 0.0 us)
Async XLA Ops:
  28.9 6.7 %collective-permute-start = (bf16[128,1152]{1,0:T(8,128)(2,1)S(1)}, bf16[128,1152]{1,0:T(8,128)(2,1)}, u32[]{:S(2)}, u32[]{:S(2)}) collective-permute-start(bf16[128,1152]{1,0:T(8,128)(2,1)S(1)} %bitcast.23), channel_id=1, source_target_pairs={{0,4},{4,0},{1,5},{5,1},{2,6},{6,2},{3,7},{7,3},{8,12},{12,8},{9,1... | collective-permute-start | bytes 884744 | tf_op jit(solution)/shard_map/ppermute | solution.py:384
  29.8 14.8 %copy-start = (f32[64,4096]{1,0:T(8,128)S(1)}, f32[64,4096]{1,0:T(8,128)}, u32[]{:S(2)}) copy-start(f32[64,4096]{1,0:T(8,128)} %ctf_ref.1) | copy-start | bytes 3145732
  29.8 14.8 %copy-start.4 = (f32[128]{0:T(128)S(1)}, f32[128]{0:T(128)}, u32[]{:S(2)}) copy-start(f32[128]{0:T(128)} %param.14) | copy-start | bytes 1540
  32.8 15.8 %collective-permute-start.4 = (bf16[128,1152]{1,0:T(8,128)(2,1)S(1)}, bf16[128,1152]{1,0:T(8,128)(2,1)}, u32[]{:S(2)}, u32[]{:S(2)}) collective-permute-start(bf16[128,1152]{1,0:T(8,128)(2,1)S(1)} %bitcast.24), channel_id=1, source_target_pairs={{0,34},{2,32},{32,2},{34,0},{1,35},{3,33},{33,3},{35,1},{4,38},{6,... | collective-permute-start | bytes 884744 | tf_op jit(solution)/shard_map/ppermute | solution.py:385
  35.6 16.0 %collective-permute-start.5 = (bf16[128,1152]{1,0:T(8,128)(2,1)}, bf16[128,1152]{1,0:T(8,128)(2,1)}, u32[]{:S(2)}, u32[]{:S(2)}) collective-permute-start(bf16[128,1152]{1,0:T(8,128)(2,1)} %collective-permute-done.side_ref), channel_id=1, source_target_pairs={{0,34},{2,32},{32,2},{34,0},{1,35},{3,33},{33,3},{35,1},{4,38},{6,... | collective-permute-start | bytes 884744 | tf_op jit(solution)/shard_map/ppermute | solution.py:389
  38.2 13.4 %copy-start.2 = (f32[8,4096]{1,0:T(8,128)S(1)}, f32[8,4096]{1,0:T(8,128)}, u32[]{:S(2)}) copy-start(f32[8,4096]{1,0:T(8,128)} %constant.28.clone.trig_ref) | copy-start | bytes 393220
  39.5 9.1 %collective-permute-start.1 = (bf16[64,1152]{1,0:T(8,128)(2,1)S(1)}, bf16[64,1152]{1,0:T(8,128)(2,1)S(1)}, u32[]{:S(2)}, u32[]{:S(2)}) collective-permute-start(bf16[64,1152]{1,0:T(8,128)(2,1)S(1)} %get-tuple-element.34), channel_id=1, source_target_pairs={{0,1},{1,0},{2,3},{3,2},{4,5},{5,4},{6,7},{7,6},{8,9},{9,8},{10,11... | collective-permute-start | bytes 442376 | tf_op jit(solution)/shard_map/ppermute | solution.py:403
  42.9 5.7 %collective-permute-start.2 = (bf16[64,1152]{1,0:T(8,128)(2,1)S(1)}, bf16[64,1152]{1,0:T(8,128)(2,1)S(1)}, u32[]{:S(2)}, u32[]{:S(2)}) collective-permute-start(bf16[64,1152]{1,0:T(8,128)(2,1)S(1)} %get-tuple-element.35), channel_id=1, source_target_pairs={{0,2},{1,3},{2,0},{3,1},{4,6},{5,7},{6,4},{7,5},{8,10},{9,11},{10,... | collective-permute-start | bytes 442376 | tf_op jit(solution)/shard_map/ppermute | solution.py:403
  42.9 8.7 %collective-permute-start.3 = (bf16[64,1152]{1,0:T(8,128)(2,1)S(1)}, bf16[64,1152]{1,0:T(8,128)(2,1)S(1)}, u32[]{:S(2)}, u32[]{:S(2)}) collective-permute-start(bf16[64,1152]{1,0:T(8,128)(2,1)S(1)} %get-tuple-element.36), channel_id=1, source_target_pairs={{0,3},{1,2},{2,1},{3,0},{4,7},{5,6},{6,5},{7,4},{8,11},{9,10},{10,... | collective-permute-start | bytes 442376 | tf_op jit(solution)/shard_map/ppermute | solution.py:403
  44.6 0.9 %copy-start.1 = (f32[8,4096]{1,0:T(8,128)S(1)}, f32[8,4096]{1,0:T(8,128)}, u32[]{:S(2)}) copy-start(f32[8,4096]{1,0:T(8,128)} %constant.28.clone.trig_ref) | copy-start | bytes 393220
  45.5 0.9 %copy-start.3 = (f32[8,4096]{1,0:T(8,128)S(1)}, f32[8,4096]{1,0:T(8,128)}, u32[]{:S(2)}) copy-start(f32[8,4096]{1,0:T(8,128)} %noise_ref.1) | copy-start | bytes 393220
  56.4 19.9 %collective-permute-start.6 = (bf16[128,1152]{1,0:T(8,128)(2,1)S(1)}, bf16[128,1152]{1,0:T(8,128)(2,1)S(1)}, u32[]{:S(2)}, u32[]{:S(2)}) collective-permute-start(bf16[128,1152]{1,0:T(8,128)(2,1)S(1)} %get-tuple-element.50), channel_id=1, source_target_pairs={{0,1},{1,0},{2,3},{3,2},{4,5},{5,4},{6,7},{7,6},{8,9},{9,8},{10,11... | collective-permute-start | bytes 884744 | tf_op jit(solution)/shard_map/ppermute | solution.py:403
  56.7 19.6 %collective-permute-start.7 = (bf16[128,1152]{1,0:T(8,128)(2,1)S(1)}, bf16[128,1152]{1,0:T(8,128)(2,1)S(1)}, u32[]{:S(2)}, u32[]{:S(2)}) collective-permute-start(bf16[128,1152]{1,0:T(8,128)(2,1)S(1)} %get-tuple-element.51), channel_id=1, source_target_pairs={{0,2},{1,3},{2,0},{3,1},{4,6},{5,7},{6,4},{7,5},{8,10},{9,11},{10,... | collective-permute-start | bytes 884744 | tf_op jit(solution)/shard_map/ppermute | solution.py:403
  56.8 19.5 %collective-permute-start.8 = (bf16[128,1152]{1,0:T(8,128)(2,1)S(1)}, bf16[128,1152]{1,0:T(8,128)(2,1)S(1)}, u32[]{:S(2)}, u32[]{:S(2)}) collective-permute-start(bf16[128,1152]{1,0:T(8,128)(2,1)S(1)} %get-tuple-element.52), channel_id=1, source_target_pairs={{0,3},{1,2},{2,1},{3,0},{4,7},{5,6},{6,5},{7,4},{8,11},{9,10},{10,... | collective-permute-start | bytes 884744 | tf_op jit(solution)/shard_map/ppermute | solution.py:403

commit v3 on v2

--- a/solution.py
+++ b/solution.py
@@ -3,7 +3,6 @@
 
 import jax
 import jax.numpy as jnp
-import numpy as np
 from jax import lax
 from jax.experimental import pallas as pl
 from jax.experimental.pallas import tpu as pltpu
@@ -28,14 +27,22 @@
 VMEM_ALL = 61 * 1024 * 1024
 
 
-def phase_rows():
-    pixel = np.arange(PIX)
-    freq_x = (pixel % SIDE + 32) % SIDE - 32
-    freq_y = (pixel // SIDE + 32) % SIDE - 32
-    turn_x = (2 * freq_x) % SIDE * (TWO_PI / SIDE)
-    turn_y = (2 * freq_y) % SIDE * (TWO_PI / SIDE)
-    rows = [np.cos(turn_x), np.sin(turn_x), np.cos(turn_y), np.sin(turn_y)]
-    return np.concatenate([np.stack(rows), np.zeros((4, PIX))]).astype(np.float32)
+def phases(step):
+    freq = (step + SIDE // 2 & SIDE - 1) - SIDE // 2
+    angle = (2 * freq & SIDE - 1).astype(F32) * (TWO_PI / SIDE)
+    return jnp.cos(angle), jnp.sin(angle)
+
+
+def phases_x(width):
+    cosine, sine = phases(lax.broadcasted_iota(jnp.int32, (8, 128), 1) & SIDE - 1)
+    many = width // 128
+    return jnp.concatenate([cosine[0:1]] * many, axis=1), jnp.concatenate([sine[0:1]] * many, axis=1)
+
+
+def phases_y(first, width):
+    pixel = lax.broadcasted_iota(jnp.int32, (8, width), 1) + first
+    cosine, sine = phases(pixel // SIDE)
+    return cosine[0:1], sine[0:1]
 
 
 def params(limit=VMEM_LIMIT):
@@ -83,7 +90,7 @@
 
 
 def refs_kernel(
-    flat_ref, trig_ref, ctf_ref, noise_ref, prior_ref, turned_ref, power_ref, ctf3_ref, noise3_ref, column_ref
+    flat_ref, ctf_ref, noise_ref, prior_ref, turned_ref, power_ref, ctf3_ref, noise3_ref, column_ref
 ):
     count = flat_ref.shape[0]
     width = 256
@@ -101,8 +108,7 @@
         high = flat_ref[:, pl.ds(pl.multiple_of(PIX + step * width, width), width)]
         real = low.astype(F32)
         imag = high.astype(F32)
-        cosine = trig_ref[2:3, at]
-        sine = trig_ref[3:4, at]
+        cosine, sine = phases_y(step * width, width)
         rc, rs, ic, si = real * cosine, real * sine, imag * cosine, imag * sine
         turned_ref[0, 0:count, at] = (rc + si).astype(BF16)
         turned_ref[1, 0:count, at] = (ic - rs).astype(BF16)
@@ -179,7 +185,7 @@
 
 
 def score_kernel(
-    place, own_ref, side_ref, far_ref, corner_ref, turned_ref, power_ref, ctf3_ref, noise3_ref, trig_ref, column_ref,
+    place, own_ref, side_ref, far_ref, corner_ref, turned_ref, power_ref, ctf3_ref, noise3_ref, column_ref,
     q0_ref, q1_ref, q2_ref, q3_ref, stats_ref, wide_ref,
 ):
     outs = (q0_ref, q1_ref, q2_ref, q3_ref)
@@ -188,11 +194,11 @@
     refs = power_ref.shape[0]
     chunk, codes = unpack((own_ref, side_ref, far_ref, corner_ref), wide_ref)
     meta = codes(0, count)
+    cos_x, sin_x = phases_x(QUART)
     cross = jnp.zeros((3 * refs, 3 * count), F32)
     self_term = jnp.zeros((refs, count), F32)
     for j in range(4):
         at = slice(j * QUART, (j + 1) * QUART)
-        cos_x, sin_x = trig_ref[0:1, at], trig_ref[1:2, at]
         for c, parts in enumerate(shift_x(chunk(j, 0, count), chunk(j + 4, 0, count), cos_x, sin_x)):
             new = jnp.concatenate(parts, axis=0).astype(BF16)
             cross += lax.dot_general(turned_ref[c, :, at], new, NT, preferred_element_type=F32)
@@ -246,7 +252,7 @@
 
 
 def final_kernel(
-    place, e0_ref, e1_ref, e2_ref, e3_ref, q0_ref, q1_ref, q2_ref, q3_ref, stats_ref, ctf3_ref, noise3_ref, trig_ref,
+    place, e0_ref, e1_ref, e2_ref, e3_ref, q0_ref, q1_ref, q2_ref, q3_ref, stats_ref, ctf3_ref, noise3_ref,
     data_ref, weight_ref, evidence_ref, post_ref, sum_ref, *, scale,
 ):
     dom, orient, y_hi, z_lo, mine = place[0], place[1], place[2], place[3], place[4]
@@ -306,12 +312,12 @@
         fill(pieces, (doms + k // 2) * pair)
 
     width = 256
+    cos_x, sin_x = phases_x(width)
     group = jnp.concatenate(groups, axis=0)
     focus = jnp.concatenate(foci, axis=0)
     for n in range(QUART // width):
         at = slice(n * width, (n + 1) * width)
         wide_at = pl.ds(pl.multiple_of(dom * QUART + n * width, width), width)
-        cos_x, sin_x = trig_ref[0:1, wide_at], trig_ref[1:2, wide_at]
         reals, imags = [], []
         side = 2 * n * width // QUART
         late_at = slice(5 * refs + n * width - side * QUART // 2, 5 * refs + (n + 1) * width - side * QUART // 2)
@@ -332,7 +338,8 @@
         sums_imag = lax.dot_general(post_ref[...], stack(imags), NN, preferred_element_type=F32)
         r0, r1, r2 = (sums_real[b * refs : (b + 1) * refs] for b in range(3))
         i0, i1, i2 = (sums_imag[b * refs : (b + 1) * refs] for b in range(3))
-        cos_y, sin_y = trig_ref[2:3, wide_at] * scale, trig_ref[3:4, wide_at] * scale
+        cos_y, sin_y = phases_y(dom * QUART + n * width, width)
+        cos_y, sin_y = cos_y * scale, sin_y * scale
         both = (
             r1 * scale + (r0 + r2) * cos_y + (i2 - i0) * sin_y,
             i1 * scale + (i0 + i2) * cos_y + (r0 - r2) * sin_y,
@@ -353,7 +360,6 @@
     orients = size["x"] * size["yh"] * size["zh"] * size["zl"]
     devices = orients * size["yl"] * size["c"]
     scale = 25.0 * (count_refs * orients) / devices
-    trig = jnp.asarray(phase_rows())
     at = {name: lax.axis_index(name) for name in AXES}
     dom = at["yl"] * size["c"] + at["c"]
     orient = ((at["x"] * size["yh"] + at["yh"]) * size["zh"] + at["zh"]) * size["zl"] + at["zl"]
@@ -406,7 +412,7 @@
     flat, early[0] = lax.optimization_barrier((flat, early[0]))
     turned, power, ctf3, noise3, column = pl.pallas_call(
         refs_kernel,
-        in_specs=[vmem] * 5,
+        in_specs=[vmem] * 4,
         out_specs=[vmem] * 5,
         out_shape=[
             shape((2, 3 * count_refs, PIX), BF16),
@@ -418,15 +424,14 @@
         compiler_params=params(),
         cost_estimate=pl.CostEstimate(flops=8 * count_refs * PIX, bytes_accessed=10 << 20, transcendentals=0),
         name="turn_refs",
-    )(flat, trig, ctf_table, noise_inv, log_prior[None, :])
+    )(flat, ctf_table, noise_inv, log_prior[None, :])
 
     early = share(early)
-    early, far, corner = lax.optimization_barrier((early, far, corner))
 
     box = (2 * orients, 5 * count_refs + QUART // 2)
     *boxes, stats = pl.pallas_call(
         score_kernel,
-        in_specs=[smem] + [vmem] * 10,
+        in_specs=[smem] + [vmem] * 9,
         out_specs=[vmem] * 5,
         out_shape=[shape(box, BF16)] * 4 + [shape((devices, 2 * orients), F32)],
         scratch_shapes=[pltpu.VMEM((8 * orients * (WIDE // 128), 128), F32)],
@@ -435,14 +440,15 @@
             flops=18 * orients * count_refs * 2 * PIX, bytes_accessed=10 << 20, transcendentals=0
         ),
         name="score",
-    )(place, own, side, far, corner, turned, power, ctf3, noise3, trig, column)
-
-    boxes = share(list(boxes))
+    )(place, own, side, far, corner, turned, power, ctf3, noise3, column)
+
+    early, boxes, stats = lax.optimization_barrier((early, list(boxes), stats))
+    boxes = share(boxes)
     stats_all = lax.all_to_all(stats, AXES, 0, 0, tiled=True)
 
     data, weight, evidence = pl.pallas_call(
         functools.partial(final_kernel, scale=scale),
-        in_specs=[smem] + [vmem] * 12,
+        in_specs=[smem] + [vmem] * 11,
         out_specs=[vmem, vmem, smem],
         scratch_shapes=[
             pltpu.VMEM((3 * count_refs, 12 * orients), BF16),
@@ -455,7 +461,7 @@
         ],
         compiler_params=params(),
         name="insert",
-    )(place, *early, *boxes, stats_all, ctf3, noise3, trig)
+    )(place, *early, *boxes, stats_all, ctf3, noise3)
     data = jnp.transpose(data.reshape(count_refs, QUART // 128, 2, 128), (0, 2, 1, 3))
     return data.reshape(count_refs, 2, QUART), weight, evidence
 

time: 81.4 us -> 80.2 us (0.985)
  waiting for transfers between devices: 3.03 us -> 0.02 us
  starting transfers between devices: 13.6 us -> 15.1 us
  local copies, waits for them, and re-layouts: 4.88 us -> 3.97 us
    ppermute x6, waiting for transfers between devices: 3.02 us -> 0.02 us  [share(): lax.ppermute(parts[k], ('yl', 'c'), moves[k])]
    ppermute x6, starting transfers between devices: 7.35 us -> 8.83 us  [share(): lax.ppermute(parts[k], ('yl', 'c'), moves[k])]
    unnamed x11 -> x7, local copies, waits for them, and re-layouts: 4.79 us -> 3.89 us
  transfers between devices with their start and end apart: 9 -> 9, of which waited for: 1 -> 0; matrix products, arithmetic and copies ran while one was open for 4% -> 4% of each run, Pallas kernels for 4% -> 11%
where the time goes in v3:
time: 80.2 us; the launch traced here: 79.8 us
  blocking collectives  42.8 us (53%)
  Pallas kernels  15.7 us (20%)
  starting transfers between devices  15.1 us (19%)
  local copies, waits for them, and re-layouts  3.97 us (5%)
  between operations  2.17 us (3%)
    all_to_all x1, blocking collectives, on_device(): own = lax.all_to_all(payload, ('x', 'zh'), 0, 0, tiled=True)  24.4 us
    all_to_all x1, blocking collectives, on_device(): stats_all = lax.all_to_all(stats, AXES, 0, 0, tiled=True)  18.4 us
    ppermute x6, starting transfers between devices, share(): lax.ppermute(parts[k], ('yl', 'c'), moves[k])  8.83 us
    pallas_call x1, Pallas kernels, on_device(): pl.pallas_call(score_kernel, in_specs=[smem] + [vmem] * 9, out_specs=[vme...  4.75 us
    pallas_call x1, Pallas kernels, on_device(): pl.pallas_call(functools.partial(final_kernel, scale=scale), in_specs=[sm...  4.69 us
    unnamed x7, local copies, waits for them, and re-layouts  3.89 us
    ppermute x1, starting transfers between devices, on_device(): far = lax.ppermute(own, ('yh', 'yl'), flip)  2.82 us
    ppermute x1, starting transfers between devices, on_device(): corner = lax.ppermute(side, ('yh', 'yl'), flip)  2.55 us
  transfers between devices with their start and end apart: 9, of which 0 were waited for; matrix products, arithmetic and copies ran while one was open for 4% of the time, Pallas kernels for 11%

profile of v3, /device:TPU:1, one launch (start us, length us, event | category | flops | bytes accessed | tf_op | source)
XLA Modules:
  0.0 79.8 jit_solution(16248982435003919592)
XLA Ops:
  1.9 2.5 %prep.1 = bf16[128,1152]{1,0:T(8,128)(2,1)} custom-call(s32[2,9]{1,0:T(2,128)} %bitcast.32, s32[1]{0:T(128)S(6)} %copy.15.groups, s32[1]{0:T(128)S(6)} %copy.16.defocus, bf16[1,2,4096]{2,1,0:T(2,128)(2,1)} %image_hbm.1, f32[8,4096]{1,0:T(8,128)} %noise_ref.1, f32[64,4096]{1,0:T(8,128)} %ctf_ref.1), custom_call_target="tpu_custom_call" | custom-call | tf_op jit(solution)/shard_map/prep/pallas_call | solution.py:374
  4.4 24.4 %all_to_all.22 = bf16[16,8,1152]{2,1,0:T(8,128)(2,1)S(1)} all-to-all(bf16[16,8,1152]{2,1,0:T(8,128)(2,1)} %bitcast.31), channel_id=1, replica_groups=mesh['x'=4,'yh'=2,'zh'=4,'zl'=2,'yl'=2,'c'=2] {'x','zh'}, dimensions={0} | all-to-all | bytes 589824 | tf_op jit(solution)/shard_map/all_to_all | solution.py:389
  28.9 0.9 %collective-permute-start = (bf16[128,1152]{1,0:T(8,128)(2,1)S(1)}, bf16[128,1152]{1,0:T(8,128)(2,1)}, u32[]{:S(2)}, u32[]{:S(2)}) collective-permute-start(bf16[128,1152]{1,0:T(8,128)(2,1)S(1)} %bitcast.23), channel_id=1, source_target_pairs={{0,4},{4,0},{1,5},{5,1},{2,6},{6,2},{3,7},{7,3},{8,12},{12,8},{9,1... | collective-permute-start | bytes 884744 | tf_op jit(solution)/shard_map/ppermute | solution.py:390
  29.8 0.0 copy-start
  29.8 0.0 copy-start.2
  29.8 3.0 %copy.14 = bf16[16,8,2,4096]{3,1,2,0:T(8,128)(2,1)S(1)} copy(bf16[16,8,2,4096]{3,2,1,0:T(2,128)(2,1)} %bitcast.30) | data formatting | bytes 4194304
  32.8 2.8 %collective-permute-start.4 = (bf16[128,1152]{1,0:T(8,128)(2,1)S(1)}, bf16[128,1152]{1,0:T(8,128)(2,1)}, u32[]{:S(2)}, u32[]{:S(2)}) collective-permute-start(bf16[128,1152]{1,0:T(8,128)(2,1)S(1)} %bitcast.24), channel_id=1, source_target_pairs={{0,34},{2,32},{32,2},{34,0},{1,35},{3,33},{33,3},{35,1},{4,38},{6,... | collective-permute-start | bytes 884744 | tf_op jit(solution)/shard_map/ppermute | solution.py:391
  35.6 0.0 collective-permute-done.side_ref
  35.6 2.6 %collective-permute-start.5 = (bf16[128,1152]{1,0:T(8,128)(2,1)}, bf16[128,1152]{1,0:T(8,128)(2,1)}, u32[]{:S(2)}, u32[]{:S(2)}) collective-permute-start(bf16[128,1152]{1,0:T(8,128)(2,1)} %collective-permute-done.side_ref), channel_id=1, source_target_pairs={{0,34},{2,32},{32,2},{34,0},{1,35},{3,33},{33,3},{35,1},{4,38},{6,... | collective-permute-start | bytes 884744 | tf_op jit(solution)/shard_map/ppermute | solution.py:395
  38.1 0.1 stack.23.place
  38.2 1.2 %quarters.1 = (bf16[64,1152]{1,0:T(8,128)(2,1)S(1)}, bf16[64,1152]{1,0:T(8,128)(2,1)S(1)}, bf16[64,1152]{1,0:T(8,128)(2,1)S(1)}, bf16[64,1152]{1,0:T(8,128)(2,1)S(1)}) custom-call(s32[5]{0:T(128)S(1)} %stack.23.place, bf16[128,1152]{1,0:T(8,128)(2,1)S(1)} %bitcast.25, bf16[128,1152]{1,0:T(8,128)(2,1)} %collective-permute-done.side_ref), custom_call_target="tpu_custom_call" | custom-call | tf_op jit(solution)/shard_map/quarters/pallas_call | solution.py:397
  39.5 3.4 %collective-permute-start.1 = (bf16[64,1152]{1,0:T(8,128)(2,1)S(1)}, bf16[64,1152]{1,0:T(8,128)(2,1)S(1)}, u32[]{:S(2)}, u32[]{:S(2)}) collective-permute-start(bf16[64,1152]{1,0:T(8,128)(2,1)S(1)} %get-tuple-element.37), channel_id=1, source_target_pairs={{0,1},{1,0},{2,3},{3,2},{4,5},{5,4},{6,7},{7,6},{8,9},{9,8},{10,11... | collective-permute-start | bytes 442376 | tf_op jit(solution)/shard_map/ppermute | solution.py:409
  42.8 0.0 collective-permute-start.2
  42.8 1.7 %collective-permute-start.3 = (bf16[64,1152]{1,0:T(8,128)(2,1)S(1)}, bf16[64,1152]{1,0:T(8,128)(2,1)S(1)}, u32[]{:S(2)}, u32[]{:S(2)}) collective-permute-start(bf16[64,1152]{1,0:T(8,128)(2,1)S(1)} %get-tuple-element.39), channel_id=1, source_target_pairs={{0,3},{1,2},{2,1},{3,0},{4,7},{5,6},{6,5},{7,4},{8,11},{9,10},{10,... | collective-permute-start | bytes 442376 | tf_op jit(solution)/shard_map/ppermute | solution.py:409
  44.6 0.0 copy-done
  44.6 0.0 copy-done.2
  44.6 0.9 %copy-done.1 = f32[8,4096]{1,0:T(8,128)S(1)} copy-done((f32[8,4096]{1,0:T(8,128)S(1)}, f32[8,4096]{1,0:T(8,128)}, u32[]{:S(2)}) %copy-start.1) | copy-done | bytes 131096
  45.5 2.5 %turn_refs.1 = (bf16[2,384,4096]{2,1,0:T(8,128)(2,1)S(1)}, bf16[128,4096]{1,0:T(8,128)(2,1)S(1)}, bf16[192,4096]{1,0:T(8,128)(2,1)S(1)}, bf16[32,4096]{1,0:T(8,128)(2,1)S(1)}, f32[128,128]{1,0:T(8,128)S(1)}) custom-call(bf16[128,8192]{1,0:T(8,128)(2,1)S(1)} %bitcast.22, f32[64,4096]{1,0:T(8,128)S(1)} %copy-done, f32[8,4096]{1,0:T(8,128)S(1)} %copy-done.1, ...), custom_call_target="tpu_custom_call" | custom-call | flops 4194304 | bytes 10485760 | tf_op jit(solution)/shard_map/turn_refs/pallas_call | solution.py:413
  48.0 0.0 collective-permute-done.4.far_ref
  48.0 0.0 collective-permute-done.5.corner_ref
  48.1 4.8 %score.1 = (bf16[128,1152]{1,0:T(8,128)(2,1)S(1)}, bf16[128,1152]{1,0:T(8,128)(2,1)S(1)}, bf16[128,1152]{1,0:T(8,128)(2,1)S(1)}, bf16[128,1152]{1,0:T(8,128)(2,1)S(1)}, f32[256,128]{1,0:T(8,128)S(1)}) custom-call(s32[5]{0:T(128)S(1)} %stack.23.place, bf16[128,1152]{1,0:T(8,128)(2,1)S(1)} %bitcast.26, bf16[128,1152]{1,0:T(8,128)(2,1)} %collective-permute-done.side_ref, ...), custom_call_target="tpu_custom_call" | custom-call | flops 1207959552 | bytes 10485760 | tf_op jit(solution)/shard_map/score/pallas_call | solution.py:432
  52.8 0.0 collective-permute-done.1.e1_ref
  52.8 0.0 collective-permute-done.2.e2_ref
  52.8 0.0 collective-permute-done.3.e3_ref
  52.8 2.0 %collective-permute-start.6 = (bf16[128,1152]{1,0:T(8,128)(2,1)S(1)}, bf16[128,1152]{1,0:T(8,128)(2,1)S(1)}, u32[]{:S(2)}, u32[]{:S(2)}) collective-permute-start(bf16[128,1152]{1,0:T(8,128)(2,1)S(1)} %get-tuple-element.56), channel_id=1, source_target_pairs={{0,1},{1,0},{2,3},{3,2},{4,5},{5,4},{6,7},{7,6},{8,9},{9,8},{10,11... | collective-permute-start | bytes 884744 | tf_op jit(solution)/shard_map/ppermute | solution.py:409
  54.9 0.0 collective-permute-start.7
  54.9 1.7 %collective-permute-start.8 = (bf16[128,1152]{1,0:T(8,128)(2,1)S(1)}, bf16[128,1152]{1,0:T(8,128)(2,1)S(1)}, u32[]{:S(2)}, u32[]{:S(2)}) collective-permute-start(bf16[128,1152]{1,0:T(8,128)(2,1)S(1)} %get-tuple-element.58), channel_id=1, source_target_pairs={{0,3},{1,2},{2,1},{3,0},{4,7},{5,6},{6,5},{7,4},{8,11},{9,10},{10,... | collective-permute-start | bytes 884744 | tf_op jit(solution)/shard_map/ppermute | solution.py:409
  56.6 18.4 %all_to_all.23 = f32[256,1,128]{2,1,0:T(1,128)S(1)} all-to-all(f32[256,1,128]{2,1,0:T(1,128)S(1)} %bitcast.28), channel_id=1, replica_groups=mesh['x'=4,'yh'=2,'zh'=4,'zl'=2,'yl'=2,'c'=2] {'x','yh','zh','zl','yl','c'}, dimensions={0} | all-to-all | bytes 262144 | tf_op jit(solution)/shard_map/all_to_all | solution.py:447
  75.0 0.0 collective-permute-done.6.q1_ref
  75.0 0.0 collective-permute-done.7.q2_ref
  75.0 0.0 collective-permute-done.8.q3_ref
  75.0 4.7 %insert.1 = (f32[2048,128]{1,0:T(8,128)}, f32[128,1024]{1,0:T(8,128)}, f32[1]{0:T(128)}) custom-call(s32[5]{0:T(128)S(1)} %stack.23.place, bf16[64,1152]{1,0:T(8,128)(2,1)S(1)} %get-tuple-element.51.e0_ref, bf16[64,1152]{1,0:T(8,128)(2,1)S(1)} %collective-permute-done.1.e1_ref, bf16[64,1152]{1,0:T(8,128)(2,1)S(1)} %collective-permute-done.2.e2_ref, ...), custom_call_target="tpu_custom_call" | custom-call | tf_op jit(solution)/shard_map/insert/pallas_call | solution.py:449
  (1 shorter events, 0.0 us)
Async XLA Ops:
  28.9 6.7 %collective-permute-start = (bf16[128,1152]{1,0:T(8,128)(2,1)S(1)}, bf16[128,1152]{1,0:T(8,128)(2,1)}, u32[]{:S(2)}, u32[]{:S(2)}) collective-permute-start(bf16[128,1152]{1,0:T(8,128)(2,1)S(1)} %bitcast.23), channel_id=1, source_target_pairs={{0,4},{4,0},{1,5},{5,1},{2,6},{6,2},{3,7},{7,3},{8,12},{12,8},{9,1... | collective-permute-start | bytes 884744 | tf_op jit(solution)/shard_map/ppermute | solution.py:390
  29.8 14.8 %copy-start = (f32[64,4096]{1,0:T(8,128)S(1)}, f32[64,4096]{1,0:T(8,128)}, u32[]{:S(2)}) copy-start(f32[64,4096]{1,0:T(8,128)} %ctf_ref.1) | copy-start | bytes 3145732
  29.8 14.8 %copy-start.2 = (f32[128]{0:T(128)S(1)}, f32[128]{0:T(128)}, u32[]{:S(2)}) copy-start(f32[128]{0:T(128)} %param.13) | copy-start | bytes 1540
  32.8 15.3 %collective-permute-start.4 = (bf16[128,1152]{1,0:T(8,128)(2,1)S(1)}, bf16[128,1152]{1,0:T(8,128)(2,1)}, u32[]{:S(2)}, u32[]{:S(2)}) collective-permute-start(bf16[128,1152]{1,0:T(8,128)(2,1)S(1)} %bitcast.24), channel_id=1, source_target_pairs={{0,34},{2,32},{32,2},{34,0},{1,35},{3,33},{33,3},{35,1},{4,38},{6,... | collective-permute-start | bytes 884744 | tf_op jit(solution)/shard_map/ppermute | solution.py:391
  35.6 12.5 %collective-permute-start.5 = (bf16[128,1152]{1,0:T(8,128)(2,1)}, bf16[128,1152]{1,0:T(8,128)(2,1)}, u32[]{:S(2)}, u32[]{:S(2)}) collective-permute-start(bf16[128,1152]{1,0:T(8,128)(2,1)} %collective-permute-done.side_ref), channel_id=1, source_target_pairs={{0,34},{2,32},{32,2},{34,0},{1,35},{3,33},{33,3},{35,1},{4,38},{6,... | collective-permute-start | bytes 884744 | tf_op jit(solution)/shard_map/ppermute | solution.py:395
  39.5 13.3 %collective-permute-start.1 = (bf16[64,1152]{1,0:T(8,128)(2,1)S(1)}, bf16[64,1152]{1,0:T(8,128)(2,1)S(1)}, u32[]{:S(2)}, u32[]{:S(2)}) collective-permute-start(bf16[64,1152]{1,0:T(8,128)(2,1)S(1)} %get-tuple-element.37), channel_id=1, source_target_pairs={{0,1},{1,0},{2,3},{3,2},{4,5},{5,4},{6,7},{7,6},{8,9},{9,8},{10,11... | collective-permute-start | bytes 442376 | tf_op jit(solution)/shard_map/ppermute | solution.py:409
  42.8 10.0 %collective-permute-start.2 = (bf16[64,1152]{1,0:T(8,128)(2,1)S(1)}, bf16[64,1152]{1,0:T(8,128)(2,1)S(1)}, u32[]{:S(2)}, u32[]{:S(2)}) collective-permute-start(bf16[64,1152]{1,0:T(8,128)(2,1)S(1)} %get-tuple-element.38), channel_id=1, source_target_pairs={{0,2},{1,3},{2,0},{3,1},{4,6},{5,7},{6,4},{7,5},{8,10},{9,11},{10,... | collective-permute-start | bytes 442376 | tf_op jit(solution)/shard_map/ppermute | solution.py:409
  42.8 10.0 %collective-permute-start.3 = (bf16[64,1152]{1,0:T(8,128)(2,1)S(1)}, bf16[64,1152]{1,0:T(8,128)(2,1)S(1)}, u32[]{:S(2)}, u32[]{:S(2)}) collective-permute-start(bf16[64,1152]{1,0:T(8,128)(2,1)S(1)} %get-tuple-element.39), channel_id=1, source_target_pairs={{0,3},{1,2},{2,1},{3,0},{4,7},{5,6},{6,5},{7,4},{8,11},{9,10},{10,... | collective-permute-start | bytes 442376 | tf_op jit(solution)/shard_map/ppermute | solution.py:409
  44.6 0.9 %copy-start.1 = (f32[8,4096]{1,0:T(8,128)S(1)}, f32[8,4096]{1,0:T(8,128)}, u32[]{:S(2)}) copy-start(f32[8,4096]{1,0:T(8,128)} %noise_ref.1) | copy-start | bytes 393220
  52.8 22.1 %collective-permute-start.6 = (bf16[128,1152]{1,0:T(8,128)(2,1)S(1)}, bf16[128,1152]{1,0:T(8,128)(2,1)S(1)}, u32[]{:S(2)}, u32[]{:S(2)}) collective-permute-start(bf16[128,1152]{1,0:T(8,128)(2,1)S(1)} %get-tuple-element.56), channel_id=1, source_target_pairs={{0,1},{1,0},{2,3},{3,2},{4,5},{5,4},{6,7},{7,6},{8,9},{9,8},{10,11... | collective-permute-start | bytes 884744 | tf_op jit(solution)/shard_map/ppermute | solution.py:409
  54.9 20.1 %collective-permute-start.7 = (bf16[128,1152]{1,0:T(8,128)(2,1)S(1)}, bf16[128,1152]{1,0:T(8,128)(2,1)S(1)}, u32[]{:S(2)}, u32[]{:S(2)}) collective-permute-start(bf16[128,1152]{1,0:T(8,128)(2,1)S(1)} %get-tuple-element.57), channel_id=1, source_target_pairs={{0,2},{1,3},{2,0},{3,1},{4,6},{5,7},{6,4},{7,5},{8,10},{9,11},{10,... | collective-permute-start | bytes 884744 | tf_op jit(solution)/shard_map/ppermute | solution.py:409
  54.9 20.1 %collective-permute-start.8 = (bf16[128,1152]{1,0:T(8,128)(2,1)S(1)}, bf16[128,1152]{1,0:T(8,128)(2,1)S(1)}, u32[]{:S(2)}, u32[]{:S(2)}) collective-permute-start(bf16[128,1152]{1,0:T(8,128)(2,1)S(1)} %get-tuple-element.58), channel_id=1, source_target_pairs={{0,3},{1,2},{2,1},{3,0},{4,7},{5,6},{6,5},{7,4},{8,11},{9,10},{10,... | collective-permute-start | bytes 884744 | tf_op jit(solution)/shard_map/ppermute | solution.py:409

commit v4 on v3

--- a/solution.py
+++ b/solution.py
@@ -23,6 +23,7 @@
 NT = (((1,), (1,)), ((), ()))
 NN = (((1,), (0,)), ((), ()))
 AXES = ("x", "yh", "zh", "zl", "yl", "c")
+TABLE_ROWS = 3 * DEFS + 4 * GROUPS
 VMEM_LIMIT = 24 * 1024 * 1024
 VMEM_ALL = 61 * 1024 * 1024
 
@@ -39,10 +40,10 @@
     return jnp.concatenate([cosine[0:1]] * many, axis=1), jnp.concatenate([sine[0:1]] * many, axis=1)
 
 
-def phases_y(first, width):
-    pixel = lax.broadcasted_iota(jnp.int32, (8, width), 1) + first
-    cosine, sine = phases(pixel // SIDE)
-    return cosine[0:1], sine[0:1]
+def phases_y(first, rows):
+    line = lax.broadcasted_iota(jnp.int32, (rows, 128), 0)
+    lane = lax.broadcasted_iota(jnp.int32, (rows, 128), 1)
+    return phases((first + 128 * line + lane) // SIDE)
 
 
 def params(limit=VMEM_LIMIT):
@@ -89,18 +90,21 @@
         out_ref[16 * k : 16 * (k + 1), :] = pair
 
 
-def refs_kernel(
-    flat_ref, ctf_ref, noise_ref, prior_ref, turned_ref, power_ref, ctf3_ref, noise3_ref, column_ref
-):
+def tables_kernel(ctf_ref, noise_ref, tables_ref):
+    def split(table):
+        first = table.astype(BF16).astype(F32)
+        second = (table - first).astype(BF16).astype(F32)
+        return [first, second, table - first - second]
+
+    noise = split(noise_ref[...])
+    rows = split(ctf_ref[...]) + noise + [jnp.zeros_like(noise[0])]
+    tables_ref[...] = jnp.concatenate(rows, axis=0).astype(BF16)
+
+
+def refs_kernel(flat_ref, prior_ref, turned_ref, power_ref, column_ref, cos_ref, sin_ref):
     count = flat_ref.shape[0]
     width = 256
-
-    def split(table):
-        first = table.astype(BF16)
-        rest = table - first.astype(F32)
-        second = rest.astype(BF16)
-        third = (rest - second.astype(F32)).astype(BF16)
-        return first, second, third
+    cos_ref[...], sin_ref[...] = phases_y(0, PIX // 128)
 
     def body(step, carry):
         at = pl.ds(pl.multiple_of(step * width, width), width)
@@ -108,7 +112,9 @@
         high = flat_ref[:, pl.ds(pl.multiple_of(PIX + step * width, width), width)]
         real = low.astype(F32)
         imag = high.astype(F32)
-        cosine, sine = phases_y(step * width, width)
+        lines = [pl.ds(step * (width // 128) + k, 1) for k in range(width // 128)]
+        cosine = jnp.concatenate([cos_ref[line, :] for line in lines], axis=1)
+        sine = jnp.concatenate([sin_ref[line, :] for line in lines], axis=1)
         rc, rs, ic, si = real * cosine, real * sine, imag * cosine, imag * sine
         turned_ref[0, 0:count, at] = (rc + si).astype(BF16)
         turned_ref[1, 0:count, at] = (ic - rs).astype(BF16)
@@ -117,9 +123,6 @@
         turned_ref[0, 2 * count : 3 * count, at] = (rc - si).astype(BF16)
         turned_ref[1, 2 * count : 3 * count, at] = (ic + rs).astype(BF16)
         power_ref[:, at] = (real * real + imag * imag).astype(BF16)
-        ctf3_ref[:, at] = jnp.concatenate(split(ctf_ref[:, at]), axis=0)
-        parts = [part.astype(F32) for part in split(noise_ref[:, at])]
-        noise3_ref[:, at] = jnp.concatenate(parts + [jnp.zeros_like(parts[0])], axis=0).astype(BF16)
         return carry
 
     lax.fori_loop(0, PIX // width, body, 0)
@@ -129,14 +132,17 @@
     column_ref[...] = jnp.broadcast_to(column, column_ref.shape)
 
 
-def ctf_power_rows(group, focus, ctf3, noise3):
-    count = group.shape[0]
-    spot = lax.broadcasted_iota(jnp.int32, (count, 3 * DEFS), 1) % DEFS
-    pick_ctf = (spot == focus.astype(jnp.int32)).astype(BF16)
-    spot = lax.broadcasted_iota(jnp.int32, (count, 4 * GROUPS), 1) % GROUPS
-    pick_noise = (spot == group.astype(jnp.int32)).astype(BF16)
-    ctf = lax.dot_general(pick_ctf, ctf3, NN, preferred_element_type=F32)
-    noise = lax.dot_general(pick_noise, noise3, NN, preferred_element_type=F32)
+def table_picks(group, focus):
+    spot = lax.broadcasted_iota(jnp.int32, (group.shape[0], TABLE_ROWS), 1)
+    ctf = (spot < 3 * DEFS) & (spot % DEFS == focus.astype(jnp.int32))
+    noise = (spot >= 3 * DEFS) & (spot < 3 * (DEFS + GROUPS)) & (spot % GROUPS == group.astype(jnp.int32))
+    return jnp.concatenate([ctf.astype(F32), noise.astype(F32)], axis=0).astype(BF16)
+
+
+def ctf_power_rows(picks, tables):
+    rows = lax.dot_general(picks, tables, NN, preferred_element_type=F32)
+    count = rows.shape[0] // 2
+    ctf, noise = rows[0:count], rows[count:]
     return (noise * ctf * ctf).astype(BF16)
 
 
@@ -185,7 +191,7 @@
 
 
 def score_kernel(
-    place, own_ref, side_ref, far_ref, corner_ref, turned_ref, power_ref, ctf3_ref, noise3_ref, column_ref,
+    place, own_ref, side_ref, far_ref, corner_ref, turned_ref, power_ref, tables_ref, column_ref,
     q0_ref, q1_ref, q2_ref, q3_ref, stats_ref, wide_ref,
 ):
     outs = (q0_ref, q1_ref, q2_ref, q3_ref)
@@ -194,6 +200,7 @@
     refs = power_ref.shape[0]
     chunk, codes = unpack((own_ref, side_ref, far_ref, corner_ref), wide_ref)
     meta = codes(0, count)
+    picks = table_picks(meta[:, 0:1], meta[:, 1:2])
     cos_x, sin_x = phases_x(QUART)
     cross = jnp.zeros((3 * refs, 3 * count), F32)
     self_term = jnp.zeros((refs, count), F32)
@@ -202,7 +209,7 @@
         for c, parts in enumerate(shift_x(chunk(j, 0, count), chunk(j + 4, 0, count), cos_x, sin_x)):
             new = jnp.concatenate(parts, axis=0).astype(BF16)
             cross += lax.dot_general(turned_ref[c, :, at], new, NT, preferred_element_type=F32)
-        ctf_power = ctf_power_rows(meta[:, 0:1], meta[:, 1:2], ctf3_ref[:, at], noise3_ref[:, at])
+        ctf_power = ctf_power_rows(picks, tables_ref[:, at])
         self_term += lax.dot_general(power_ref[:, at], ctf_power, NT, preferred_element_type=F32)
         part = place[0] ^ j
         late = jnp.concatenate([chunk(part, half, half), chunk(part + 4, half, half)], axis=0).astype(BF16)
@@ -252,7 +259,7 @@
 
 
 def final_kernel(
-    place, e0_ref, e1_ref, e2_ref, e3_ref, q0_ref, q1_ref, q2_ref, q3_ref, stats_ref, ctf3_ref, noise3_ref,
+    place, e0_ref, e1_ref, e2_ref, e3_ref, q0_ref, q1_ref, q2_ref, q3_ref, stats_ref, tables_ref,
     data_ref, weight_ref, evidence_ref, post_ref, sum_ref, *, scale,
 ):
     dom, orient, y_hi, z_lo, mine = place[0], place[1], place[2], place[3], place[4]
@@ -295,13 +302,15 @@
             post = pieces[b].astype(BF16)
             post_ref[b * refs : (b + 1) * refs, spot : spot + pair] = post
             total = total + post.astype(F32)
-        sum_ref[:, spot : spot + pair] = total.astype(BF16)
+        return total
 
     def block(k, number):
         return boxes[k][:, number * refs : (number + 1) * refs].astype(F32) * factors[k]
 
+    totals = []
     for k in range(doms):
-        fill([block(k, b) for b in range(3)], k * pair)
+        total = fill([block(k, b) for b in range(3)], k * pair)
+        totals.append(total + pltpu.roll(total, count, 1))
     for k in range(0, doms, 2):
         even, odd = block(k, 3), block(k + 1, 3)
         pieces = [
@@ -309,12 +318,14 @@
             jnp.where(left, pltpu.roll(even, count, 1), odd),
             jnp.where(left, block(k, 4), block(k + 1, 4)),
         ]
-        fill(pieces, (doms + k // 2) * pair)
+        total = fill(pieces, (doms + k // 2) * pair) + jnp.where(left, totals[k], totals[k + 1])
+        sum_ref[:, k * count : (k + 2) * count] = total.astype(BF16)
 
     width = 256
     cos_x, sin_x = phases_x(width)
-    group = jnp.concatenate(groups, axis=0)
-    focus = jnp.concatenate(foci, axis=0)
+    picks = table_picks(jnp.concatenate(groups, axis=0), jnp.concatenate(foci, axis=0))
+    cos_rows, sin_rows = phases_y(dom * QUART, QUART // 128)
+    cos_rows, sin_rows = cos_rows * scale, sin_rows * scale
     for n in range(QUART // width):
         at = slice(n * width, (n + 1) * width)
         wide_at = pl.ds(pl.multiple_of(dom * QUART + n * width, width), width)
@@ -338,8 +349,9 @@
         sums_imag = lax.dot_general(post_ref[...], stack(imags), NN, preferred_element_type=F32)
         r0, r1, r2 = (sums_real[b * refs : (b + 1) * refs] for b in range(3))
         i0, i1, i2 = (sums_imag[b * refs : (b + 1) * refs] for b in range(3))
-        cos_y, sin_y = phases_y(dom * QUART + n * width, width)
-        cos_y, sin_y = cos_y * scale, sin_y * scale
+        lines = [n * (width // 128) + tile for tile in range(width // 128)]
+        cos_y = jnp.concatenate([cos_rows[line : line + 1] for line in lines], axis=1)
+        sin_y = jnp.concatenate([sin_rows[line : line + 1] for line in lines], axis=1)
         both = (
             r1 * scale + (r0 + r2) * cos_y + (i2 - i0) * sin_y,
             i1 * scale + (i0 + i2) * cos_y + (r0 - r2) * sin_y,
@@ -348,10 +360,8 @@
             for c in range(2):
                 first = 2 * (n * (width // 128) + tile) + c
                 data_ref[pl.ds(first, refs, stride=2 * (QUART // 128)), :] = both[c][:, 128 * tile : 128 * (tile + 1)]
-        ctf_power = ctf_power_rows(group, focus, ctf3_ref[:, wide_at], noise3_ref[:, wide_at])
-        owns = [ctf_power[k * count : (k + 1) * count] for k in range(doms)]
-        spread = jnp.concatenate([own for own in owns for _ in range(2)] + owns, axis=0)
-        weight_ref[:, at] = lax.dot_general(sum_ref[...], spread, NN, preferred_element_type=F32) * scale
+        ctf_power = ctf_power_rows(picks, tables_ref[:, wide_at])
+        weight_ref[:, at] = lax.dot_general(sum_ref[...], ctf_power, NN, preferred_element_type=F32) * scale
 
 
 def on_device(images, offsets, groups, defocus, refs, log_prior, noise_inv, ctf_table):
@@ -391,7 +401,16 @@
     far = lax.ppermute(own, ("yh", "yl"), flip)
 
     flat = refs.reshape(count_refs, 2 * PIX)
-    side, flat = lax.optimization_barrier((side, flat))
+    flat, ctf_late, noise_late = lax.optimization_barrier((flat, ctf_table, noise_inv))
+    tables = pl.pallas_call(
+        tables_kernel,
+        in_specs=[vmem] * 2,
+        out_specs=vmem,
+        out_shape=shape((TABLE_ROWS, PIX), BF16),
+        compiler_params=params(VMEM_LIMIT // 3),
+        name="tables",
+    )(ctf_late, noise_late)
+    side, _, flat, tables = lax.optimization_barrier((side, far, flat, tables))
     corner = lax.ppermute(side, ("yh", "yl"), flip)
 
     early = pl.pallas_call(
@@ -400,7 +419,7 @@
         out_specs=[vmem] * 4,
         out_shape=[shape((orients, WIDE), BF16)] * 4,
         scratch_shapes=[pltpu.VMEM((4 * orients * (WIDE // 128), 128), F32)],
-        compiler_params=params(),
+        compiler_params=params(VMEM_LIMIT // 3),
         name="quarters",
     )(place, own, side)
 
@@ -410,28 +429,26 @@
 
     early = list(early)
     flat, early[0] = lax.optimization_barrier((flat, early[0]))
-    turned, power, ctf3, noise3, column = pl.pallas_call(
+    turned, power, column = pl.pallas_call(
         refs_kernel,
-        in_specs=[vmem] * 4,
-        out_specs=[vmem] * 5,
+        in_specs=[vmem] * 2,
+        out_specs=[vmem] * 3,
         out_shape=[
             shape((2, 3 * count_refs, PIX), BF16),
             shape((count_refs, PIX), BF16),
-            shape((3 * DEFS, PIX), BF16),
-            shape((4 * GROUPS, PIX), BF16),
             shape((count_refs, 128), F32),
         ],
+        scratch_shapes=[pltpu.VMEM((PIX // 128, 128), F32)] * 2,
         compiler_params=params(),
         cost_estimate=pl.CostEstimate(flops=8 * count_refs * PIX, bytes_accessed=10 << 20, transcendentals=0),
         name="turn_refs",
-    )(flat, ctf_table, noise_inv, log_prior[None, :])
-
+    )(flat, log_prior[None, :])
     early = share(early)
 
     box = (2 * orients, 5 * count_refs + QUART // 2)
     *boxes, stats = pl.pallas_call(
         score_kernel,
-        in_specs=[smem] + [vmem] * 9,
+        in_specs=[smem] + [vmem] * 8,
         out_specs=[vmem] * 5,
         out_shape=[shape(box, BF16)] * 4 + [shape((devices, 2 * orients), F32)],
         scratch_shapes=[pltpu.VMEM((8 * orients * (WIDE // 128), 128), F32)],
@@ -440,7 +457,7 @@
             flops=18 * orients * count_refs * 2 * PIX, bytes_accessed=10 << 20, transcendentals=0
         ),
         name="score",
-    )(place, own, side, far, corner, turned, power, ctf3, noise3, column)
+    )(place, own, side, far, corner, turned, power, tables, column)
 
     early, boxes, stats = lax.optimization_barrier((early, list(boxes), stats))
     boxes = share(boxes)
@@ -448,11 +465,11 @@
 
     data, weight, evidence = pl.pallas_call(
         functools.partial(final_kernel, scale=scale),
-        in_specs=[smem] + [vmem] * 11,
+        in_specs=[smem] + [vmem] * 10,
         out_specs=[vmem, vmem, smem],
         scratch_shapes=[
             pltpu.VMEM((3 * count_refs, 12 * orients), BF16),
-            pltpu.VMEM((count_refs, 12 * orients), BF16),
+            pltpu.VMEM((count_refs, 4 * orients), BF16),
         ],
         out_shape=[
             shape((2 * count_refs * (QUART // 128), 128), F32),
@@ -461,7 +478,7 @@
         ],
         compiler_params=params(),
         name="insert",
-    )(place, *early, *boxes, stats_all, ctf3, noise3)
+    )(place, *early, *boxes, stats_all, tables)
     data = jnp.transpose(data.reshape(count_refs, QUART // 128, 2, 128), (0, 2, 1, 3))
     return data.reshape(count_refs, 2, QUART), weight, evidence
 

time: 80.2 us -> 77.7 us (0.969)
  starting transfers between devices: 15.1 us -> 12.5 us
  local copies, waits for them, and re-layouts: 3.97 us -> 6 us
  Pallas kernels: 15.7 us -> 14.2 us
    unnamed x7 -> x9, local copies, waits for them, and re-layouts: 3.89 us -> 5.92 us
    ppermute x6, starting transfers between devices: 8.83 us -> 7.32 us  [share(): lax.ppermute(parts[k], ('yl', 'c'), moves[k])]
    ppermute x1, starting transfers between devices: 2.55 us -> 1.49 us  [on_device(): corner = lax.ppermute(side, ('yh', 'yl'), flip)]
    pallas_call x2 -> x3, Pallas kernels: 7.3 us -> 6.28 us  [the longest x1 3.93 us: on_device(): pl.pallas_call(score_kernel, in_specs=[smem] + [vmem] * 8, out_specs=[vme...]
  transfers between devices with their start and end apart: 9 -> 9, of which waited for: 0 -> 1; matrix products, arithmetic and copies ran while one was open for 4% -> 6% of each run, Pallas kernels for 11% -> 9%
where the time goes in v4:
time: 77.7 us; the launch traced here: 77.5 us
  blocking collectives  42 us (54%)
  Pallas kernels  14.2 us (18%)
  starting transfers between devices  12.5 us (16%)
  local copies, waits for them, and re-layouts  6 us (8%)
  between operations  2.17 us (3%)
    all_to_all x1, blocking collectives, on_device(): own = lax.all_to_all(payload, ('x', 'zh'), 0, 0, tiled=True)  24.4 us
    all_to_all x1, blocking collectives, on_device(): stats_all = lax.all_to_all(stats, AXES, 0, 0, tiled=True)  17.6 us
    ppermute x6, starting transfers between devices, share(): lax.ppermute(parts[k], ('yl', 'c'), moves[k])  7.32 us
    unnamed x9, local copies, waits for them, and re-layouts  5.92 us
    pallas_call x1, Pallas kernels, on_device(): pl.pallas_call(functools.partial(final_kernel, scale=scale), in_specs=[sm...  4.58 us
    pallas_call x1, Pallas kernels, on_device(): pl.pallas_call(score_kernel, in_specs=[smem] + [vmem] * 8, out_specs=[vme...  3.93 us
    ppermute x1, starting transfers between devices, on_device(): far = lax.ppermute(own, ('yh', 'yl'), flip)  2.73 us
    pallas_call x1, Pallas kernels, on_device(): pl.pallas_call(prep_kernel, in_specs=[smem] * 3 + [hbm] * 3, out_specs=vm...  2.52 us
  transfers between devices with their start and end apart: 9, of which 1 were waited for; matrix products, arithmetic and copies ran while one was open for 6% of the time, Pallas kernels for 9%

profile of v4, /device:TPU:1, one launch (start us, length us, event | category | flops | bytes accessed | tf_op | source)
XLA Modules:
  0.0 77.5 jit_solution(621597723596443371)
XLA Ops:
  1.9 2.5 %prep.1 = bf16[128,1152]{1,0:T(8,128)(2,1)} custom-call(s32[2,9]{1,0:T(2,128)} %bitcast.32, s32[1]{0:T(128)S(6)} %copy.15.groups, s32[1]{0:T(128)S(6)} %copy.16.defocus, bf16[1,2,4096]{2,1,0:T(2,128)(2,1)} %image_hbm.1, f32[8,4096]{1,0:T(8,128)} %noise_ref, f32[64,4096]{1,0:T(8,128)} %ctf_ref), custom_call_target="tpu_custom_call" | custom-call | tf_op jit(solution)/shard_map/prep/pallas_call | solution.py:384
  4.4 24.4 %all_to_all.22 = bf16[16,8,1152]{2,1,0:T(8,128)(2,1)S(1)} all-to-all(bf16[16,8,1152]{2,1,0:T(8,128)(2,1)} %bitcast.31), channel_id=1, replica_groups=mesh['x'=4,'yh'=2,'zh'=4,'zl'=2,'yl'=2,'c'=2] {'x','zh'}, dimensions={0} | all-to-all | bytes 589824 | tf_op jit(solution)/shard_map/all_to_all | solution.py:399
  28.9 2.7 %collective-permute-start.1 = (bf16[128,1152]{1,0:T(8,128)(2,1)S(1)}, bf16[128,1152]{1,0:T(8,128)(2,1)S(1)}, u32[]{:S(2)}, u32[]{:S(2)}) collective-permute-start(bf16[128,1152]{1,0:T(8,128)(2,1)S(1)} %bitcast.23), channel_id=1, source_target_pairs={{0,34},{2,32},{32,2},{34,0},{1,35},{3,33},{33,3},{35,1},{4,38},{6,... | collective-permute-start | bytes 884744 | tf_op jit(solution)/shard_map/ppermute | solution.py:401
  31.6 0.9 %collective-permute-start = (bf16[128,1152]{1,0:T(8,128)(2,1)S(1)}, bf16[128,1152]{1,0:T(8,128)(2,1)S(1)}, u32[]{:S(2)}, u32[]{:S(2)}) collective-permute-start(bf16[128,1152]{1,0:T(8,128)(2,1)S(1)} %bitcast.24), channel_id=1, source_target_pairs={{0,4},{4,0},{1,5},{5,1},{2,6},{6,2},{3,7},{7,3},{8,12},{12,8},{9,1... | collective-permute-start | bytes 884744 | tf_op jit(solution)/shard_map/ppermute | solution.py:400
  32.5 4.3 %copy.14 = bf16[16,8,2,4096]{3,1,2,0:T(8,128)(2,1)} copy(bf16[16,8,2,4096]{3,2,1,0:T(2,128)(2,1)} %bitcast.30) | data formatting | bytes 4194304
  36.8 0.0 copy-done.1
  36.8 0.0 copy-done.2
  36.8 0.3 tables.1.tables_ref
  37.2 0.0 collective-permute-done.1.far_ref
  37.2 0.6 collective-permute-done.side_ref
  37.8 1.5 %collective-permute-start.5 = (bf16[128,1152]{1,0:T(8,128)(2,1)S(1)}, bf16[128,1152]{1,0:T(8,128)(2,1)S(1)}, u32[]{:S(2)}, u32[]{:S(2)}) collective-permute-start(bf16[128,1152]{1,0:T(8,128)(2,1)S(1)} %collective-permute-done.side_ref), channel_id=1, source_target_pairs={{0,34},{2,32},{32,2},{34,0},{1,35},{3,33},{33,3},{35,1},{4,38},{6,... | collective-permute-start | bytes 884744 | tf_op jit(solution)/shard_map/ppermute | solution.py:414
  39.3 0.1 stack.23.place
  39.3 0.8 %quarters.1 = (bf16[64,1152]{1,0:T(8,128)(2,1)S(1)}, bf16[64,1152]{1,0:T(8,128)(2,1)S(1)}, bf16[64,1152]{1,0:T(8,128)(2,1)S(1)}, bf16[64,1152]{1,0:T(8,128)(2,1)S(1)}) custom-call(s32[5]{0:T(128)S(1)} %stack.23.place, bf16[128,1152]{1,0:T(8,128)(2,1)S(1)} %bitcast.25, bf16[128,1152]{1,0:T(8,128)(2,1)S(1)} %collective-permute-done.side_ref), custom_call_target="tpu_custom_call" | custom-call | tf_op jit(solution)/shard_map/quarters/pallas_call | solution.py:416
  40.2 3.4 %collective-permute-start.2 = (bf16[64,1152]{1,0:T(8,128)(2,1)S(1)}, bf16[64,1152]{1,0:T(8,128)(2,1)S(1)}, u32[]{:S(2)}, u32[]{:S(2)}) collective-permute-start(bf16[64,1152]{1,0:T(8,128)(2,1)S(1)} %get-tuple-element.42), channel_id=1, source_target_pairs={{0,1},{1,0},{2,3},{3,2},{4,5},{5,4},{6,7},{7,6},{8,9},{9,8},{10,11... | collective-permute-start | bytes 442376 | tf_op jit(solution)/shard_map/ppermute | solution.py:428
  43.5 0.0 collective-permute-start.3
  43.5 1.7 %collective-permute-start.4 = (bf16[64,1152]{1,0:T(8,128)(2,1)S(1)}, bf16[64,1152]{1,0:T(8,128)(2,1)S(1)}, u32[]{:S(2)}, u32[]{:S(2)}) collective-permute-start(bf16[64,1152]{1,0:T(8,128)(2,1)S(1)} %get-tuple-element.44), channel_id=1, source_target_pairs={{0,3},{1,2},{2,1},{3,0},{4,7},{5,6},{6,5},{7,4},{8,11},{9,10},{10,... | collective-permute-start | bytes 442376 | tf_op jit(solution)/shard_map/ppermute | solution.py:428
  45.2 0.0 copy-done.3
  45.2 1.6 %copy-done = bf16[16,8,2,4096]{3,1,2,0:T(8,128)(2,1)S(1)} copy-done((bf16[16,8,2,4096]{3,1,2,0:T(8,128)(2,1)S(1)}, bf16[16,8,2,4096]{3,1,2,0:T(8,128)(2,1)}, u32[]{:S(2)}) %copy-start) | copy-done | bytes 2097176
  46.8 2.0 %turn_refs.1 = (bf16[2,384,4096]{2,1,0:T(8,128)(2,1)S(1)}, bf16[128,4096]{1,0:T(8,128)(2,1)S(1)}, f32[128,128]{1,0:T(8,128)S(1)}) custom-call(bf16[128,8192]{1,0:T(8,128)(2,1)S(1)} %bitcast.22, f32[1,128]{1,0:T(1,128)S(1)} %bitcast.29), custom_call_target="tpu_custom_call" | custom-call | flops 4194304 | bytes 10485760 | tf_op jit(solution)/shard_map/turn_refs/pallas_call | solution.py:432
  48.9 0.0 collective-permute-done.5.corner_ref
  48.9 3.9 %score.1 = (bf16[128,1152]{1,0:T(8,128)(2,1)S(1)}, bf16[128,1152]{1,0:T(8,128)(2,1)S(1)}, bf16[128,1152]{1,0:T(8,128)(2,1)S(1)}, bf16[128,1152]{1,0:T(8,128)(2,1)S(1)}, f32[256,128]{1,0:T(8,128)S(1)}) custom-call(s32[5]{0:T(128)S(1)} %stack.23.place, bf16[128,1152]{1,0:T(8,128)(2,1)S(1)} %bitcast.26, bf16[128,1152]{1,0:T(8,128)(2,1)S(1)} %collective-permute-done.side_ref, ...), custom_call_target="tpu_custom_call" | custom-call | flops 1207959552 | bytes 10485760 | tf_op jit(solution)/shard_map/score/pallas_call | solution.py:449
  52.8 0.0 collective-permute-done.2.e1_ref
  52.8 0.0 collective-permute-done.3.e2_ref
  52.8 0.0 collective-permute-done.4.e3_ref
  52.9 0.2 collective-permute-start.6
  53.1 0.0 collective-permute-start.7
  53.1 2.0 %collective-permute-start.8 = (bf16[128,1152]{1,0:T(8,128)(2,1)S(1)}, bf16[128,1152]{1,0:T(8,128)(2,1)S(1)}, u32[]{:S(2)}, u32[]{:S(2)}) collective-permute-start(bf16[128,1152]{1,0:T(8,128)(2,1)S(1)} %get-tuple-element.62), channel_id=1, source_target_pairs={{0,3},{1,2},{2,1},{3,0},{4,7},{5,6},{6,5},{7,4},{8,11},{9,10},{10,... | collective-permute-start | bytes 884744 | tf_op jit(solution)/shard_map/ppermute | solution.py:428
  55.1 17.6 %all_to_all.23 = f32[256,1,128]{2,1,0:T(1,128)S(1)} all-to-all(f32[256,1,128]{2,1,0:T(1,128)S(1)} %bitcast.28), channel_id=1, replica_groups=mesh['x'=4,'yh'=2,'zh'=4,'zl'=2,'yl'=2,'c'=2] {'x','yh','zh','zl','yl','c'}, dimensions={0} | all-to-all | bytes 262144 | tf_op jit(solution)/shard_map/all_to_all | solution.py:464
  72.7 0.0 collective-permute-done.6.q1_ref
  72.7 0.0 collective-permute-done.7.q2_ref
  72.7 0.0 collective-permute-done.8.q3_ref
  72.7 4.6 %insert.1 = (f32[2048,128]{1,0:T(8,128)}, f32[128,1024]{1,0:T(8,128)}, f32[1]{0:T(128)}) custom-call(s32[5]{0:T(128)S(1)} %stack.23.place, bf16[64,1152]{1,0:T(8,128)(2,1)S(1)} %get-tuple-element.55.e0_ref, bf16[64,1152]{1,0:T(8,128)(2,1)S(1)} %collective-permute-done.2.e1_ref, bf16[64,1152]{1,0:T(8,128)(2,1)S(1)} %collective-permute-done.3.e2_ref, ...), custom_call_target="tpu_custom_call" | custom-call | tf_op jit(solution)/shard_map/insert/pallas_call | solution.py:466
  (4 shorter events, 0.0 us)
Async XLA Ops:
  28.9 8.3 %collective-permute-start.1 = (bf16[128,1152]{1,0:T(8,128)(2,1)S(1)}, bf16[128,1152]{1,0:T(8,128)(2,1)S(1)}, u32[]{:S(2)}, u32[]{:S(2)}) collective-permute-start(bf16[128,1152]{1,0:T(8,128)(2,1)S(1)} %bitcast.23), channel_id=1, source_target_pairs={{0,34},{2,32},{32,2},{34,0},{1,35},{3,33},{33,3},{35,1},{4,38},{6,... | collective-permute-start | bytes 884744 | tf_op jit(solution)/shard_map/ppermute | solution.py:401
  31.6 6.1 %collective-permute-start = (bf16[128,1152]{1,0:T(8,128)(2,1)S(1)}, bf16[128,1152]{1,0:T(8,128)(2,1)S(1)}, u32[]{:S(2)}, u32[]{:S(2)}) collective-permute-start(bf16[128,1152]{1,0:T(8,128)(2,1)S(1)} %bitcast.24), channel_id=1, source_target_pairs={{0,4},{4,0},{1,5},{5,1},{2,6},{6,2},{3,7},{7,3},{8,12},{12,8},{9,1... | collective-permute-start | bytes 884744 | tf_op jit(solution)/shard_map/ppermute | solution.py:400
  32.5 4.3 %copy-start.1 = (f32[64,4096]{1,0:T(8,128)S(1)}, f32[64,4096]{1,0:T(8,128)}, u32[]{:S(2)}) copy-start(f32[64,4096]{1,0:T(8,128)} %ctf_ref) | copy-start | bytes 3145732
  32.5 4.3 %copy-start.2 = (f32[8,4096]{1,0:T(8,128)S(1)}, f32[8,4096]{1,0:T(8,128)}, u32[]{:S(2)}) copy-start(f32[8,4096]{1,0:T(8,128)} %noise_ref) | copy-start | bytes 393220
  36.8 8.4 %copy-start.3 = (f32[128]{0:T(128)S(1)}, f32[128]{0:T(128)}, u32[]{:S(2)}) copy-start(f32[128]{0:T(128)} %param.13) | copy-start | bytes 1540
  37.8 11.1 %collective-permute-start.5 = (bf16[128,1152]{1,0:T(8,128)(2,1)S(1)}, bf16[128,1152]{1,0:T(8,128)(2,1)S(1)}, u32[]{:S(2)}, u32[]{:S(2)}) collective-permute-start(bf16[128,1152]{1,0:T(8,128)(2,1)S(1)} %collective-permute-done.side_ref), channel_id=1, source_target_pairs={{0,34},{2,32},{32,2},{34,0},{1,35},{3,33},{33,3},{35,1},{4,38},{6,... | collective-permute-start | bytes 884744 | tf_op jit(solution)/shard_map/ppermute | solution.py:414
  40.2 12.7 %collective-permute-start.2 = (bf16[64,1152]{1,0:T(8,128)(2,1)S(1)}, bf16[64,1152]{1,0:T(8,128)(2,1)S(1)}, u32[]{:S(2)}, u32[]{:S(2)}) collective-permute-start(bf16[64,1152]{1,0:T(8,128)(2,1)S(1)} %get-tuple-element.42), channel_id=1, source_target_pairs={{0,1},{1,0},{2,3},{3,2},{4,5},{5,4},{6,7},{7,6},{8,9},{9,8},{10,11... | collective-permute-start | bytes 442376 | tf_op jit(solution)/shard_map/ppermute | solution.py:428
  43.5 9.3 %collective-permute-start.3 = (bf16[64,1152]{1,0:T(8,128)(2,1)S(1)}, bf16[64,1152]{1,0:T(8,128)(2,1)S(1)}, u32[]{:S(2)}, u32[]{:S(2)}) collective-permute-start(bf16[64,1152]{1,0:T(8,128)(2,1)S(1)} %get-tuple-element.43), channel_id=1, source_target_pairs={{0,2},{1,3},{2,0},{3,1},{4,6},{5,7},{6,4},{7,5},{8,10},{9,11},{10,... | collective-permute-start | bytes 442376 | tf_op jit(solution)/shard_map/ppermute | solution.py:428
  43.5 9.3 %collective-permute-start.4 = (bf16[64,1152]{1,0:T(8,128)(2,1)S(1)}, bf16[64,1152]{1,0:T(8,128)(2,1)S(1)}, u32[]{:S(2)}, u32[]{:S(2)}) collective-permute-start(bf16[64,1152]{1,0:T(8,128)(2,1)S(1)} %get-tuple-element.44), channel_id=1, source_target_pairs={{0,3},{1,2},{2,1},{3,0},{4,7},{5,6},{6,5},{7,4},{8,11},{9,10},{10,... | collective-permute-start | bytes 442376 | tf_op jit(solution)/shard_map/ppermute | solution.py:428
  45.2 1.6 %copy-start = (bf16[16,8,2,4096]{3,1,2,0:T(8,128)(2,1)S(1)}, bf16[16,8,2,4096]{3,1,2,0:T(8,128)(2,1)}, u32[]{:S(2)}) copy-start(bf16[16,8,2,4096]{3,1,2,0:T(8,128)(2,1)} %copy.14) | copy-start | bytes 6291460
  52.9 19.8 %collective-permute-start.6 = (bf16[128,1152]{1,0:T(8,128)(2,1)S(1)}, bf16[128,1152]{1,0:T(8,128)(2,1)S(1)}, u32[]{:S(2)}, u32[]{:S(2)}) collective-permute-start(bf16[128,1152]{1,0:T(8,128)(2,1)S(1)} %get-tuple-element.60), channel_id=1, source_target_pairs={{0,1},{1,0},{2,3},{3,2},{4,5},{5,4},{6,7},{7,6},{8,9},{9,8},{10,11... | collective-permute-start | bytes 884744 | tf_op jit(solution)/shard_map/ppermute | solution.py:428
  53.1 19.6 %collective-permute-start.7 = (bf16[128,1152]{1,0:T(8,128)(2,1)S(1)}, bf16[128,1152]{1,0:T(8,128)(2,1)S(1)}, u32[]{:S(2)}, u32[]{:S(2)}) collective-permute-start(bf16[128,1152]{1,0:T(8,128)(2,1)S(1)} %get-tuple-element.61), channel_id=1, source_target_pairs={{0,2},{1,3},{2,0},{3,1},{4,6},{5,7},{6,4},{7,5},{8,10},{9,11},{10,... | collective-permute-start | bytes 884744 | tf_op jit(solution)/shard_map/ppermute | solution.py:428
  53.1 19.6 %collective-permute-start.8 = (bf16[128,1152]{1,0:T(8,128)(2,1)S(1)}, bf16[128,1152]{1,0:T(8,128)(2,1)S(1)}, u32[]{:S(2)}, u32[]{:S(2)}) collective-permute-start(bf16[128,1152]{1,0:T(8,128)(2,1)S(1)} %get-tuple-element.62), channel_id=1, source_target_pairs={{0,3},{1,2},{2,1},{3,0},{4,7},{5,6},{6,5},{7,4},{8,11},{9,10},{10,... | collective-permute-start | bytes 884744 | tf_op jit(solution)/shard_map/ppermute | solution.py:428

commit v5 on v4

--- a/solution.py
+++ b/solution.py
@@ -321,7 +321,7 @@
         total = fill(pieces, (doms + k // 2) * pair) + jnp.where(left, totals[k], totals[k + 1])
         sum_ref[:, k * count : (k + 2) * count] = total.astype(BF16)
 
-    width = 256
+    width = 512
     cos_x, sin_x = phases_x(width)
     picks = table_picks(jnp.concatenate(groups, axis=0), jnp.concatenate(foci, axis=0))
     cos_rows, sin_rows = phases_y(dom * QUART, QUART // 128)
@@ -401,7 +401,6 @@
     far = lax.ppermute(own, ("yh", "yl"), flip)
 
     flat = refs.reshape(count_refs, 2 * PIX)
-    flat, ctf_late, noise_late = lax.optimization_barrier((flat, ctf_table, noise_inv))
     tables = pl.pallas_call(
         tables_kernel,
         in_specs=[vmem] * 2,
@@ -409,8 +408,8 @@
         out_shape=shape((TABLE_ROWS, PIX), BF16),
         compiler_params=params(VMEM_LIMIT // 3),
         name="tables",
-    )(ctf_late, noise_late)
-    side, _, flat, tables = lax.optimization_barrier((side, far, flat, tables))
+    )(ctf_table, noise_inv)
+    side, _, flat = lax.optimization_barrier((side, far, flat))
     corner = lax.ppermute(side, ("yh", "yl"), flip)
 
     early = pl.pallas_call(

time: 77.7 us -> 79.4 us (1.022)
  waiting for transfers between devices: 0.6 us -> 1.94 us
  local copies, waits for them, and re-layouts: 6 us -> 4.69 us
  starting transfers between devices: 12.5 us -> 13.7 us
    ppermute x1, waiting for transfers between devices: 0.01 us -> 1.92 us  [on_device(): far = lax.ppermute(own, ('yh', 'yl'), flip)]
    unnamed x9 -> x11, local copies, waits for them, and re-layouts: 5.92 us -> 4.61 us
    ppermute x1, starting transfers between devices: 1.49 us -> 2.61 us  [on_device(): corner = lax.ppermute(side, ('yh', 'yl'), flip)]
  transfers between devices with their start and end apart: 9 -> 9, of which waited for: 1 -> 1; matrix products, arithmetic and copies ran while one was open for 6% -> 4% of each run, Pallas kernels for 9% -> 10%
where the time goes in v5:
time: 79.4 us; the launch traced here: 79.1 us
  blocking collectives  42 us (53%)
  Pallas kernels  14.7 us (19%)
  starting transfers between devices  13.7 us (17%)
  local copies, waits for them, and re-layouts  4.69 us (6%)
  between operations  2.04 us (3%)
  waiting for transfers between devices  1.94 us (2%)
    all_to_all x1, blocking collectives, on_device(): own = lax.all_to_all(payload, ('x', 'zh'), 0, 0, tiled=True)  24.4 us
    all_to_all x1, blocking collectives, on_device(): stats_all = lax.all_to_all(stats, AXES, 0, 0, tiled=True)  17.6 us
    ppermute x6, starting transfers between devices, share(): lax.ppermute(parts[k], ('yl', 'c'), moves[k])  7.42 us
    unnamed x11, local copies, waits for them, and re-layouts  4.61 us
    pallas_call x1, Pallas kernels, on_device(): pl.pallas_call(score_kernel, in_specs=[smem] + [vmem] * 8, out_specs=[vme...  4.44 us
    pallas_call x1, Pallas kernels, on_device(): pl.pallas_call(functools.partial(final_kernel, scale=scale), in_specs=[sm...  4.3 us
    ppermute x1, starting transfers between devices, on_device(): far = lax.ppermute(own, ('yh', 'yl'), flip)  2.73 us
    ppermute x1, starting transfers between devices, on_device(): corner = lax.ppermute(side, ('yh', 'yl'), flip)  2.61 us
  transfers between devices with their start and end apart: 9, of which 1 were waited for; matrix products, arithmetic and copies ran while one was open for 4% of the time, Pallas kernels for 10%

profile of v5, /device:TPU:1, one launch (start us, length us, event | category | flops | bytes accessed | tf_op | source)
XLA Modules:
  0.0 79.1 jit_solution(16929302723281748392)
XLA Ops:
  1.9 2.5 %prep.1 = bf16[128,1152]{1,0:T(8,128)(2,1)} custom-call(s32[2,9]{1,0:T(2,128)} %bitcast.32, s32[1]{0:T(128)S(6)} %copy.15.groups, s32[1]{0:T(128)S(6)} %copy.16.defocus, bf16[1,2,4096]{2,1,0:T(2,128)(2,1)} %image_hbm.1, f32[8,4096]{1,0:T(8,128)} %noise_ref.1, f32[64,4096]{1,0:T(8,128)} %ctf_ref.1), custom_call_target="tpu_custom_call" | custom-call | tf_op jit(solution)/shard_map/prep/pallas_call | solution.py:384
  4.4 24.4 %all_to_all.22 = bf16[16,8,1152]{2,1,0:T(8,128)(2,1)S(1)} all-to-all(bf16[16,8,1152]{2,1,0:T(8,128)(2,1)} %bitcast.31), channel_id=1, replica_groups=mesh['x'=4,'yh'=2,'zh'=4,'zl'=2,'yl'=2,'c'=2] {'x','zh'}, dimensions={0} | all-to-all | bytes 589824 | tf_op jit(solution)/shard_map/all_to_all | solution.py:399
  28.9 0.9 %collective-permute-start = (bf16[128,1152]{1,0:T(8,128)(2,1)S(1)}, bf16[128,1152]{1,0:T(8,128)(2,1)}, u32[]{:S(2)}, u32[]{:S(2)}) collective-permute-start(bf16[128,1152]{1,0:T(8,128)(2,1)S(1)} %bitcast.23), channel_id=1, source_target_pairs={{0,4},{4,0},{1,5},{5,1},{2,6},{6,2},{3,7},{7,3},{8,12},{12,8},{9,1... | collective-permute-start | bytes 884744 | tf_op jit(solution)/shard_map/ppermute | solution.py:400
  29.8 2.7 %collective-permute-start.1 = (bf16[128,1152]{1,0:T(8,128)(2,1)S(1)}, bf16[128,1152]{1,0:T(8,128)(2,1)S(1)}, u32[]{:S(2)}, u32[]{:S(2)}) collective-permute-start(bf16[128,1152]{1,0:T(8,128)(2,1)S(1)} %bitcast.24), channel_id=1, source_target_pairs={{0,34},{2,32},{32,2},{34,0},{1,35},{3,33},{33,3},{35,1},{4,38},{6,... | collective-permute-start | bytes 884744 | tf_op jit(solution)/shard_map/ppermute | solution.py:401
  32.5 3.0 %copy.14 = bf16[16,8,2,4096]{3,1,2,0:T(8,128)(2,1)S(1)} copy(bf16[16,8,2,4096]{3,2,1,0:T(2,128)(2,1)} %bitcast.30) | data formatting | bytes 4194304
  35.5 0.0 copy-start.4
  35.5 0.0 collective-permute-done.side_ref
  35.5 1.9 %collective-permute-done.1.far_ref = bf16[128,1152]{1,0:T(8,128)(2,1)S(1)} collective-permute-done((bf16[128,1152]{1,0:T(8,128)(2,1)S(1)}, bf16[128,1152]{1,0:T(8,128)(2,1)S(1)}, u32[]{:S(2)}, u32[]{:S(2)}) %collective-permute-start.1) | collective-permute-done | bytes 294944 | tf_op jit(solution)/shard_map/ppermute | solution.py:401
  37.4 0.7 copy-done.2
  38.2 2.6 %collective-permute-start.5 = (bf16[128,1152]{1,0:T(8,128)(2,1)}, bf16[128,1152]{1,0:T(8,128)(2,1)}, u32[]{:S(2)}, u32[]{:S(2)}) collective-permute-start(bf16[128,1152]{1,0:T(8,128)(2,1)} %collective-permute-done.side_ref), channel_id=1, source_target_pairs={{0,34},{2,32},{32,2},{34,0},{1,35},{3,33},{33,3},{35,1},{4,38},{6,... | collective-permute-start | bytes 884744 | tf_op jit(solution)/shard_map/ppermute | solution.py:413
  40.8 0.1 stack.23.place
  40.9 1.2 %quarters.1 = (bf16[64,1152]{1,0:T(8,128)(2,1)S(1)}, bf16[64,1152]{1,0:T(8,128)(2,1)S(1)}, bf16[64,1152]{1,0:T(8,128)(2,1)S(1)}, bf16[64,1152]{1,0:T(8,128)(2,1)S(1)}) custom-call(s32[5]{0:T(128)S(1)} %stack.23.place, bf16[128,1152]{1,0:T(8,128)(2,1)S(1)} %bitcast.25, bf16[128,1152]{1,0:T(8,128)(2,1)} %collective-permute-done.side_ref), custom_call_target="tpu_custom_call" | custom-call | tf_op jit(solution)/shard_map/quarters/pallas_call | solution.py:415
  42.1 3.5 %collective-permute-start.2 = (bf16[64,1152]{1,0:T(8,128)(2,1)S(1)}, bf16[64,1152]{1,0:T(8,128)(2,1)S(1)}, u32[]{:S(2)}, u32[]{:S(2)}) collective-permute-start(bf16[64,1152]{1,0:T(8,128)(2,1)S(1)} %get-tuple-element.35), channel_id=1, source_target_pairs={{0,1},{1,0},{2,3},{3,2},{4,5},{5,4},{6,7},{7,6},{8,9},{9,8},{10,11... | collective-permute-start | bytes 442376 | tf_op jit(solution)/shard_map/ppermute | solution.py:427
  45.6 0.0 collective-permute-start.3
  45.6 1.7 %collective-permute-start.4 = (bf16[64,1152]{1,0:T(8,128)(2,1)S(1)}, bf16[64,1152]{1,0:T(8,128)(2,1)S(1)}, u32[]{:S(2)}, u32[]{:S(2)}) collective-permute-start(bf16[64,1152]{1,0:T(8,128)(2,1)S(1)} %get-tuple-element.37), channel_id=1, source_target_pairs={{0,3},{1,2},{2,1},{3,0},{4,7},{5,6},{6,5},{7,4},{8,11},{9,10},{10,... | collective-permute-start | bytes 442376 | tf_op jit(solution)/shard_map/ppermute | solution.py:427
  47.3 0.0 copy-done
  47.3 0.9 %copy-done.1 = f32[8,4096]{1,0:T(8,128)S(1)} copy-done((f32[8,4096]{1,0:T(8,128)S(1)}, f32[8,4096]{1,0:T(8,128)}, u32[]{:S(2)}) %copy-start.1) | copy-done | bytes 131096
  48.2 0.3 tables.1.tables_ref
  48.5 1.9 %turn_refs.1 = (bf16[2,384,4096]{2,1,0:T(8,128)(2,1)S(1)}, bf16[128,4096]{1,0:T(8,128)(2,1)S(1)}, f32[128,128]{1,0:T(8,128)S(1)}) custom-call(bf16[128,8192]{1,0:T(8,128)(2,1)S(1)} %bitcast.22, f32[1,128]{1,0:T(1,128)S(1)} %bitcast.29), custom_call_target="tpu_custom_call" | custom-call | flops 4194304 | bytes 10485760 | tf_op jit(solution)/shard_map/turn_refs/pallas_call | solution.py:431
  50.4 0.0 collective-permute-done.5.corner_ref
  50.5 4.4 %score.1 = (bf16[128,1152]{1,0:T(8,128)(2,1)S(1)}, bf16[128,1152]{1,0:T(8,128)(2,1)S(1)}, bf16[128,1152]{1,0:T(8,128)(2,1)S(1)}, bf16[128,1152]{1,0:T(8,128)(2,1)S(1)}, f32[256,128]{1,0:T(8,128)S(1)}) custom-call(s32[5]{0:T(128)S(1)} %stack.23.place, bf16[128,1152]{1,0:T(8,128)(2,1)S(1)} %bitcast.26, bf16[128,1152]{1,0:T(8,128)(2,1)} %collective-permute-done.side_ref, ...), custom_call_target="tpu_custom_call" | custom-call | flops 1207959552 | bytes 10485760 | tf_op jit(solution)/shard_map/score/pallas_call | solution.py:448
  54.9 0.0 collective-permute-done.2.e1_ref
  54.9 0.0 collective-permute-done.3.e2_ref
  54.9 0.0 collective-permute-done.4.e3_ref
  54.9 0.2 collective-permute-start.6
  55.2 0.0 collective-permute-start.7
  55.2 2.0 %collective-permute-start.8 = (bf16[128,1152]{1,0:T(8,128)(2,1)S(1)}, bf16[128,1152]{1,0:T(8,128)(2,1)S(1)}, u32[]{:S(2)}, u32[]{:S(2)}) collective-permute-start(bf16[128,1152]{1,0:T(8,128)(2,1)S(1)} %get-tuple-element.54), channel_id=1, source_target_pairs={{0,3},{1,2},{2,1},{3,0},{4,7},{5,6},{6,5},{7,4},{8,11},{9,10},{10,... | collective-permute-start | bytes 884744 | tf_op jit(solution)/shard_map/ppermute | solution.py:427
  57.2 17.6 %all_to_all.23 = f32[256,1,128]{2,1,0:T(1,128)S(1)} all-to-all(f32[256,1,128]{2,1,0:T(1,128)S(1)} %bitcast.28), channel_id=1, replica_groups=mesh['x'=4,'yh'=2,'zh'=4,'zl'=2,'yl'=2,'c'=2] {'x','yh','zh','zl','yl','c'}, dimensions={0} | all-to-all | bytes 262144 | tf_op jit(solution)/shard_map/all_to_all | solution.py:463
  74.8 0.0 collective-permute-done.6.q1_ref
  74.8 0.0 collective-permute-done.7.q2_ref
  74.8 0.0 collective-permute-done.8.q3_ref
  74.8 4.3 %insert.1 = (f32[2048,128]{1,0:T(8,128)}, f32[128,1024]{1,0:T(8,128)}, f32[1]{0:T(128)}) custom-call(s32[5]{0:T(128)S(1)} %stack.23.place, bf16[64,1152]{1,0:T(8,128)(2,1)S(1)} %get-tuple-element.47.e0_ref, bf16[64,1152]{1,0:T(8,128)(2,1)S(1)} %collective-permute-done.2.e1_ref, bf16[64,1152]{1,0:T(8,128)(2,1)S(1)} %collective-permute-done.3.e2_ref, ...), custom_call_target="tpu_custom_call" | custom-call | tf_op jit(solution)/shard_map/insert/pallas_call | solution.py:465
  (6 shorter events, 0.0 us)
Async XLA Ops:
  28.9 6.6 %collective-permute-start = (bf16[128,1152]{1,0:T(8,128)(2,1)S(1)}, bf16[128,1152]{1,0:T(8,128)(2,1)}, u32[]{:S(2)}, u32[]{:S(2)}) collective-permute-start(bf16[128,1152]{1,0:T(8,128)(2,1)S(1)} %bitcast.23), channel_id=1, source_target_pairs={{0,4},{4,0},{1,5},{5,1},{2,6},{6,2},{3,7},{7,3},{8,12},{12,8},{9,1... | collective-permute-start | bytes 884744 | tf_op jit(solution)/shard_map/ppermute | solution.py:400
  29.8 7.7 %collective-permute-start.1 = (bf16[128,1152]{1,0:T(8,128)(2,1)S(1)}, bf16[128,1152]{1,0:T(8,128)(2,1)S(1)}, u32[]{:S(2)}, u32[]{:S(2)}) collective-permute-start(bf16[128,1152]{1,0:T(8,128)(2,1)S(1)} %bitcast.24), channel_id=1, source_target_pairs={{0,34},{2,32},{32,2},{34,0},{1,35},{3,33},{33,3},{35,1},{4,38},{6,... | collective-permute-start | bytes 884744 | tf_op jit(solution)/shard_map/ppermute | solution.py:401
  32.5 14.8 %copy-start = (f32[64,4096]{1,0:T(8,128)S(1)}, f32[64,4096]{1,0:T(8,128)}, u32[]{:S(2)}) copy-start(f32[64,4096]{1,0:T(8,128)} %ctf_ref.1) | copy-start | bytes 3145732
  35.5 13.0 %copy-start.4 = (f32[128]{0:T(128)S(1)}, f32[128]{0:T(128)}, u32[]{:S(2)}) copy-start(f32[128]{0:T(128)} %param.13) | copy-start | bytes 1540
  37.4 0.7 copy-start.2
  38.2 12.3 %collective-permute-start.5 = (bf16[128,1152]{1,0:T(8,128)(2,1)}, bf16[128,1152]{1,0:T(8,128)(2,1)}, u32[]{:S(2)}, u32[]{:S(2)}) collective-permute-start(bf16[128,1152]{1,0:T(8,128)(2,1)} %collective-permute-done.side_ref), channel_id=1, source_target_pairs={{0,34},{2,32},{32,2},{34,0},{1,35},{3,33},{33,3},{35,1},{4,38},{6,... | collective-permute-start | bytes 884744 | tf_op jit(solution)/shard_map/ppermute | solution.py:413
  42.1 12.8 %collective-permute-start.2 = (bf16[64,1152]{1,0:T(8,128)(2,1)S(1)}, bf16[64,1152]{1,0:T(8,128)(2,1)S(1)}, u32[]{:S(2)}, u32[]{:S(2)}) collective-permute-start(bf16[64,1152]{1,0:T(8,128)(2,1)S(1)} %get-tuple-element.35), channel_id=1, source_target_pairs={{0,1},{1,0},{2,3},{3,2},{4,5},{5,4},{6,7},{7,6},{8,9},{9,8},{10,11... | collective-permute-start | bytes 442376 | tf_op jit(solution)/shard_map/ppermute | solution.py:427
  45.6 9.4 %collective-permute-start.3 = (bf16[64,1152]{1,0:T(8,128)(2,1)S(1)}, bf16[64,1152]{1,0:T(8,128)(2,1)S(1)}, u32[]{:S(2)}, u32[]{:S(2)}) collective-permute-start(bf16[64,1152]{1,0:T(8,128)(2,1)S(1)} %get-tuple-element.36), channel_id=1, source_target_pairs={{0,2},{1,3},{2,0},{3,1},{4,6},{5,7},{6,4},{7,5},{8,10},{9,11},{10,... | collective-permute-start | bytes 442376 | tf_op jit(solution)/shard_map/ppermute | solution.py:427
  45.6 9.4 %collective-permute-start.4 = (bf16[64,1152]{1,0:T(8,128)(2,1)S(1)}, bf16[64,1152]{1,0:T(8,128)(2,1)S(1)}, u32[]{:S(2)}, u32[]{:S(2)}) collective-permute-start(bf16[64,1152]{1,0:T(8,128)(2,1)S(1)} %get-tuple-element.37), channel_id=1, source_target_pairs={{0,3},{1,2},{2,1},{3,0},{4,7},{5,6},{6,5},{7,4},{8,11},{9,10},{10,... | collective-permute-start | bytes 442376 | tf_op jit(solution)/shard_map/ppermute | solution.py:427
  47.3 0.9 %copy-start.1 = (f32[8,4096]{1,0:T(8,128)S(1)}, f32[8,4096]{1,0:T(8,128)}, u32[]{:S(2)}) copy-start(f32[8,4096]{1,0:T(8,128)} %noise_ref.1) | copy-start | bytes 393220
  48.2 2.3 %copy-start.3 = (bf16[128,1152]{1,0:T(8,128)(2,1)S(1)}, bf16[128,1152]{1,0:T(8,128)(2,1)}, u32[]{:S(2)}) copy-start(bf16[128,1152]{1,0:T(8,128)(2,1)} %copy-done.2) | copy-start | bytes 884740
  54.9 19.8 %collective-permute-start.6 = (bf16[128,1152]{1,0:T(8,128)(2,1)S(1)}, bf16[128,1152]{1,0:T(8,128)(2,1)S(1)}, u32[]{:S(2)}, u32[]{:S(2)}) collective-permute-start(bf16[128,1152]{1,0:T(8,128)(2,1)S(1)} %get-tuple-element.52), channel_id=1, source_target_pairs={{0,1},{1,0},{2,3},{3,2},{4,5},{5,4},{6,7},{7,6},{8,9},{9,8},{10,11... | collective-permute-start | bytes 884744 | tf_op jit(solution)/shard_map/ppermute | solution.py:427
  55.2 19.6 %collective-permute-start.7 = (bf16[128,1152]{1,0:T(8,128)(2,1)S(1)}, bf16[128,1152]{1,0:T(8,128)(2,1)S(1)}, u32[]{:S(2)}, u32[]{:S(2)}) collective-permute-start(bf16[128,1152]{1,0:T(8,128)(2,1)S(1)} %get-tuple-element.53), channel_id=1, source_target_pairs={{0,2},{1,3},{2,0},{3,1},{4,6},{5,7},{6,4},{7,5},{8,10},{9,11},{10,... | collective-permute-start | bytes 884744 | tf_op jit(solution)/shard_map/ppermute | solution.py:427
  55.2 19.6 %collective-permute-start.8 = (bf16[128,1152]{1,0:T(8,128)(2,1)S(1)}, bf16[128,1152]{1,0:T(8,128)(2,1)S(1)}, u32[]{:S(2)}, u32[]{:S(2)}) collective-permute-start(bf16[128,1152]{1,0:T(8,128)(2,1)S(1)} %get-tuple-element.54), channel_id=1, source_target_pairs={{0,3},{1,2},{2,1},{3,0},{4,7},{5,6},{6,5},{7,4},{8,11},{9,10},{10,... | collective-permute-start | bytes 884744 | tf_op jit(solution)/shard_map/ppermute | solution.py:427

commit v6 on v4

--- a/solution.py
+++ b/solution.py
@@ -178,7 +178,7 @@
     return jnp.where(flag == 1, other, row)
 
 
-def quarter_kernel(place, own_ref, side_ref, q0_ref, q1_ref, q2_ref, q3_ref, wide_ref):
+def quarter_kernel(place, own_ref, side_ref, flat_ref, q0_ref, q1_ref, q2_ref, q3_ref, wide_ref):
     outs = (q0_ref, q1_ref, q2_ref, q3_ref)
     count = 2 * own_ref.shape[0] // 8
     chunk, codes = unpack((own_ref, side_ref), wide_ref)
@@ -206,11 +206,13 @@
     self_term = jnp.zeros((refs, count), F32)
     for j in range(4):
         at = slice(j * QUART, (j + 1) * QUART)
+        ctf_power = ctf_power_rows(picks, tables_ref[:, at])
+        self_term += lax.dot_general(power_ref[:, at], ctf_power, NT, preferred_element_type=F32)
+    for j in range(4):
+        at = slice(j * QUART, (j + 1) * QUART)
         for c, parts in enumerate(shift_x(chunk(j, 0, count), chunk(j + 4, 0, count), cos_x, sin_x)):
             new = jnp.concatenate(parts, axis=0).astype(BF16)
             cross += lax.dot_general(turned_ref[c, :, at], new, NT, preferred_element_type=F32)
-        ctf_power = ctf_power_rows(picks, tables_ref[:, at])
-        self_term += lax.dot_general(power_ref[:, at], ctf_power, NT, preferred_element_type=F32)
         part = place[0] ^ j
         late = jnp.concatenate([chunk(part, half, half), chunk(part + 4, half, half)], axis=0).astype(BF16)
         for side in range(2):
@@ -260,7 +262,7 @@
 
 def final_kernel(
     place, e0_ref, e1_ref, e2_ref, e3_ref, q0_ref, q1_ref, q2_ref, q3_ref, stats_ref, tables_ref,
-    data_ref, weight_ref, evidence_ref, post_ref, sum_ref, *, scale,
+    data_ref, weight_ref, evidence_ref, post_ref, sum_ref, power_ref, *, scale,
 ):
     dom, orient, y_hi, z_lo, mine = place[0], place[1], place[2], place[3], place[4]
     early = (e0_ref, e1_ref, e2_ref, e3_ref)
@@ -296,6 +298,12 @@
         groups += [first[:, 0:1], notes[:, spot : spot + 1]]
         foci += [first[:, 1:2], notes[:, spot + 1 : spot + 2]]
 
+    picks = table_picks(jnp.concatenate(groups, axis=0), jnp.concatenate(foci, axis=0))
+    for n in range(4):
+        at = slice(n * QUART // 4, (n + 1) * QUART // 4)
+        start = pl.multiple_of(dom * QUART + n * QUART // 4, QUART // 4)
+        power_ref[:, at] = ctf_power_rows(picks, tables_ref[:, pl.ds(start, QUART // 4)])
+
     def fill(pieces, spot):
         total = jnp.zeros((refs, pair), F32)
         for b in range(3):
@@ -321,14 +329,12 @@
         total = fill(pieces, (doms + k // 2) * pair) + jnp.where(left, totals[k], totals[k + 1])
         sum_ref[:, k * count : (k + 2) * count] = total.astype(BF16)
 
-    width = 256
+    width = 512
     cos_x, sin_x = phases_x(width)
-    picks = table_picks(jnp.concatenate(groups, axis=0), jnp.concatenate(foci, axis=0))
     cos_rows, sin_rows = phases_y(dom * QUART, QUART // 128)
     cos_rows, sin_rows = cos_rows * scale, sin_rows * scale
     for n in range(QUART // width):
         at = slice(n * width, (n + 1) * width)
-        wide_at = pl.ds(pl.multiple_of(dom * QUART + n * width, width), width)
         reals, imags = [], []
         side = 2 * n * width // QUART
         late_at = slice(5 * refs + n * width - side * QUART // 2, 5 * refs + (n + 1) * width - side * QUART // 2)
@@ -360,8 +366,7 @@
             for c in range(2):
                 first = 2 * (n * (width // 128) + tile) + c
                 data_ref[pl.ds(first, refs, stride=2 * (QUART // 128)), :] = both[c][:, 128 * tile : 128 * (tile + 1)]
-        ctf_power = ctf_power_rows(picks, tables_ref[:, wide_at])
-        weight_ref[:, at] = lax.dot_general(sum_ref[...], ctf_power, NN, preferred_element_type=F32) * scale
+        weight_ref[:, at] = lax.dot_general(sum_ref[...], power_ref[:, at], NN, preferred_element_type=F32) * scale
 
 
 def on_device(images, offsets, groups, defocus, refs, log_prior, noise_inv, ctf_table):
@@ -415,13 +420,13 @@
 
     early = pl.pallas_call(
         quarter_kernel,
-        in_specs=[smem] + [vmem] * 2,
+        in_specs=[smem] + [vmem] * 3,
         out_specs=[vmem] * 4,
         out_shape=[shape((orients, WIDE), BF16)] * 4,
         scratch_shapes=[pltpu.VMEM((4 * orients * (WIDE // 128), 128), F32)],
         compiler_params=params(VMEM_LIMIT // 3),
         name="quarters",
-    )(place, own, side)
+    )(place, own, side, flat)
 
     def share(parts):
         moves = [[(d, d ^ k) for d in range(4)] for k in range(4)]
@@ -470,6 +475,7 @@
         scratch_shapes=[
             pltpu.VMEM((3 * count_refs, 12 * orients), BF16),
             pltpu.VMEM((count_refs, 4 * orients), BF16),
+            pltpu.VMEM((4 * orients, QUART), BF16),
         ],
         out_shape=[
             shape((2 * count_refs * (QUART // 128), 128), F32),

time: 77.7 us -> 77.2 us (level)
  local copies, waits for them, and re-layouts: 6 us -> 4.34 us
  waiting for transfers between devices: 0.6 us -> 1.83 us
    unnamed x9 -> x11, local copies, waits for them, and re-layouts: 5.92 us -> 4.25 us
    ppermute x6, waiting for transfers between devices: 0.02 us -> 1.19 us  [share(): lax.ppermute(parts[k], ('yl', 'c'), moves[k])]
  transfers between devices with their start and end apart: 9 -> 9, of which waited for: 1 -> 2; matrix products, arithmetic and copies ran while one was open for 6% -> 4% of each run, Pallas kernels for 9% -> 9%
where the time goes in v6:
time: 77.2 us; the launch traced here: 77 us
  blocking collectives  42.3 us (55%)
  Pallas kernels  13.8 us (18%)
  starting transfers between devices  12.7 us (16%)
  local copies, waits for them, and re-layouts  4.34 us (6%)
  between operations  2.03 us (3%)
  waiting for transfers between devices  1.83 us (2%)
    all_to_all x1, blocking collectives, on_device(): own = lax.all_to_all(payload, ('x', 'zh'), 0, 0, tiled=True)  24.4 us
    all_to_all x1, blocking collectives, on_device(): stats_all = lax.all_to_all(stats, AXES, 0, 0, tiled=True)  17.9 us
    ppermute x6, starting transfers between devices, share(): lax.ppermute(parts[k], ('yl', 'c'), moves[k])  7.52 us
    pallas_call x1, Pallas kernels, on_device(): pl.pallas_call(functools.partial(final_kernel, scale=scale), in_specs=[sm...  4.39 us
    unnamed x11, local copies, waits for them, and re-layouts  4.25 us
    pallas_call x1, Pallas kernels, on_device(): pl.pallas_call(score_kernel, in_specs=[smem] + [vmem] * 8, out_specs=[vme...  3.86 us
    ppermute x1, starting transfers between devices, on_device(): far = lax.ppermute(own, ('yh', 'yl'), flip)  2.73 us
    pallas_call x1, Pallas kernels, on_device(): pl.pallas_call(prep_kernel, in_specs=[smem] * 3 + [hbm] * 3, out_specs=vm...  2.52 us
  transfers between devices with their start and end apart: 9, of which 2 were waited for; matrix products, arithmetic and copies ran while one was open for 4% of the time, Pallas kernels for 9%

profile of v6, /device:TPU:1, one launch (start us, length us, event | category | flops | bytes accessed | tf_op | source)
XLA Modules:
  0.0 77.0 jit_solution(17180314464017830042)
XLA Ops:
  1.9 2.5 %prep.1 = bf16[128,1152]{1,0:T(8,128)(2,1)} custom-call(s32[2,9]{1,0:T(2,128)} %bitcast.33, s32[1]{0:T(128)S(6)} %copy.15.groups, s32[1]{0:T(128)S(6)} %copy.16.defocus, bf16[1,2,4096]{2,1,0:T(2,128)(2,1)} %image_hbm.1, f32[8,4096]{1,0:T(8,128)} %noise_ref, f32[64,4096]{1,0:T(8,128)} %ctf_ref), custom_call_target="tpu_custom_call" | custom-call | tf_op jit(solution)/shard_map/prep/pallas_call | solution.py:389
  4.4 24.4 %all_to_all.22 = bf16[16,8,1152]{2,1,0:T(8,128)(2,1)S(1)} all-to-all(bf16[16,8,1152]{2,1,0:T(8,128)(2,1)} %bitcast.32), channel_id=1, replica_groups=mesh['x'=4,'yh'=2,'zh'=4,'zl'=2,'yl'=2,'c'=2] {'x','zh'}, dimensions={0} | all-to-all | bytes 589824 | tf_op jit(solution)/shard_map/all_to_all | solution.py:404
  28.9 2.7 %collective-permute-start.1 = (bf16[128,1152]{1,0:T(8,128)(2,1)S(1)}, bf16[128,1152]{1,0:T(8,128)(2,1)S(1)}, u32[]{:S(2)}, u32[]{:S(2)}) collective-permute-start(bf16[128,1152]{1,0:T(8,128)(2,1)S(1)} %bitcast.24), channel_id=1, source_target_pairs={{0,34},{2,32},{32,2},{34,0},{1,35},{3,33},{33,3},{35,1},{4,38},{6,... | collective-permute-start | bytes 884744 | tf_op jit(solution)/shard_map/ppermute | solution.py:406
  31.6 0.9 %collective-permute-start = (bf16[128,1152]{1,0:T(8,128)(2,1)S(1)}, bf16[128,1152]{1,0:T(8,128)(2,1)S(1)}, u32[]{:S(2)}, u32[]{:S(2)}) collective-permute-start(bf16[128,1152]{1,0:T(8,128)(2,1)S(1)} %bitcast.25), channel_id=1, source_target_pairs={{0,4},{4,0},{1,5},{5,1},{2,6},{6,2},{3,7},{7,3},{8,12},{12,8},{9,1... | collective-permute-start | bytes 884744 | tf_op jit(solution)/shard_map/ppermute | solution.py:405
  32.5 3.0 %copy.14 = bf16[16,8,2,4096]{3,1,2,0:T(8,128)(2,1)S(1)} copy(bf16[16,8,2,4096]{3,2,1,0:T(2,128)(2,1)} %bitcast.31) | data formatting | bytes 4194304
  35.5 0.0 copy-done.2
  35.5 0.0 copy-done.3
  35.5 0.3 tables.1.tables_ref
  35.9 0.0 copy-start
  35.9 1.3 %copy-done = bf16[224,4096]{1,0:T(8,128)(2,1)} copy-done((bf16[224,4096]{1,0:T(8,128)(2,1)}, bf16[224,4096]{1,0:T(8,128)(2,1)S(1)}, u32[]{:S(2)}) %copy-start) | copy-done | bytes 1835032
  37.1 0.0 collective-permute-done.1.far_ref
  37.1 0.6 collective-permute-done.side_ref
  37.8 1.5 %collective-permute-start.5 = (bf16[128,1152]{1,0:T(8,128)(2,1)S(1)}, bf16[128,1152]{1,0:T(8,128)(2,1)S(1)}, u32[]{:S(2)}, u32[]{:S(2)}) collective-permute-start(bf16[128,1152]{1,0:T(8,128)(2,1)S(1)} %collective-permute-done.side_ref), channel_id=1, source_target_pairs={{0,34},{2,32},{32,2},{34,0},{1,35},{3,33},{33,3},{35,1},{4,38},{6,... | collective-permute-start | bytes 884744 | tf_op jit(solution)/shard_map/ppermute | solution.py:419
  39.3 0.1 stack.23.place
  39.3 0.8 %quarters.1 = (bf16[64,1152]{1,0:T(8,128)(2,1)S(1)}, bf16[64,1152]{1,0:T(8,128)(2,1)S(1)}, bf16[64,1152]{1,0:T(8,128)(2,1)S(1)}, bf16[64,1152]{1,0:T(8,128)(2,1)S(1)}) custom-call(s32[5]{0:T(128)S(1)} %stack.23.place, bf16[128,1152]{1,0:T(8,128)(2,1)S(1)} %bitcast.26, bf16[128,1152]{1,0:T(8,128)(2,1)S(1)} %collective-permute-done.side_ref, ...), custom_call_target="tpu_custom_call" | custom-call | tf_op jit(solution)/shard_map/quarters/pallas_call | solution.py:421
  40.2 3.4 %collective-permute-start.2 = (bf16[64,1152]{1,0:T(8,128)(2,1)S(1)}, bf16[64,1152]{1,0:T(8,128)(2,1)S(1)}, u32[]{:S(2)}, u32[]{:S(2)}) collective-permute-start(bf16[64,1152]{1,0:T(8,128)(2,1)S(1)} %get-tuple-element.42), channel_id=1, source_target_pairs={{0,1},{1,0},{2,3},{3,2},{4,5},{5,4},{6,7},{7,6},{8,9},{9,8},{10,11... | collective-permute-start | bytes 442376 | tf_op jit(solution)/shard_map/ppermute | solution.py:433
  43.5 0.0 collective-permute-start.3
  43.5 1.7 %collective-permute-start.4 = (bf16[64,1152]{1,0:T(8,128)(2,1)S(1)}, bf16[64,1152]{1,0:T(8,128)(2,1)S(1)}, u32[]{:S(2)}, u32[]{:S(2)}) collective-permute-start(bf16[64,1152]{1,0:T(8,128)(2,1)S(1)} %get-tuple-element.44), channel_id=1, source_target_pairs={{0,3},{1,2},{2,1},{3,0},{4,7},{5,6},{6,5},{7,4},{8,11},{9,10},{10,... | collective-permute-start | bytes 442376 | tf_op jit(solution)/shard_map/ppermute | solution.py:433
  45.2 1.9 %turn_refs.1 = (bf16[2,384,4096]{2,1,0:T(8,128)(2,1)S(1)}, bf16[128,4096]{1,0:T(8,128)(2,1)S(1)}, f32[128,128]{1,0:T(8,128)S(1)}) custom-call(bf16[128,8192]{1,0:T(8,128)(2,1)S(1)} %bitcast.23, f32[1,128]{1,0:T(1,128)S(1)} %bitcast.30), custom_call_target="tpu_custom_call" | custom-call | flops 4194304 | bytes 10485760 | tf_op jit(solution)/shard_map/turn_refs/pallas_call | solution.py:437
  47.2 0.0 collective-permute-done.5.corner_ref
  47.2 3.9 %score.1 = (bf16[128,1152]{1,0:T(8,128)(2,1)S(1)}, bf16[128,1152]{1,0:T(8,128)(2,1)S(1)}, bf16[128,1152]{1,0:T(8,128)(2,1)S(1)}, bf16[128,1152]{1,0:T(8,128)(2,1)S(1)}, f32[256,128]{1,0:T(8,128)S(1)}) custom-call(s32[5]{0:T(128)S(1)} %stack.23.place, bf16[128,1152]{1,0:T(8,128)(2,1)S(1)} %bitcast.27, bf16[128,1152]{1,0:T(8,128)(2,1)S(1)} %collective-permute-done.side_ref, ...), custom_call_target="tpu_custom_call" | custom-call | flops 1207959552 | bytes 10485760 | tf_op jit(solution)/shard_map/score/pallas_call | solution.py:454
  51.1 0.0 collective-permute-done.2.e1_ref
  51.1 0.0 collective-permute-done.3.e2_ref
  51.1 1.2 %collective-permute-done.4.e3_ref = bf16[64,1152]{1,0:T(8,128)(2,1)S(1)} collective-permute-done((bf16[64,1152]{1,0:T(8,128)(2,1)S(1)}, bf16[64,1152]{1,0:T(8,128)(2,1)S(1)}, u32[]{:S(2)}, u32[]{:S(2)}) %collective-permute-start.4) | collective-permute-done | bytes 147488 | tf_op jit(solution)/shard_map/ppermute | solution.py:433
  52.3 0.7 collective-permute-start.6
  53.0 0.0 collective-permute-start.7
  53.0 1.7 %collective-permute-start.8 = (bf16[128,1152]{1,0:T(8,128)(2,1)S(1)}, bf16[128,1152]{1,0:T(8,128)(2,1)S(1)}, u32[]{:S(2)}, u32[]{:S(2)}) collective-permute-start(bf16[128,1152]{1,0:T(8,128)(2,1)S(1)} %get-tuple-element.62), channel_id=1, source_target_pairs={{0,3},{1,2},{2,1},{3,0},{4,7},{5,6},{6,5},{7,4},{8,11},{9,10},{10,... | collective-permute-start | bytes 884744 | tf_op jit(solution)/shard_map/ppermute | solution.py:433
  54.7 17.9 %all_to_all.23 = f32[256,1,128]{2,1,0:T(1,128)S(1)} all-to-all(f32[256,1,128]{2,1,0:T(1,128)S(1)} %bitcast.29), channel_id=1, replica_groups=mesh['x'=4,'yh'=2,'zh'=4,'zl'=2,'yl'=2,'c'=2] {'x','yh','zh','zl','yl','c'}, dimensions={0} | all-to-all | bytes 262144 | tf_op jit(solution)/shard_map/all_to_all | solution.py:469
  72.6 0.0 collective-permute-done.6.q1_ref
  72.6 0.0 collective-permute-done.7.q2_ref
  72.6 0.0 collective-permute-done.8.q3_ref
  72.6 4.4 %insert.1 = (f32[2048,128]{1,0:T(8,128)}, f32[128,1024]{1,0:T(8,128)}, f32[1]{0:T(128)}) custom-call(s32[5]{0:T(128)S(1)} %stack.23.place, bf16[64,1152]{1,0:T(8,128)(2,1)S(1)} %get-tuple-element.55.e0_ref, bf16[64,1152]{1,0:T(8,128)(2,1)S(1)} %collective-permute-done.2.e1_ref, bf16[64,1152]{1,0:T(8,128)(2,1)S(1)} %collective-permute-done.3.e2_ref, ...), custom_call_target="tpu_custom_call" | custom-call | tf_op jit(solution)/shard_map/insert/pallas_call | solution.py:471
  (6 shorter events, 0.0 us)
Async XLA Ops:
  28.9 8.2 %collective-permute-start.1 = (bf16[128,1152]{1,0:T(8,128)(2,1)S(1)}, bf16[128,1152]{1,0:T(8,128)(2,1)S(1)}, u32[]{:S(2)}, u32[]{:S(2)}) collective-permute-start(bf16[128,1152]{1,0:T(8,128)(2,1)S(1)} %bitcast.24), channel_id=1, source_target_pairs={{0,34},{2,32},{32,2},{34,0},{1,35},{3,33},{33,3},{35,1},{4,38},{6,... | collective-permute-start | bytes 884744 | tf_op jit(solution)/shard_map/ppermute | solution.py:406
  31.6 6.1 %collective-permute-start = (bf16[128,1152]{1,0:T(8,128)(2,1)S(1)}, bf16[128,1152]{1,0:T(8,128)(2,1)S(1)}, u32[]{:S(2)}, u32[]{:S(2)}) collective-permute-start(bf16[128,1152]{1,0:T(8,128)(2,1)S(1)} %bitcast.25), channel_id=1, source_target_pairs={{0,4},{4,0},{1,5},{5,1},{2,6},{6,2},{3,7},{7,3},{8,12},{12,8},{9,1... | collective-permute-start | bytes 884744 | tf_op jit(solution)/shard_map/ppermute | solution.py:405
  32.5 3.0 %copy-start.2 = (f32[64,4096]{1,0:T(8,128)S(1)}, f32[64,4096]{1,0:T(8,128)}, u32[]{:S(2)}) copy-start(f32[64,4096]{1,0:T(8,128)} %ctf_ref) | copy-start | bytes 3145732
  32.5 3.0 %copy-start.3 = (f32[8,4096]{1,0:T(8,128)S(1)}, f32[8,4096]{1,0:T(8,128)}, u32[]{:S(2)}) copy-start(f32[8,4096]{1,0:T(8,128)} %noise_ref) | copy-start | bytes 393220
  35.9 1.3 %copy-start = (bf16[224,4096]{1,0:T(8,128)(2,1)}, bf16[224,4096]{1,0:T(8,128)(2,1)S(1)}, u32[]{:S(2)}) copy-start(bf16[224,4096]{1,0:T(8,128)(2,1)S(1)} %tables.1.tables_ref) | copy-start | bytes 5505028
  37.1 8.1 %copy-start.4 = (f32[128]{0:T(128)S(1)}, f32[128]{0:T(128)}, u32[]{:S(2)}) copy-start(f32[128]{0:T(128)} %param.13) | copy-start | bytes 1540
  37.8 9.4 %collective-permute-start.5 = (bf16[128,1152]{1,0:T(8,128)(2,1)S(1)}, bf16[128,1152]{1,0:T(8,128)(2,1)S(1)}, u32[]{:S(2)}, u32[]{:S(2)}) collective-permute-start(bf16[128,1152]{1,0:T(8,128)(2,1)S(1)} %collective-permute-done.side_ref), channel_id=1, source_target_pairs={{0,34},{2,32},{32,2},{34,0},{1,35},{3,33},{33,3},{35,1},{4,38},{6,... | collective-permute-start | bytes 884744 | tf_op jit(solution)/shard_map/ppermute | solution.py:419
  39.3 7.9 %copy-start.1 = (bf16[224,4096]{1,0:T(8,128)(2,1)S(1)}, bf16[224,4096]{1,0:T(8,128)(2,1)}, u32[]{:S(2)}) copy-start(bf16[224,4096]{1,0:T(8,128)(2,1)} %copy-done) | copy-start | bytes 5505028
  40.2 10.9 %collective-permute-start.2 = (bf16[64,1152]{1,0:T(8,128)(2,1)S(1)}, bf16[64,1152]{1,0:T(8,128)(2,1)S(1)}, u32[]{:S(2)}, u32[]{:S(2)}) collective-permute-start(bf16[64,1152]{1,0:T(8,128)(2,1)S(1)} %get-tuple-element.42), channel_id=1, source_target_pairs={{0,1},{1,0},{2,3},{3,2},{4,5},{5,4},{6,7},{7,6},{8,9},{9,8},{10,11... | collective-permute-start | bytes 442376 | tf_op jit(solution)/shard_map/ppermute | solution.py:433
  43.5 7.6 %collective-permute-start.3 = (bf16[64,1152]{1,0:T(8,128)(2,1)S(1)}, bf16[64,1152]{1,0:T(8,128)(2,1)S(1)}, u32[]{:S(2)}, u32[]{:S(2)}) collective-permute-start(bf16[64,1152]{1,0:T(8,128)(2,1)S(1)} %get-tuple-element.43), channel_id=1, source_target_pairs={{0,2},{1,3},{2,0},{3,1},{4,6},{5,7},{6,4},{7,5},{8,10},{9,11},{10,... | collective-permute-start | bytes 442376 | tf_op jit(solution)/shard_map/ppermute | solution.py:433
  43.5 8.7 %collective-permute-start.4 = (bf16[64,1152]{1,0:T(8,128)(2,1)S(1)}, bf16[64,1152]{1,0:T(8,128)(2,1)S(1)}, u32[]{:S(2)}, u32[]{:S(2)}) collective-permute-start(bf16[64,1152]{1,0:T(8,128)(2,1)S(1)} %get-tuple-element.44), channel_id=1, source_target_pairs={{0,3},{1,2},{2,1},{3,0},{4,7},{5,6},{6,5},{7,4},{8,11},{9,10},{10,... | collective-permute-start | bytes 442376 | tf_op jit(solution)/shard_map/ppermute | solution.py:433
  52.3 20.3 %collective-permute-start.6 = (bf16[128,1152]{1,0:T(8,128)(2,1)S(1)}, bf16[128,1152]{1,0:T(8,128)(2,1)S(1)}, u32[]{:S(2)}, u32[]{:S(2)}) collective-permute-start(bf16[128,1152]{1,0:T(8,128)(2,1)S(1)} %get-tuple-element.60), channel_id=1, source_target_pairs={{0,1},{1,0},{2,3},{3,2},{4,5},{5,4},{6,7},{7,6},{8,9},{9,8},{10,11... | collective-permute-start | bytes 884744 | tf_op jit(solution)/shard_map/ppermute | solution.py:433
  53.0 19.6 %collective-permute-start.7 = (bf16[128,1152]{1,0:T(8,128)(2,1)S(1)}, bf16[128,1152]{1,0:T(8,128)(2,1)S(1)}, u32[]{:S(2)}, u32[]{:S(2)}) collective-permute-start(bf16[128,1152]{1,0:T(8,128)(2,1)S(1)} %get-tuple-element.61), channel_id=1, source_target_pairs={{0,2},{1,3},{2,0},{3,1},{4,6},{5,7},{6,4},{7,5},{8,10},{9,11},{10,... | collective-permute-start | bytes 884744 | tf_op jit(solution)/shard_map/ppermute | solution.py:433
  53.0 19.6 %collective-permute-start.8 = (bf16[128,1152]{1,0:T(8,128)(2,1)S(1)}, bf16[128,1152]{1,0:T(8,128)(2,1)S(1)}, u32[]{:S(2)}, u32[]{:S(2)}) collective-permute-start(bf16[128,1152]{1,0:T(8,128)(2,1)S(1)} %get-tuple-element.62), channel_id=1, source_target_pairs={{0,3},{1,2},{2,1},{3,0},{4,7},{5,6},{6,5},{7,4},{8,11},{9,10},{10,... | collective-permute-start | bytes 884744 | tf_op jit(solution)/shard_map/ppermute | solution.py:433

commit v7 on v6

--- a/solution.py
+++ b/solution.py
@@ -262,7 +262,7 @@
 
 def final_kernel(
     place, e0_ref, e1_ref, e2_ref, e3_ref, q0_ref, q1_ref, q2_ref, q3_ref, stats_ref, tables_ref,
-    data_ref, weight_ref, evidence_ref, post_ref, sum_ref, power_ref, *, scale,
+    data_hbm, weight_hbm, evidence_ref, post_ref, sum_ref, power_ref, data_ref, weight_ref, sems, *, scale,
 ):
     dom, orient, y_hi, z_lo, mine = place[0], place[1], place[2], place[3], place[4]
     early = (e0_ref, e1_ref, e2_ref, e3_ref)
@@ -329,6 +329,9 @@
         total = fill(pieces, (doms + k // 2) * pair) + jnp.where(left, totals[k], totals[k + 1])
         sum_ref[:, k * count : (k + 2) * count] = total.astype(BF16)
 
+    weight_ref[...] = lax.dot_general(sum_ref[...], power_ref[...], NN, preferred_element_type=F32) * scale
+    copies = [pltpu.make_async_copy(weight_ref, weight_hbm, sems.at[2])]
+    copies[0].start()
     width = 512
     cos_x, sin_x = phases_x(width)
     cos_rows, sin_rows = phases_y(dom * QUART, QUART // 128)
@@ -362,11 +365,17 @@
             r1 * scale + (r0 + r2) * cos_y + (i2 - i0) * sin_y,
             i1 * scale + (i0 + i2) * cos_y + (r0 - r2) * sin_y,
         )
+        lines = 2 * width // 128
         for tile in range(width // 128):
             for c in range(2):
-                first = 2 * (n * (width // 128) + tile) + c
-                data_ref[pl.ds(first, refs, stride=2 * (QUART // 128)), :] = both[c][:, 128 * tile : 128 * (tile + 1)]
-        weight_ref[:, at] = lax.dot_general(sum_ref[...], power_ref[:, at], NN, preferred_element_type=F32) * scale
+                data_ref[n, pl.ds(2 * tile + c, refs, stride=lines), :] = both[c][:, 128 * tile : 128 * (tile + 1)]
+        copy = pltpu.make_async_copy(
+            data_ref.at[n].reshape(refs, lines, 128), data_hbm.at[:, n * lines : (n + 1) * lines], sems.at[n]
+        )
+        copy.start()
+        copies.append(copy)
+    for copy in copies:
+        copy.wait()
 
 
 def on_device(images, offsets, groups, defocus, refs, log_prior, noise_inv, ctf_table):
@@ -464,21 +473,25 @@
         name="score",
     )(place, own, side, far, corner, turned, power, tables, column)
 
-    early, boxes, stats = lax.optimization_barrier((early, list(boxes), stats))
+    boxes = list(boxes)
+    early, stats = lax.optimization_barrier((early, stats))
     boxes = share(boxes)
     stats_all = lax.all_to_all(stats, AXES, 0, 0, tiled=True)
 
     data, weight, evidence = pl.pallas_call(
         functools.partial(final_kernel, scale=scale),
         in_specs=[smem] + [vmem] * 10,
-        out_specs=[vmem, vmem, smem],
+        out_specs=[hbm, hbm, smem],
         scratch_shapes=[
             pltpu.VMEM((3 * count_refs, 12 * orients), BF16),
             pltpu.VMEM((count_refs, 4 * orients), BF16),
             pltpu.VMEM((4 * orients, QUART), BF16),
+            pltpu.VMEM((2, count_refs * (QUART // 128), 128), F32),
+            pltpu.VMEM((count_refs, QUART), F32),
+            pltpu.SemaphoreType.DMA((3,)),
         ],
         out_shape=[
-            shape((2 * count_refs * (QUART // 128), 128), F32),
+            shape((count_refs, 2 * (QUART // 128), 128), F32),
             shape((count_refs, QUART), F32),
             shape((1,), F32),
         ],

time: 77.2 us -> 77.3 us (level)
  waiting for transfers between devices: 1.83 us -> 0.65 us
  starting transfers between devices: 12.7 us -> 13.8 us
    ppermute x6, waiting for transfers between devices: 1.19 us -> 0.02 us  [share(): lax.ppermute(parts[k], ('yl', 'c'), moves[k])]
    ppermute x6, starting transfers between devices: 7.52 us -> 8.69 us  [share(): lax.ppermute(parts[k], ('yl', 'c'), moves[k])]
  transfers between devices with their start and end apart: 9 -> 9, of which waited for: 2 -> 1; matrix products, arithmetic and copies ran while one was open for 4% -> 4% of each run, Pallas kernels for 9% -> 9%
where the time goes in v7:
time: 77.3 us; the launch traced here: 77 us
  blocking collectives  42.3 us (55%)
  Pallas kernels  13.9 us (18%)
  starting transfers between devices  13.8 us (18%)
  local copies, waits for them, and re-layouts  4.34 us (6%)
  between operations  2.02 us (3%)
    all_to_all x1, blocking collectives, on_device(): own = lax.all_to_all(payload, ('x', 'zh'), 0, 0, tiled=True)  24.4 us
    all_to_all x1, blocking collectives, on_device(): stats_all = lax.all_to_all(stats, AXES, 0, 0, tiled=True)  17.9 us
    ppermute x6, starting transfers between devices, share(): lax.ppermute(parts[k], ('yl', 'c'), moves[k])  8.69 us
    pallas_call x1, Pallas kernels, on_device(): pl.pallas_call(functools.partial(final_kernel, scale=scale), in_specs=[sm...  4.45 us
    unnamed x11, local copies, waits for them, and re-layouts  4.25 us
    pallas_call x1, Pallas kernels, on_device(): pl.pallas_call(score_kernel, in_specs=[smem] + [vmem] * 8, out_specs=[vme...  3.86 us
    ppermute x1, starting transfers between devices, on_device(): far = lax.ppermute(own, ('yh', 'yl'), flip)  2.73 us
    pallas_call x1, Pallas kernels, on_device(): pl.pallas_call(prep_kernel, in_specs=[smem] * 3 + [hbm] * 3, out_specs=vm...  2.52 us
  transfers between devices with their start and end apart: 9, of which 1 were waited for; matrix products, arithmetic and copies ran while one was open for 4% of the time, Pallas kernels for 9%

profile of v7, /device:TPU:1, one launch (start us, length us, event | category | flops | bytes accessed | tf_op | source)
XLA Modules:
  0.0 77.0 jit_solution(18058428068482686267)
XLA Ops:
  1.9 2.5 %prep.1 = bf16[128,1152]{1,0:T(8,128)(2,1)} custom-call(s32[2,9]{1,0:T(2,128)} %bitcast.33, s32[1]{0:T(128)S(6)} %copy.15.groups, s32[1]{0:T(128)S(6)} %copy.16.defocus, bf16[1,2,4096]{2,1,0:T(2,128)(2,1)} %image_hbm.1, f32[8,4096]{1,0:T(8,128)} %noise_ref, f32[64,4096]{1,0:T(8,128)} %ctf_ref), custom_call_target="tpu_custom_call" | custom-call | tf_op jit(solution)/shard_map/prep/pallas_call | solution.py:398
  4.4 24.4 %all_to_all.22 = bf16[16,8,1152]{2,1,0:T(8,128)(2,1)S(1)} all-to-all(bf16[16,8,1152]{2,1,0:T(8,128)(2,1)} %bitcast.32), channel_id=1, replica_groups=mesh['x'=4,'yh'=2,'zh'=4,'zl'=2,'yl'=2,'c'=2] {'x','zh'}, dimensions={0} | all-to-all | bytes 589824 | tf_op jit(solution)/shard_map/all_to_all | solution.py:413
  28.9 2.7 %collective-permute-start.1 = (bf16[128,1152]{1,0:T(8,128)(2,1)S(1)}, bf16[128,1152]{1,0:T(8,128)(2,1)S(1)}, u32[]{:S(2)}, u32[]{:S(2)}) collective-permute-start(bf16[128,1152]{1,0:T(8,128)(2,1)S(1)} %bitcast.24), channel_id=1, source_target_pairs={{0,34},{2,32},{32,2},{34,0},{1,35},{3,33},{33,3},{35,1},{4,38},{6,... | collective-permute-start | bytes 884744 | tf_op jit(solution)/shard_map/ppermute | solution.py:415
  31.6 0.9 %collective-permute-start = (bf16[128,1152]{1,0:T(8,128)(2,1)S(1)}, bf16[128,1152]{1,0:T(8,128)(2,1)S(1)}, u32[]{:S(2)}, u32[]{:S(2)}) collective-permute-start(bf16[128,1152]{1,0:T(8,128)(2,1)S(1)} %bitcast.25), channel_id=1, source_target_pairs={{0,4},{4,0},{1,5},{5,1},{2,6},{6,2},{3,7},{7,3},{8,12},{12,8},{9,1... | collective-permute-start | bytes 884744 | tf_op jit(solution)/shard_map/ppermute | solution.py:414
  32.5 3.0 %copy.14 = bf16[16,8,2,4096]{3,1,2,0:T(8,128)(2,1)S(1)} copy(bf16[16,8,2,4096]{3,2,1,0:T(2,128)(2,1)} %bitcast.31) | data formatting | bytes 4194304
  35.5 0.3 tables.1.tables_ref
  35.9 0.0 copy-start
  35.9 1.3 %copy-done = bf16[224,4096]{1,0:T(8,128)(2,1)} copy-done((bf16[224,4096]{1,0:T(8,128)(2,1)}, bf16[224,4096]{1,0:T(8,128)(2,1)S(1)}, u32[]{:S(2)}) %copy-start) | copy-done | bytes 1835032
  37.1 0.0 collective-permute-done.1.far_ref
  37.1 0.6 collective-permute-done.side_ref
  37.8 1.5 %collective-permute-start.5 = (bf16[128,1152]{1,0:T(8,128)(2,1)S(1)}, bf16[128,1152]{1,0:T(8,128)(2,1)S(1)}, u32[]{:S(2)}, u32[]{:S(2)}) collective-permute-start(bf16[128,1152]{1,0:T(8,128)(2,1)S(1)} %collective-permute-done.side_ref), channel_id=1, source_target_pairs={{0,34},{2,32},{32,2},{34,0},{1,35},{3,33},{33,3},{35,1},{4,38},{6,... | collective-permute-start | bytes 884744 | tf_op jit(solution)/shard_map/ppermute | solution.py:428
  39.3 0.1 stack.23.place
  39.3 0.8 %quarters.1 = (bf16[64,1152]{1,0:T(8,128)(2,1)S(1)}, bf16[64,1152]{1,0:T(8,128)(2,1)S(1)}, bf16[64,1152]{1,0:T(8,128)(2,1)S(1)}, bf16[64,1152]{1,0:T(8,128)(2,1)S(1)}) custom-call(s32[5]{0:T(128)S(1)} %stack.23.place, bf16[128,1152]{1,0:T(8,128)(2,1)S(1)} %bitcast.26, bf16[128,1152]{1,0:T(8,128)(2,1)S(1)} %collective-permute-done.side_ref, ...), custom_call_target="tpu_custom_call" | custom-call | tf_op jit(solution)/shard_map/quarters/pallas_call | solution.py:430
  40.2 3.4 %collective-permute-start.2 = (bf16[64,1152]{1,0:T(8,128)(2,1)S(1)}, bf16[64,1152]{1,0:T(8,128)(2,1)S(1)}, u32[]{:S(2)}, u32[]{:S(2)}) collective-permute-start(bf16[64,1152]{1,0:T(8,128)(2,1)S(1)} %get-tuple-element.38), channel_id=1, source_target_pairs={{0,1},{1,0},{2,3},{3,2},{4,5},{5,4},{6,7},{7,6},{8,9},{9,8},{10,11... | collective-permute-start | bytes 442376 | tf_op jit(solution)/shard_map/ppermute | solution.py:442
  43.5 0.0 collective-permute-start.3
  43.5 1.7 %collective-permute-start.4 = (bf16[64,1152]{1,0:T(8,128)(2,1)S(1)}, bf16[64,1152]{1,0:T(8,128)(2,1)S(1)}, u32[]{:S(2)}, u32[]{:S(2)}) collective-permute-start(bf16[64,1152]{1,0:T(8,128)(2,1)S(1)} %get-tuple-element.40), channel_id=1, source_target_pairs={{0,3},{1,2},{2,1},{3,0},{4,7},{5,6},{6,5},{7,4},{8,11},{9,10},{10,... | collective-permute-start | bytes 442376 | tf_op jit(solution)/shard_map/ppermute | solution.py:442
  45.2 0.0 copy-done.4
  45.2 1.9 %turn_refs.1 = (bf16[2,384,4096]{2,1,0:T(8,128)(2,1)S(1)}, bf16[128,4096]{1,0:T(8,128)(2,1)S(1)}, f32[128,128]{1,0:T(8,128)S(1)}) custom-call(bf16[128,8192]{1,0:T(8,128)(2,1)S(1)} %bitcast.23, f32[1,128]{1,0:T(1,128)S(1)} %bitcast.30), custom_call_target="tpu_custom_call" | custom-call | flops 4194304 | bytes 10485760 | tf_op jit(solution)/shard_map/turn_refs/pallas_call | solution.py:446
  47.2 0.0 collective-permute-done.5.corner_ref
  47.2 0.0 copy-done.1
  47.2 3.9 %score.1 = (bf16[128,1152]{1,0:T(8,128)(2,1)S(1)}, bf16[128,1152]{1,0:T(8,128)(2,1)S(1)}, bf16[128,1152]{1,0:T(8,128)(2,1)S(1)}, bf16[128,1152]{1,0:T(8,128)(2,1)S(1)}, f32[256,128]{1,0:T(8,128)S(1)}) custom-call(s32[5]{0:T(128)S(1)} %stack.23.place, bf16[128,1152]{1,0:T(8,128)(2,1)S(1)} %bitcast.27, bf16[128,1152]{1,0:T(8,128)(2,1)S(1)} %collective-permute-done.side_ref, ...), custom_call_target="tpu_custom_call" | custom-call | flops 1207959552 | bytes 10485760 | tf_op jit(solution)/shard_map/score/pallas_call | solution.py:463
  51.1 1.9 %collective-permute-start.6 = (bf16[128,1152]{1,0:T(8,128)(2,1)S(1)}, bf16[128,1152]{1,0:T(8,128)(2,1)S(1)}, u32[]{:S(2)}, u32[]{:S(2)}) collective-permute-start(bf16[128,1152]{1,0:T(8,128)(2,1)S(1)} %get-tuple-element.52), channel_id=1, source_target_pairs={{0,1},{1,0},{2,3},{3,2},{4,5},{5,4},{6,7},{7,6},{8,9},{9,8},{10,11... | collective-permute-start | bytes 884744 | tf_op jit(solution)/shard_map/ppermute | solution.py:442
  52.9 0.0 collective-permute-start.7
  52.9 0.0 collective-permute-done.2.e1_ref
  52.9 1.7 %collective-permute-start.8 = (bf16[128,1152]{1,0:T(8,128)(2,1)S(1)}, bf16[128,1152]{1,0:T(8,128)(2,1)S(1)}, u32[]{:S(2)}, u32[]{:S(2)}) collective-permute-start(bf16[128,1152]{1,0:T(8,128)(2,1)S(1)} %get-tuple-element.54), channel_id=1, source_target_pairs={{0,3},{1,2},{2,1},{3,0},{4,7},{5,6},{6,5},{7,4},{8,11},{9,10},{10,... | collective-permute-start | bytes 884744 | tf_op jit(solution)/shard_map/ppermute | solution.py:442
  54.7 0.0 collective-permute-done.3.e2_ref
  54.7 0.0 collective-permute-done.4.e3_ref
  54.7 17.9 %all_to_all.23 = f32[256,1,128]{2,1,0:T(1,128)S(1)} all-to-all(f32[256,1,128]{2,1,0:T(1,128)S(1)} %bitcast.29), channel_id=1, replica_groups=mesh['x'=4,'yh'=2,'zh'=4,'zl'=2,'yl'=2,'c'=2] {'x','yh','zh','zl','yl','c'}, dimensions={0} | all-to-all | bytes 262144 | tf_op jit(solution)/shard_map/all_to_all | solution.py:479
  72.6 0.0 collective-permute-done.6.q1_ref
  72.6 0.0 collective-permute-done.7.q2_ref
  72.6 0.0 collective-permute-done.8.q3_ref
  72.6 4.5 %insert.1 = (f32[128,16,128]{2,1,0:T(8,128)}, f32[128,1024]{1,0:T(8,128)}, f32[1]{0:T(128)}) custom-call(s32[5]{0:T(128)S(1)} %stack.23.place, bf16[64,1152]{1,0:T(8,128)(2,1)S(1)} %get-tuple-element.47.e0_ref, bf16[64,1152]{1,0:T(8,128)(2,1)S(1)} %collective-permute-done.2.e1_ref, bf16[64,1152]{1,0:T(8,128)(2,1)S(1)} %collective-permute-done.3.e2_ref, ...), custom_call_target="tpu_custom_call" | custom-call | tf_op jit(solution)/shard_map/insert/pallas_call | solution.py:481
  (6 shorter events, 0.0 us)
Async XLA Ops:
  28.9 8.2 %collective-permute-start.1 = (bf16[128,1152]{1,0:T(8,128)(2,1)S(1)}, bf16[128,1152]{1,0:T(8,128)(2,1)S(1)}, u32[]{:S(2)}, u32[]{:S(2)}) collective-permute-start(bf16[128,1152]{1,0:T(8,128)(2,1)S(1)} %bitcast.24), channel_id=1, source_target_pairs={{0,34},{2,32},{32,2},{34,0},{1,35},{3,33},{33,3},{35,1},{4,38},{6,... | collective-permute-start | bytes 884744 | tf_op jit(solution)/shard_map/ppermute | solution.py:415
  31.6 6.1 %collective-permute-start = (bf16[128,1152]{1,0:T(8,128)(2,1)S(1)}, bf16[128,1152]{1,0:T(8,128)(2,1)S(1)}, u32[]{:S(2)}, u32[]{:S(2)}) collective-permute-start(bf16[128,1152]{1,0:T(8,128)(2,1)S(1)} %bitcast.25), channel_id=1, source_target_pairs={{0,4},{4,0},{1,5},{5,1},{2,6},{6,2},{3,7},{7,3},{8,12},{12,8},{9,1... | collective-permute-start | bytes 884744 | tf_op jit(solution)/shard_map/ppermute | solution.py:414
  32.5 3.0 %copy-start.2 = (f32[64,4096]{1,0:T(8,128)S(1)}, f32[64,4096]{1,0:T(8,128)}, u32[]{:S(2)}) copy-start(f32[64,4096]{1,0:T(8,128)} %ctf_ref) | copy-start | bytes 3145732
  32.5 3.0 %copy-start.3 = (f32[8,4096]{1,0:T(8,128)S(1)}, f32[8,4096]{1,0:T(8,128)}, u32[]{:S(2)}) copy-start(f32[8,4096]{1,0:T(8,128)} %noise_ref) | copy-start | bytes 393220
  35.9 1.3 %copy-start = (bf16[224,4096]{1,0:T(8,128)(2,1)}, bf16[224,4096]{1,0:T(8,128)(2,1)S(1)}, u32[]{:S(2)}) copy-start(bf16[224,4096]{1,0:T(8,128)(2,1)S(1)} %tables.1.tables_ref) | copy-start | bytes 5505028
  37.1 8.1 %copy-start.4 = (f32[128]{0:T(128)S(1)}, f32[128]{0:T(128)}, u32[]{:S(2)}) copy-start(f32[128]{0:T(128)} %param.13) | copy-start | bytes 1540
  37.8 9.4 %collective-permute-start.5 = (bf16[128,1152]{1,0:T(8,128)(2,1)S(1)}, bf16[128,1152]{1,0:T(8,128)(2,1)S(1)}, u32[]{:S(2)}, u32[]{:S(2)}) collective-permute-start(bf16[128,1152]{1,0:T(8,128)(2,1)S(1)} %collective-permute-done.side_ref), channel_id=1, source_target_pairs={{0,34},{2,32},{32,2},{34,0},{1,35},{3,33},{33,3},{35,1},{4,38},{6,... | collective-permute-start | bytes 884744 | tf_op jit(solution)/shard_map/ppermute | solution.py:428
  39.3 7.9 %copy-start.1 = (bf16[224,4096]{1,0:T(8,128)(2,1)S(1)}, bf16[224,4096]{1,0:T(8,128)(2,1)}, u32[]{:S(2)}) copy-start(bf16[224,4096]{1,0:T(8,128)(2,1)} %copy-done) | copy-start | bytes 5505028
  40.2 12.8 %collective-permute-start.2 = (bf16[64,1152]{1,0:T(8,128)(2,1)S(1)}, bf16[64,1152]{1,0:T(8,128)(2,1)S(1)}, u32[]{:S(2)}, u32[]{:S(2)}) collective-permute-start(bf16[64,1152]{1,0:T(8,128)(2,1)S(1)} %get-tuple-element.38), channel_id=1, source_target_pairs={{0,1},{1,0},{2,3},{3,2},{4,5},{5,4},{6,7},{7,6},{8,9},{9,8},{10,11... | collective-permute-start | bytes 442376 | tf_op jit(solution)/shard_map/ppermute | solution.py:442
  43.5 11.2 %collective-permute-start.3 = (bf16[64,1152]{1,0:T(8,128)(2,1)S(1)}, bf16[64,1152]{1,0:T(8,128)(2,1)S(1)}, u32[]{:S(2)}, u32[]{:S(2)}) collective-permute-start(bf16[64,1152]{1,0:T(8,128)(2,1)S(1)} %get-tuple-element.39), channel_id=1, source_target_pairs={{0,2},{1,3},{2,0},{3,1},{4,6},{5,7},{6,4},{7,5},{8,10},{9,11},{10,... | collective-permute-start | bytes 442376 | tf_op jit(solution)/shard_map/ppermute | solution.py:442
  43.5 11.2 %collective-permute-start.4 = (bf16[64,1152]{1,0:T(8,128)(2,1)S(1)}, bf16[64,1152]{1,0:T(8,128)(2,1)S(1)}, u32[]{:S(2)}, u32[]{:S(2)}) collective-permute-start(bf16[64,1152]{1,0:T(8,128)(2,1)S(1)} %get-tuple-element.40), channel_id=1, source_target_pairs={{0,3},{1,2},{2,1},{3,0},{4,7},{5,6},{6,5},{7,4},{8,11},{9,10},{10,... | collective-permute-start | bytes 442376 | tf_op jit(solution)/shard_map/ppermute | solution.py:442
  51.1 21.5 %collective-permute-start.6 = (bf16[128,1152]{1,0:T(8,128)(2,1)S(1)}, bf16[128,1152]{1,0:T(8,128)(2,1)S(1)}, u32[]{:S(2)}, u32[]{:S(2)}) collective-permute-start(bf16[128,1152]{1,0:T(8,128)(2,1)S(1)} %get-tuple-element.52), channel_id=1, source_target_pairs={{0,1},{1,0},{2,3},{3,2},{4,5},{5,4},{6,7},{7,6},{8,9},{9,8},{10,11... | collective-permute-start | bytes 884744 | tf_op jit(solution)/shard_map/ppermute | solution.py:442
  52.9 19.6 %collective-permute-start.7 = (bf16[128,1152]{1,0:T(8,128)(2,1)S(1)}, bf16[128,1152]{1,0:T(8,128)(2,1)S(1)}, u32[]{:S(2)}, u32[]{:S(2)}) collective-permute-start(bf16[128,1152]{1,0:T(8,128)(2,1)S(1)} %get-tuple-element.53), channel_id=1, source_target_pairs={{0,2},{1,3},{2,0},{3,1},{4,6},{5,7},{6,4},{7,5},{8,10},{9,11},{10,... | collective-permute-start | bytes 884744 | tf_op jit(solution)/shard_map/ppermute | solution.py:442
  52.9 19.6 %collective-permute-start.8 = (bf16[128,1152]{1,0:T(8,128)(2,1)S(1)}, bf16[128,1152]{1,0:T(8,128)(2,1)S(1)}, u32[]{:S(2)}, u32[]{:S(2)}) collective-permute-start(bf16[128,1152]{1,0:T(8,128)(2,1)S(1)} %get-tuple-element.54), channel_id=1, source_target_pairs={{0,3},{1,2},{2,1},{3,0},{4,7},{5,6},{6,5},{7,4},{8,11},{9,10},{10,... | collective-permute-start | bytes 884744 | tf_op jit(solution)/shard_map/ppermute | solution.py:442

commit v8 on v7

--- a/solution.py
+++ b/solution.py
@@ -178,13 +178,13 @@
     return jnp.where(flag == 1, other, row)
 
 
-def quarter_kernel(place, own_ref, side_ref, flat_ref, q0_ref, q1_ref, q2_ref, q3_ref, wide_ref):
-    outs = (q0_ref, q1_ref, q2_ref, q3_ref)
+def quarter_kernel(place, own_ref, side_ref, flat_ref, q0_ref, q2_ref, q3_ref, wide_ref):
+    outs = {0: q0_ref, 2: q2_ref, 3: q3_ref}
     count = 2 * own_ref.shape[0] // 8
     chunk, codes = unpack((own_ref, side_ref), wide_ref)
     meta = codes(0, count)
     both = jnp.concatenate([meta, meta], axis=0).astype(BF16)
-    for k in range(4):
+    for k in outs:
         part = place[0] ^ k
         outs[k][:, 0:QUART] = jnp.concatenate([chunk(part, 0, count), chunk(part + 4, 0, count)], axis=0).astype(BF16)
         outs[k][:, QUART:WIDE] = both
@@ -219,6 +219,13 @@
             outs[j][side * count : (side + 1) * count, 5 * refs : 5 * refs + QUART // 2] = late[
                 :, side * QUART // 2 : (side + 1) * QUART // 2
             ]
+    part = place[0] ^ 1
+    soon = jnp.concatenate([chunk(part, 0, half), chunk(part + 4, 0, half)], axis=0).astype(BF16)
+    base = 5 * refs + QUART // 2
+    for side in range(2):
+        rows = slice(side * count, (side + 1) * count)
+        q1_ref[rows, base : base + QUART // 2] = soon[:, side * QUART // 2 : (side + 1) * QUART // 2]
+        q1_ref[rows, base + QUART // 2 : base + QUART // 2 + META] = meta.astype(BF16)
 
     base = column_ref[:, 0:count] - 0.5 * self_term
     base_pair = jnp.concatenate([base, base], axis=1)
@@ -261,16 +268,17 @@
 
 
 def final_kernel(
-    place, e0_ref, e1_ref, e2_ref, e3_ref, q0_ref, q1_ref, q2_ref, q3_ref, stats_ref, tables_ref,
+    place, e0_ref, e2_ref, e3_ref, q0_ref, q1_ref, q2_ref, q3_ref, stats_ref, tables_ref,
     data_hbm, weight_hbm, evidence_ref, post_ref, sum_ref, power_ref, data_ref, weight_ref, sems, *, scale,
 ):
     dom, orient, y_hi, z_lo, mine = place[0], place[1], place[2], place[3], place[4]
-    early = (e0_ref, e1_ref, e2_ref, e3_ref)
+    early = {0: e0_ref, 2: e2_ref, 3: e3_ref}
     boxes = (q0_ref, q1_ref, q2_ref, q3_ref)
     doms = 4
     count = q0_ref.shape[0] // 2
     half = count // 2
     refs = sum_ref.shape[0]
+    tail = 5 * refs + QUART // 2
     pair = 2 * count
     orients = stats_ref.shape[0] // doms
     lane = lax.broadcasted_iota(jnp.int32, (1, pair), 1)
@@ -293,7 +301,10 @@
         if k == 0:
             evidence_ref[0] = jnp.sum(jnp.where(lane == mine, evidence, 0.0))
         notes = boxes[k][0:half, 4 * refs : 5 * refs].astype(F32)
-        first = early[k][0:half, QUART:WIDE].astype(F32)
+        if k in early:
+            first = early[k][0:half, QUART:WIDE].astype(F32)
+        else:
+            first = boxes[k][0:half, tail + QUART // 2 : tail + QUART // 2 + META].astype(F32)
         spot = count if k % 2 == 0 else 0
         groups += [first[:, 0:1], notes[:, spot : spot + 1]]
         foci += [first[:, 1:2], notes[:, spot + 1 : spot + 2]]
@@ -343,7 +354,11 @@
         late_at = slice(5 * refs + n * width - side * QUART // 2, 5 * refs + (n + 1) * width - side * QUART // 2)
         for k in range(doms):
             late = boxes[k][side * count : (side + 1) * count, late_at].astype(F32)
-            soon = early[k][:, at].astype(F32)
+            if k in early:
+                soon = early[k][:, at].astype(F32)
+            else:
+                start = tail + n * width - side * QUART // 2
+                soon = boxes[k][side * count : (side + 1) * count, start : start + width].astype(F32)
             real = jnp.concatenate([soon[0:half], late[0:half]], axis=0)
             imag = jnp.concatenate([soon[half:], late[half:]], axis=0)
             new_real, new_imag = shift_x(real, imag, cos_x, sin_x)
@@ -430,8 +445,8 @@
     early = pl.pallas_call(
         quarter_kernel,
         in_specs=[smem] + [vmem] * 3,
-        out_specs=[vmem] * 4,
-        out_shape=[shape((orients, WIDE), BF16)] * 4,
+        out_specs=[vmem] * 3,
+        out_shape=[shape((orients, WIDE), BF16)] * 3,
         scratch_shapes=[pltpu.VMEM((4 * orients * (WIDE // 128), 128), F32)],
         compiler_params=params(VMEM_LIMIT // 3),
         name="quarters",
@@ -439,9 +454,9 @@
 
     def share(parts):
         moves = [[(d, d ^ k) for d in range(4)] for k in range(4)]
-        return parts[0:1] + [lax.ppermute(parts[k], ("yl", "c"), moves[k]) for k in range(1, 4)]
-
-    early = list(early)
+        return {k: lax.ppermute(part, ("yl", "c"), moves[k]) if k else part for k, part in parts.items()}
+
+    early = dict(zip((0, 2, 3), early))
     flat, early[0] = lax.optimization_barrier((flat, early[0]))
     turned, power, column = pl.pallas_call(
         refs_kernel,
@@ -464,7 +479,8 @@
         score_kernel,
         in_specs=[smem] + [vmem] * 8,
         out_specs=[vmem] * 5,
-        out_shape=[shape(box, BF16)] * 4 + [shape((devices, 2 * orients), F32)],
+        out_shape=[shape((box[0], box[1] + (k == 1) * (QUART // 2 + META)), BF16) for k in range(4)]
+        + [shape((devices, 2 * orients), F32)],
         scratch_shapes=[pltpu.VMEM((8 * orients * (WIDE // 128), 128), F32)],
         compiler_params=params(),
         cost_estimate=pl.CostEstimate(
@@ -473,14 +489,14 @@
         name="score",
     )(place, own, side, far, corner, turned, power, tables, column)
 
-    boxes = list(boxes)
-    early, stats = lax.optimization_barrier((early, stats))
+    boxes = dict(enumerate(boxes))
+    early, boxes, stats = lax.optimization_barrier((early, boxes, stats))
     boxes = share(boxes)
     stats_all = lax.all_to_all(stats, AXES, 0, 0, tiled=True)
 
     data, weight, evidence = pl.pallas_call(
         functools.partial(final_kernel, scale=scale),
-        in_specs=[smem] + [vmem] * 10,
+        in_specs=[smem] + [vmem] * 9,
         out_specs=[hbm, hbm, smem],
         scratch_shapes=[
             pltpu.VMEM((3 * count_refs, 12 * orients), BF16),
@@ -497,7 +513,7 @@
         ],
         compiler_params=params(),
         name="insert",
-    )(place, *early, *boxes, stats_all, tables)
+    )(place, *(early[k] for k in (0, 2, 3)), *(boxes[k] for k in range(4)), stats_all, tables)
     data = jnp.transpose(data.reshape(count_refs, QUART // 128, 2, 128), (0, 2, 1, 3))
     return data.reshape(count_refs, 2, QUART), weight, evidence
 

time: 77.3 us -> 77.3 us (level)
    ppermute x6 -> x5, starting transfers between devices: 8.69 us -> 8.72 us  [share(): lax.ppermute(part, ('yl', 'c'), moves[k])]
  transfers between devices with their start and end apart: 9 -> 8, of which waited for: 1 -> 1; matrix products, arithmetic and copies ran while one was open for 4% -> 4% of each run, Pallas kernels for 9% -> 9%
where the time goes in v8:
time: 77.3 us; the launch traced here: 77.1 us
  blocking collectives  42.3 us (55%)
  Pallas kernels  13.9 us (18%)
  starting transfers between devices  13.9 us (18%)
  local copies, waits for them, and re-layouts  4.34 us (6%)
  between operations  2.04 us (3%)
    all_to_all x1, blocking collectives, on_device(): own = lax.all_to_all(payload, ('x', 'zh'), 0, 0, tiled=True)  24.4 us
    all_to_all x1, blocking collectives, on_device(): stats_all = lax.all_to_all(stats, AXES, 0, 0, tiled=True)  17.9 us
    ppermute x5, starting transfers between devices, share(): lax.ppermute(part, ('yl', 'c'), moves[k])  8.72 us
    pallas_call x1, Pallas kernels, on_device(): pl.pallas_call(functools.partial(final_kernel, scale=scale), in_specs=[sm...  4.46 us
    unnamed x11, local copies, waits for them, and re-layouts  4.26 us
    pallas_call x1, Pallas kernels, on_device(): pl.pallas_call(score_kernel, in_specs=[smem] + [vmem] * 8, out_specs=[vme...  3.9 us
    ppermute x1, starting transfers between devices, on_device(): far = lax.ppermute(own, ('yh', 'yl'), flip)  2.73 us
    pallas_call x1, Pallas kernels, on_device(): pl.pallas_call(prep_kernel, in_specs=[smem] * 3 + [hbm] * 3, out_specs=vm...  2.52 us
  transfers between devices with their start and end apart: 8, of which 1 were waited for; matrix products, arithmetic and copies ran while one was open for 4% of the time, Pallas kernels for 9%

profile of v8, /device:TPU:1, one launch (start us, length us, event | category | flops | bytes accessed | tf_op | source)
XLA Modules:
  0.0 77.1 jit_solution(13657431751699130760)
XLA Ops:
  1.9 2.5 %prep.1 = bf16[128,1152]{1,0:T(8,128)(2,1)} custom-call(s32[2,9]{1,0:T(2,128)} %bitcast.33, s32[1]{0:T(128)S(6)} %copy.15.groups, s32[1]{0:T(128)S(6)} %copy.16.defocus, bf16[1,2,4096]{2,1,0:T(2,128)(2,1)} %image_hbm.1, f32[8,4096]{1,0:T(8,128)} %noise_ref, f32[64,4096]{1,0:T(8,128)} %ctf_ref), custom_call_target="tpu_custom_call" | custom-call | tf_op jit(solution)/shard_map/prep/pallas_call | solution.py:413
  4.4 24.4 %all_to_all.22 = bf16[16,8,1152]{2,1,0:T(8,128)(2,1)S(1)} all-to-all(bf16[16,8,1152]{2,1,0:T(8,128)(2,1)} %bitcast.32), channel_id=1, replica_groups=mesh['x'=4,'yh'=2,'zh'=4,'zl'=2,'yl'=2,'c'=2] {'x','zh'}, dimensions={0} | all-to-all | bytes 589824 | tf_op jit(solution)/shard_map/all_to_all | solution.py:428
  28.9 2.7 %collective-permute-start.1 = (bf16[128,1152]{1,0:T(8,128)(2,1)S(1)}, bf16[128,1152]{1,0:T(8,128)(2,1)S(1)}, u32[]{:S(2)}, u32[]{:S(2)}) collective-permute-start(bf16[128,1152]{1,0:T(8,128)(2,1)S(1)} %bitcast.24), channel_id=1, source_target_pairs={{0,34},{2,32},{32,2},{34,0},{1,35},{3,33},{33,3},{35,1},{4,38},{6,... | collective-permute-start | bytes 884744 | tf_op jit(solution)/shard_map/ppermute | solution.py:430
  31.6 0.9 %collective-permute-start = (bf16[128,1152]{1,0:T(8,128)(2,1)S(1)}, bf16[128,1152]{1,0:T(8,128)(2,1)S(1)}, u32[]{:S(2)}, u32[]{:S(2)}) collective-permute-start(bf16[128,1152]{1,0:T(8,128)(2,1)S(1)} %bitcast.25), channel_id=1, source_target_pairs={{0,4},{4,0},{1,5},{5,1},{2,6},{6,2},{3,7},{7,3},{8,12},{12,8},{9,1... | collective-permute-start | bytes 884744 | tf_op jit(solution)/shard_map/ppermute | solution.py:429
  32.5 3.0 %copy.14 = bf16[16,8,2,4096]{3,1,2,0:T(8,128)(2,1)S(1)} copy(bf16[16,8,2,4096]{3,2,1,0:T(2,128)(2,1)} %bitcast.31) | data formatting | bytes 4194304
  35.5 0.0 copy-done.2
  35.5 0.0 copy-done.3
  35.5 0.3 tables.1.tables_ref
  35.9 0.0 copy-start
  35.9 1.3 %copy-done = bf16[224,4096]{1,0:T(8,128)(2,1)} copy-done((bf16[224,4096]{1,0:T(8,128)(2,1)}, bf16[224,4096]{1,0:T(8,128)(2,1)S(1)}, u32[]{:S(2)}) %copy-start) | copy-done | bytes 1835032
  37.1 0.0 collective-permute-done.1.far_ref
  37.1 0.6 collective-permute-done.side_ref
  37.8 1.5 %collective-permute-start.4 = (bf16[128,1152]{1,0:T(8,128)(2,1)S(1)}, bf16[128,1152]{1,0:T(8,128)(2,1)S(1)}, u32[]{:S(2)}, u32[]{:S(2)}) collective-permute-start(bf16[128,1152]{1,0:T(8,128)(2,1)S(1)} %collective-permute-done.side_ref), channel_id=1, source_target_pairs={{0,34},{2,32},{32,2},{34,0},{1,35},{3,33},{33,3},{35,1},{4,38},{6,... | collective-permute-start | bytes 884744 | tf_op jit(solution)/shard_map/ppermute | solution.py:443
  39.3 0.1 stack.23.place
  39.3 0.8 quarters.1
  40.1 0.1 collective-permute-start.2
  40.2 4.9 %collective-permute-start.3 = (bf16[64,1152]{1,0:T(8,128)(2,1)S(1)}, bf16[64,1152]{1,0:T(8,128)(2,1)S(1)}, u32[]{:S(2)}, u32[]{:S(2)}) collective-permute-start(bf16[64,1152]{1,0:T(8,128)(2,1)S(1)} %get-tuple-element.41), channel_id=1, source_target_pairs={{0,3},{1,2},{2,1},{3,0},{4,7},{5,6},{6,5},{7,4},{8,11},{9,10},{10,... | collective-permute-start | bytes 442376 | tf_op jit(solution)/shard_map/ppermute | solution.py:457
  45.1 0.0 copy-done.4
  45.1 1.9 %turn_refs.1 = (bf16[2,384,4096]{2,1,0:T(8,128)(2,1)S(1)}, bf16[128,4096]{1,0:T(8,128)(2,1)S(1)}, f32[128,128]{1,0:T(8,128)S(1)}) custom-call(bf16[128,8192]{1,0:T(8,128)(2,1)S(1)} %bitcast.23, f32[1,128]{1,0:T(1,128)S(1)} %bitcast.30), custom_call_target="tpu_custom_call" | custom-call | flops 4194304 | bytes 10485760 | tf_op jit(solution)/shard_map/turn_refs/pallas_call | solution.py:461
  47.0 0.0 collective-permute-done.4.corner_ref
  47.0 0.0 copy-done.1
  47.1 3.9 %score.1 = (bf16[128,1152]{1,0:T(8,128)(2,1)S(1)}, bf16[128,1792]{1,0:T(8,128)(2,1)S(1)}, bf16[128,1152]{1,0:T(8,128)(2,1)S(1)}, bf16[128,1152]{1,0:T(8,128)(2,1)S(1)}, f32[256,128]{1,0:T(8,128)S(1)}) custom-call(s32[5]{0:T(128)S(1)} %stack.23.place, bf16[128,1152]{1,0:T(8,128)(2,1)S(1)} %bitcast.27, bf16[128,1152]{1,0:T(8,128)(2,1)S(1)} %collective-permute-done.side_ref, ...), custom_call_target="tpu_custom_call" | custom-call | flops 1207959552 | bytes 10485760 | tf_op jit(solution)/shard_map/score/pallas_call | solution.py:478
  51.0 0.0 collective-permute-done.2.e2_ref
  51.0 0.0 collective-permute-done.3.e3_ref
  51.0 2.0 %collective-permute-start.5 = (bf16[128,1792]{1,0:T(8,128)(2,1)S(1)}, bf16[128,1792]{1,0:T(8,128)(2,1)S(1)}, u32[]{:S(2)}, u32[]{:S(2)}) collective-permute-start(bf16[128,1792]{1,0:T(8,128)(2,1)S(1)} %get-tuple-element.56), channel_id=1, source_target_pairs={{0,1},{1,0},{2,3},{3,2},{4,5},{5,4},{6,7},{7,6},{8,9},{9,8},{10,11... | collective-permute-start | bytes 1376264 | tf_op jit(solution)/shard_map/ppermute | solution.py:457
  53.0 0.0 collective-permute-start.6
  53.0 1.7 %collective-permute-start.7 = (bf16[128,1152]{1,0:T(8,128)(2,1)S(1)}, bf16[128,1152]{1,0:T(8,128)(2,1)S(1)}, u32[]{:S(2)}, u32[]{:S(2)}) collective-permute-start(bf16[128,1152]{1,0:T(8,128)(2,1)S(1)} %get-tuple-element.58), channel_id=1, source_target_pairs={{0,3},{1,2},{2,1},{3,0},{4,7},{5,6},{6,5},{7,4},{8,11},{9,10},{10,... | collective-permute-start | bytes 884744 | tf_op jit(solution)/shard_map/ppermute | solution.py:457
  54.7 17.9 %all_to_all.23 = f32[256,1,128]{2,1,0:T(1,128)S(1)} all-to-all(f32[256,1,128]{2,1,0:T(1,128)S(1)} %bitcast.29), channel_id=1, replica_groups=mesh['x'=4,'yh'=2,'zh'=4,'zl'=2,'yl'=2,'c'=2] {'x','yh','zh','zl','yl','c'}, dimensions={0} | all-to-all | bytes 262144 | tf_op jit(solution)/shard_map/all_to_all | solution.py:495
  72.6 0.0 collective-permute-done.6.q2_ref
  72.6 0.0 collective-permute-done.7.q3_ref
  72.6 0.0 collective-permute-done.5.q1_ref
  72.6 4.5 %insert.1 = (f32[128,16,128]{2,1,0:T(8,128)}, f32[128,1024]{1,0:T(8,128)}, f32[1]{0:T(128)}) custom-call(s32[5]{0:T(128)S(1)} %stack.23.place, bf16[64,1152]{1,0:T(8,128)(2,1)S(1)} %get-tuple-element.52.e0_ref, bf16[64,1152]{1,0:T(8,128)(2,1)S(1)} %collective-permute-done.2.e2_ref, bf16[64,1152]{1,0:T(8,128)(2,1)S(1)} %collective-permute-done.3.e3_ref, ...), custom_call_target="tpu_custom_call" | custom-call | tf_op jit(solution)/shard_map/insert/pallas_call | solution.py:497
  (4 shorter events, 0.0 us)
Async XLA Ops:
  28.9 8.3 %collective-permute-start.1 = (bf16[128,1152]{1,0:T(8,128)(2,1)S(1)}, bf16[128,1152]{1,0:T(8,128)(2,1)S(1)}, u32[]{:S(2)}, u32[]{:S(2)}) collective-permute-start(bf16[128,1152]{1,0:T(8,128)(2,1)S(1)} %bitcast.24), channel_id=1, source_target_pairs={{0,34},{2,32},{32,2},{34,0},{1,35},{3,33},{33,3},{35,1},{4,38},{6,... | collective-permute-start | bytes 884744 | tf_op jit(solution)/shard_map/ppermute | solution.py:430
  31.6 6.1 %collective-permute-start = (bf16[128,1152]{1,0:T(8,128)(2,1)S(1)}, bf16[128,1152]{1,0:T(8,128)(2,1)S(1)}, u32[]{:S(2)}, u32[]{:S(2)}) collective-permute-start(bf16[128,1152]{1,0:T(8,128)(2,1)S(1)} %bitcast.25), channel_id=1, source_target_pairs={{0,4},{4,0},{1,5},{5,1},{2,6},{6,2},{3,7},{7,3},{8,12},{12,8},{9,1... | collective-permute-start | bytes 884744 | tf_op jit(solution)/shard_map/ppermute | solution.py:429
  32.5 3.0 %copy-start.2 = (f32[64,4096]{1,0:T(8,128)S(1)}, f32[64,4096]{1,0:T(8,128)}, u32[]{:S(2)}) copy-start(f32[64,4096]{1,0:T(8,128)} %ctf_ref) | copy-start | bytes 3145732
  32.5 3.0 %copy-start.3 = (f32[8,4096]{1,0:T(8,128)S(1)}, f32[8,4096]{1,0:T(8,128)}, u32[]{:S(2)}) copy-start(f32[8,4096]{1,0:T(8,128)} %noise_ref) | copy-start | bytes 393220
  35.9 1.3 %copy-start = (bf16[224,4096]{1,0:T(8,128)(2,1)}, bf16[224,4096]{1,0:T(8,128)(2,1)S(1)}, u32[]{:S(2)}) copy-start(bf16[224,4096]{1,0:T(8,128)(2,1)S(1)} %tables.1.tables_ref) | copy-start | bytes 5505028
  37.1 8.0 %copy-start.4 = (f32[128]{0:T(128)S(1)}, f32[128]{0:T(128)}, u32[]{:S(2)}) copy-start(f32[128]{0:T(128)} %param.13) | copy-start | bytes 1540
  37.8 9.3 %collective-permute-start.4 = (bf16[128,1152]{1,0:T(8,128)(2,1)S(1)}, bf16[128,1152]{1,0:T(8,128)(2,1)S(1)}, u32[]{:S(2)}, u32[]{:S(2)}) collective-permute-start(bf16[128,1152]{1,0:T(8,128)(2,1)S(1)} %collective-permute-done.side_ref), channel_id=1, source_target_pairs={{0,34},{2,32},{32,2},{34,0},{1,35},{3,33},{33,3},{35,1},{4,38},{6,... | collective-permute-start | bytes 884744 | tf_op jit(solution)/shard_map/ppermute | solution.py:443
  39.3 7.7 %copy-start.1 = (bf16[224,4096]{1,0:T(8,128)(2,1)S(1)}, bf16[224,4096]{1,0:T(8,128)(2,1)}, u32[]{:S(2)}) copy-start(bf16[224,4096]{1,0:T(8,128)(2,1)} %copy-done) | copy-start | bytes 5505028
  40.1 10.9 %collective-permute-start.2 = (bf16[64,1152]{1,0:T(8,128)(2,1)S(1)}, bf16[64,1152]{1,0:T(8,128)(2,1)S(1)}, u32[]{:S(2)}, u32[]{:S(2)}) collective-permute-start(bf16[64,1152]{1,0:T(8,128)(2,1)S(1)} %get-tuple-element.40), channel_id=1, source_target_pairs={{0,2},{1,3},{2,0},{3,1},{4,6},{5,7},{6,4},{7,5},{8,10},{9,11},{10,... | collective-permute-start | bytes 442376 | tf_op jit(solution)/shard_map/ppermute | solution.py:457
  40.2 10.8 %collective-permute-start.3 = (bf16[64,1152]{1,0:T(8,128)(2,1)S(1)}, bf16[64,1152]{1,0:T(8,128)(2,1)S(1)}, u32[]{:S(2)}, u32[]{:S(2)}) collective-permute-start(bf16[64,1152]{1,0:T(8,128)(2,1)S(1)} %get-tuple-element.41), channel_id=1, source_target_pairs={{0,3},{1,2},{2,1},{3,0},{4,7},{5,6},{6,5},{7,4},{8,11},{9,10},{10,... | collective-permute-start | bytes 442376 | tf_op jit(solution)/shard_map/ppermute | solution.py:457
  51.0 21.6 %collective-permute-start.5 = (bf16[128,1792]{1,0:T(8,128)(2,1)S(1)}, bf16[128,1792]{1,0:T(8,128)(2,1)S(1)}, u32[]{:S(2)}, u32[]{:S(2)}) collective-permute-start(bf16[128,1792]{1,0:T(8,128)(2,1)S(1)} %get-tuple-element.56), channel_id=1, source_target_pairs={{0,1},{1,0},{2,3},{3,2},{4,5},{5,4},{6,7},{7,6},{8,9},{9,8},{10,11... | collective-permute-start | bytes 1376264 | tf_op jit(solution)/shard_map/ppermute | solution.py:457
  53.0 19.6 %collective-permute-start.6 = (bf16[128,1152]{1,0:T(8,128)(2,1)S(1)}, bf16[128,1152]{1,0:T(8,128)(2,1)S(1)}, u32[]{:S(2)}, u32[]{:S(2)}) collective-permute-start(bf16[128,1152]{1,0:T(8,128)(2,1)S(1)} %get-tuple-element.57), channel_id=1, source_target_pairs={{0,2},{1,3},{2,0},{3,1},{4,6},{5,7},{6,4},{7,5},{8,10},{9,11},{10,... | collective-permute-start | bytes 884744 | tf_op jit(solution)/shard_map/ppermute | solution.py:457
  53.0 19.6 %collective-permute-start.7 = (bf16[128,1152]{1,0:T(8,128)(2,1)S(1)}, bf16[128,1152]{1,0:T(8,128)(2,1)S(1)}, u32[]{:S(2)}, u32[]{:S(2)}) collective-permute-start(bf16[128,1152]{1,0:T(8,128)(2,1)S(1)} %get-tuple-element.58), channel_id=1, source_target_pairs={{0,3},{1,2},{2,1},{3,0},{4,7},{5,6},{6,5},{7,4},{8,11},{9,10},{10,... | collective-permute-start | bytes 884744 | tf_op jit(solution)/shard_map/ppermute | solution.py:457

commit v9 on v7

--- a/solution.py
+++ b/solution.py
@@ -439,7 +439,8 @@
 
     def share(parts):
         moves = [[(d, d ^ k) for d in range(4)] for k in range(4)]
-        return parts[0:1] + [lax.ppermute(parts[k], ("yl", "c"), moves[k]) for k in range(1, 4)]
+        sent = {k: lax.ppermute(parts[k], ("yl", "c"), moves[k]) for k in (2, 3, 1)}
+        return parts[0:1] + [sent[k] for k in range(1, 4)]
 
     early = list(early)
     flat, early[0] = lax.optimization_barrier((flat, early[0]))

time: 77.3 us -> 77.3 us (level)
  no operation moved by 1% of the time
where the time goes in v9:
time: 77.3 us; the launch traced here: 77 us
  blocking collectives  42.3 us (55%)
  Pallas kernels  13.9 us (18%)
  starting transfers between devices  13.8 us (18%)
  local copies, waits for them, and re-layouts  4.34 us (6%)
  between operations  2.02 us (3%)
    all_to_all x1, blocking collectives, on_device(): own = lax.all_to_all(payload, ('x', 'zh'), 0, 0, tiled=True)  24.4 us
    all_to_all x1, blocking collectives, on_device(): stats_all = lax.all_to_all(stats, AXES, 0, 0, tiled=True)  17.9 us
    ppermute x6, starting transfers between devices, share(): sent = {k: lax.ppermute(parts[k], ('yl', 'c'), moves[k]) for k in (2, 3, 1)}  8.69 us
    pallas_call x1, Pallas kernels, on_device(): pl.pallas_call(functools.partial(final_kernel, scale=scale), in_specs=[sm...  4.45 us
    unnamed x11, local copies, waits for them, and re-layouts  4.25 us
    pallas_call x1, Pallas kernels, on_device(): pl.pallas_call(score_kernel, in_specs=[smem] + [vmem] * 8, out_specs=[vme...  3.86 us
    ppermute x1, starting transfers between devices, on_device(): far = lax.ppermute(own, ('yh', 'yl'), flip)  2.73 us
    pallas_call x1, Pallas kernels, on_device(): pl.pallas_call(prep_kernel, in_specs=[smem] * 3 + [hbm] * 3, out_specs=vm...  2.52 us
  transfers between devices with their start and end apart: 9, of which 1 were waited for; matrix products, arithmetic and copies ran while one was open for 4% of the time, Pallas kernels for 9%

profile of v9, /device:TPU:1, one launch (start us, length us, event | category | flops | bytes accessed | tf_op | source)
XLA Modules:
  0.0 77.0 jit_solution(18058428068482686267)
XLA Ops:
  1.9 2.5 %prep.1 = bf16[128,1152]{1,0:T(8,128)(2,1)} custom-call(s32[2,9]{1,0:T(2,128)} %bitcast.33, s32[1]{0:T(128)S(6)} %copy.15.groups, s32[1]{0:T(128)S(6)} %copy.16.defocus, bf16[1,2,4096]{2,1,0:T(2,128)(2,1)} %image_hbm.1, f32[8,4096]{1,0:T(8,128)} %noise_ref, f32[64,4096]{1,0:T(8,128)} %ctf_ref), custom_call_target="tpu_custom_call" | custom-call | tf_op jit(solution)/shard_map/prep/pallas_call | solution.py:398
  4.4 24.4 %all_to_all.22 = bf16[16,8,1152]{2,1,0:T(8,128)(2,1)S(1)} all-to-all(bf16[16,8,1152]{2,1,0:T(8,128)(2,1)} %bitcast.32), channel_id=1, replica_groups=mesh['x'=4,'yh'=2,'zh'=4,'zl'=2,'yl'=2,'c'=2] {'x','zh'}, dimensions={0} | all-to-all | bytes 589824 | tf_op jit(solution)/shard_map/all_to_all | solution.py:413
  28.9 2.7 %collective-permute-start.1 = (bf16[128,1152]{1,0:T(8,128)(2,1)S(1)}, bf16[128,1152]{1,0:T(8,128)(2,1)S(1)}, u32[]{:S(2)}, u32[]{:S(2)}) collective-permute-start(bf16[128,1152]{1,0:T(8,128)(2,1)S(1)} %bitcast.24), channel_id=1, source_target_pairs={{0,34},{2,32},{32,2},{34,0},{1,35},{3,33},{33,3},{35,1},{4,38},{6,... | collective-permute-start | bytes 884744 | tf_op jit(solution)/shard_map/ppermute | solution.py:415
  31.6 0.9 %collective-permute-start = (bf16[128,1152]{1,0:T(8,128)(2,1)S(1)}, bf16[128,1152]{1,0:T(8,128)(2,1)S(1)}, u32[]{:S(2)}, u32[]{:S(2)}) collective-permute-start(bf16[128,1152]{1,0:T(8,128)(2,1)S(1)} %bitcast.25), channel_id=1, source_target_pairs={{0,4},{4,0},{1,5},{5,1},{2,6},{6,2},{3,7},{7,3},{8,12},{12,8},{9,1... | collective-permute-start | bytes 884744 | tf_op jit(solution)/shard_map/ppermute | solution.py:414
  32.5 3.0 %copy.14 = bf16[16,8,2,4096]{3,1,2,0:T(8,128)(2,1)S(1)} copy(bf16[16,8,2,4096]{3,2,1,0:T(2,128)(2,1)} %bitcast.31) | data formatting | bytes 4194304
  35.5 0.3 tables.1.tables_ref
  35.9 0.0 copy-start
  35.9 1.3 %copy-done = bf16[224,4096]{1,0:T(8,128)(2,1)} copy-done((bf16[224,4096]{1,0:T(8,128)(2,1)}, bf16[224,4096]{1,0:T(8,128)(2,1)S(1)}, u32[]{:S(2)}) %copy-start) | copy-done | bytes 1835032
  37.1 0.0 collective-permute-done.1.far_ref
  37.1 0.6 collective-permute-done.side_ref
  37.8 1.5 %collective-permute-start.5 = (bf16[128,1152]{1,0:T(8,128)(2,1)S(1)}, bf16[128,1152]{1,0:T(8,128)(2,1)S(1)}, u32[]{:S(2)}, u32[]{:S(2)}) collective-permute-start(bf16[128,1152]{1,0:T(8,128)(2,1)S(1)} %collective-permute-done.side_ref), channel_id=1, source_target_pairs={{0,34},{2,32},{32,2},{34,0},{1,35},{3,33},{33,3},{35,1},{4,38},{6,... | collective-permute-start | bytes 884744 | tf_op jit(solution)/shard_map/ppermute | solution.py:428
  39.3 0.1 stack.23.place
  39.3 0.8 %quarters.1 = (bf16[64,1152]{1,0:T(8,128)(2,1)S(1)}, bf16[64,1152]{1,0:T(8,128)(2,1)S(1)}, bf16[64,1152]{1,0:T(8,128)(2,1)S(1)}, bf16[64,1152]{1,0:T(8,128)(2,1)S(1)}) custom-call(s32[5]{0:T(128)S(1)} %stack.23.place, bf16[128,1152]{1,0:T(8,128)(2,1)S(1)} %bitcast.26, bf16[128,1152]{1,0:T(8,128)(2,1)S(1)} %collective-permute-done.side_ref, ...), custom_call_target="tpu_custom_call" | custom-call | tf_op jit(solution)/shard_map/quarters/pallas_call | solution.py:430
  40.2 3.4 %collective-permute-start.2 = (bf16[64,1152]{1,0:T(8,128)(2,1)S(1)}, bf16[64,1152]{1,0:T(8,128)(2,1)S(1)}, u32[]{:S(2)}, u32[]{:S(2)}) collective-permute-start(bf16[64,1152]{1,0:T(8,128)(2,1)S(1)} %get-tuple-element.38), channel_id=1, source_target_pairs={{0,1},{1,0},{2,3},{3,2},{4,5},{5,4},{6,7},{7,6},{8,9},{9,8},{10,11... | collective-permute-start | bytes 442376 | tf_op jit(solution)/shard_map/ppermute | solution.py:442
  43.5 0.0 collective-permute-start.3
  43.5 1.7 %collective-permute-start.4 = (bf16[64,1152]{1,0:T(8,128)(2,1)S(1)}, bf16[64,1152]{1,0:T(8,128)(2,1)S(1)}, u32[]{:S(2)}, u32[]{:S(2)}) collective-permute-start(bf16[64,1152]{1,0:T(8,128)(2,1)S(1)} %get-tuple-element.40), channel_id=1, source_target_pairs={{0,3},{1,2},{2,1},{3,0},{4,7},{5,6},{6,5},{7,4},{8,11},{9,10},{10,... | collective-permute-start | bytes 442376 | tf_op jit(solution)/shard_map/ppermute | solution.py:442
  45.2 0.0 copy-done.4
  45.2 1.9 %turn_refs.1 = (bf16[2,384,4096]{2,1,0:T(8,128)(2,1)S(1)}, bf16[128,4096]{1,0:T(8,128)(2,1)S(1)}, f32[128,128]{1,0:T(8,128)S(1)}) custom-call(bf16[128,8192]{1,0:T(8,128)(2,1)S(1)} %bitcast.23, f32[1,128]{1,0:T(1,128)S(1)} %bitcast.30), custom_call_target="tpu_custom_call" | custom-call | flops 4194304 | bytes 10485760 | tf_op jit(solution)/shard_map/turn_refs/pallas_call | solution.py:447
  47.2 0.0 collective-permute-done.5.corner_ref
  47.2 0.0 copy-done.1
  47.2 3.9 %score.1 = (bf16[128,1152]{1,0:T(8,128)(2,1)S(1)}, bf16[128,1152]{1,0:T(8,128)(2,1)S(1)}, bf16[128,1152]{1,0:T(8,128)(2,1)S(1)}, bf16[128,1152]{1,0:T(8,128)(2,1)S(1)}, f32[256,128]{1,0:T(8,128)S(1)}) custom-call(s32[5]{0:T(128)S(1)} %stack.23.place, bf16[128,1152]{1,0:T(8,128)(2,1)S(1)} %bitcast.27, bf16[128,1152]{1,0:T(8,128)(2,1)S(1)} %collective-permute-done.side_ref, ...), custom_call_target="tpu_custom_call" | custom-call | flops 1207959552 | bytes 10485760 | tf_op jit(solution)/shard_map/score/pallas_call | solution.py:464
  51.1 1.9 %collective-permute-start.6 = (bf16[128,1152]{1,0:T(8,128)(2,1)S(1)}, bf16[128,1152]{1,0:T(8,128)(2,1)S(1)}, u32[]{:S(2)}, u32[]{:S(2)}) collective-permute-start(bf16[128,1152]{1,0:T(8,128)(2,1)S(1)} %get-tuple-element.52), channel_id=1, source_target_pairs={{0,1},{1,0},{2,3},{3,2},{4,5},{5,4},{6,7},{7,6},{8,9},{9,8},{10,11... | collective-permute-start | bytes 884744 | tf_op jit(solution)/shard_map/ppermute | solution.py:442
  52.9 0.0 collective-permute-start.7
  52.9 0.0 collective-permute-done.2.e1_ref
  52.9 1.7 %collective-permute-start.8 = (bf16[128,1152]{1,0:T(8,128)(2,1)S(1)}, bf16[128,1152]{1,0:T(8,128)(2,1)S(1)}, u32[]{:S(2)}, u32[]{:S(2)}) collective-permute-start(bf16[128,1152]{1,0:T(8,128)(2,1)S(1)} %get-tuple-element.54), channel_id=1, source_target_pairs={{0,3},{1,2},{2,1},{3,0},{4,7},{5,6},{6,5},{7,4},{8,11},{9,10},{10,... | collective-permute-start | bytes 884744 | tf_op jit(solution)/shard_map/ppermute | solution.py:442
  54.7 0.0 collective-permute-done.3.e2_ref
  54.7 0.0 collective-permute-done.4.e3_ref
  54.7 17.9 %all_to_all.23 = f32[256,1,128]{2,1,0:T(1,128)S(1)} all-to-all(f32[256,1,128]{2,1,0:T(1,128)S(1)} %bitcast.29), channel_id=1, replica_groups=mesh['x'=4,'yh'=2,'zh'=4,'zl'=2,'yl'=2,'c'=2] {'x','yh','zh','zl','yl','c'}, dimensions={0} | all-to-all | bytes 262144 | tf_op jit(solution)/shard_map/all_to_all | solution.py:480
  72.6 0.0 collective-permute-done.6.q1_ref
  72.6 0.0 collective-permute-done.7.q2_ref
  72.6 0.0 collective-permute-done.8.q3_ref
  72.6 4.5 %insert.1 = (f32[128,16,128]{2,1,0:T(8,128)}, f32[128,1024]{1,0:T(8,128)}, f32[1]{0:T(128)}) custom-call(s32[5]{0:T(128)S(1)} %stack.23.place, bf16[64,1152]{1,0:T(8,128)(2,1)S(1)} %get-tuple-element.47.e0_ref, bf16[64,1152]{1,0:T(8,128)(2,1)S(1)} %collective-permute-done.2.e1_ref, bf16[64,1152]{1,0:T(8,128)(2,1)S(1)} %collective-permute-done.3.e2_ref, ...), custom_call_target="tpu_custom_call" | custom-call | tf_op jit(solution)/shard_map/insert/pallas_call | solution.py:482
  (6 shorter events, 0.0 us)
Async XLA Ops:
  28.9 8.2 %collective-permute-start.1 = (bf16[128,1152]{1,0:T(8,128)(2,1)S(1)}, bf16[128,1152]{1,0:T(8,128)(2,1)S(1)}, u32[]{:S(2)}, u32[]{:S(2)}) collective-permute-start(bf16[128,1152]{1,0:T(8,128)(2,1)S(1)} %bitcast.24), channel_id=1, source_target_pairs={{0,34},{2,32},{32,2},{34,0},{1,35},{3,33},{33,3},{35,1},{4,38},{6,... | collective-permute-start | bytes 884744 | tf_op jit(solution)/shard_map/ppermute | solution.py:415
  31.6 6.1 %collective-permute-start = (bf16[128,1152]{1,0:T(8,128)(2,1)S(1)}, bf16[128,1152]{1,0:T(8,128)(2,1)S(1)}, u32[]{:S(2)}, u32[]{:S(2)}) collective-permute-start(bf16[128,1152]{1,0:T(8,128)(2,1)S(1)} %bitcast.25), channel_id=1, source_target_pairs={{0,4},{4,0},{1,5},{5,1},{2,6},{6,2},{3,7},{7,3},{8,12},{12,8},{9,1... | collective-permute-start | bytes 884744 | tf_op jit(solution)/shard_map/ppermute | solution.py:414
  32.5 3.0 %copy-start.2 = (f32[64,4096]{1,0:T(8,128)S(1)}, f32[64,4096]{1,0:T(8,128)}, u32[]{:S(2)}) copy-start(f32[64,4096]{1,0:T(8,128)} %ctf_ref) | copy-start | bytes 3145732
  32.5 3.0 %copy-start.3 = (f32[8,4096]{1,0:T(8,128)S(1)}, f32[8,4096]{1,0:T(8,128)}, u32[]{:S(2)}) copy-start(f32[8,4096]{1,0:T(8,128)} %noise_ref) | copy-start | bytes 393220
  35.9 1.3 %copy-start = (bf16[224,4096]{1,0:T(8,128)(2,1)}, bf16[224,4096]{1,0:T(8,128)(2,1)S(1)}, u32[]{:S(2)}) copy-start(bf16[224,4096]{1,0:T(8,128)(2,1)S(1)} %tables.1.tables_ref) | copy-start | bytes 5505028
  37.1 8.1 %copy-start.4 = (f32[128]{0:T(128)S(1)}, f32[128]{0:T(128)}, u32[]{:S(2)}) copy-start(f32[128]{0:T(128)} %param.13) | copy-start | bytes 1540
  37.8 9.4 %collective-permute-start.5 = (bf16[128,1152]{1,0:T(8,128)(2,1)S(1)}, bf16[128,1152]{1,0:T(8,128)(2,1)S(1)}, u32[]{:S(2)}, u32[]{:S(2)}) collective-permute-start(bf16[128,1152]{1,0:T(8,128)(2,1)S(1)} %collective-permute-done.side_ref), channel_id=1, source_target_pairs={{0,34},{2,32},{32,2},{34,0},{1,35},{3,33},{33,3},{35,1},{4,38},{6,... | collective-permute-start | bytes 884744 | tf_op jit(solution)/shard_map/ppermute | solution.py:428
  39.3 7.9 %copy-start.1 = (bf16[224,4096]{1,0:T(8,128)(2,1)S(1)}, bf16[224,4096]{1,0:T(8,128)(2,1)}, u32[]{:S(2)}) copy-start(bf16[224,4096]{1,0:T(8,128)(2,1)} %copy-done) | copy-start | bytes 5505028
  40.2 12.8 %collective-permute-start.2 = (bf16[64,1152]{1,0:T(8,128)(2,1)S(1)}, bf16[64,1152]{1,0:T(8,128)(2,1)S(1)}, u32[]{:S(2)}, u32[]{:S(2)}) collective-permute-start(bf16[64,1152]{1,0:T(8,128)(2,1)S(1)} %get-tuple-element.38), channel_id=1, source_target_pairs={{0,1},{1,0},{2,3},{3,2},{4,5},{5,4},{6,7},{7,6},{8,9},{9,8},{10,11... | collective-permute-start | bytes 442376 | tf_op jit(solution)/shard_map/ppermute | solution.py:442
  43.5 11.2 %collective-permute-start.3 = (bf16[64,1152]{1,0:T(8,128)(2,1)S(1)}, bf16[64,1152]{1,0:T(8,128)(2,1)S(1)}, u32[]{:S(2)}, u32[]{:S(2)}) collective-permute-start(bf16[64,1152]{1,0:T(8,128)(2,1)S(1)} %get-tuple-element.39), channel_id=1, source_target_pairs={{0,2},{1,3},{2,0},{3,1},{4,6},{5,7},{6,4},{7,5},{8,10},{9,11},{10,... | collective-permute-start | bytes 442376 | tf_op jit(solution)/shard_map/ppermute | solution.py:442
  43.5 11.2 %collective-permute-start.4 = (bf16[64,1152]{1,0:T(8,128)(2,1)S(1)}, bf16[64,1152]{1,0:T(8,128)(2,1)S(1)}, u32[]{:S(2)}, u32[]{:S(2)}) collective-permute-start(bf16[64,1152]{1,0:T(8,128)(2,1)S(1)} %get-tuple-element.40), channel_id=1, source_target_pairs={{0,3},{1,2},{2,1},{3,0},{4,7},{5,6},{6,5},{7,4},{8,11},{9,10},{10,... | collective-permute-start | bytes 442376 | tf_op jit(solution)/shard_map/ppermute | solution.py:442
  51.1 21.5 %collective-permute-start.6 = (bf16[128,1152]{1,0:T(8,128)(2,1)S(1)}, bf16[128,1152]{1,0:T(8,128)(2,1)S(1)}, u32[]{:S(2)}, u32[]{:S(2)}) collective-permute-start(bf16[128,1152]{1,0:T(8,128)(2,1)S(1)} %get-tuple-element.52), channel_id=1, source_target_pairs={{0,1},{1,0},{2,3},{3,2},{4,5},{5,4},{6,7},{7,6},{8,9},{9,8},{10,11... | collective-permute-start | bytes 884744 | tf_op jit(solution)/shard_map/ppermute | solution.py:442
  52.9 19.6 %collective-permute-start.7 = (bf16[128,1152]{1,0:T(8,128)(2,1)S(1)}, bf16[128,1152]{1,0:T(8,128)(2,1)S(1)}, u32[]{:S(2)}, u32[]{:S(2)}) collective-permute-start(bf16[128,1152]{1,0:T(8,128)(2,1)S(1)} %get-tuple-element.53), channel_id=1, source_target_pairs={{0,2},{1,3},{2,0},{3,1},{4,6},{5,7},{6,4},{7,5},{8,10},{9,11},{10,... | collective-permute-start | bytes 884744 | tf_op jit(solution)/shard_map/ppermute | solution.py:442
  52.9 19.6 %collective-permute-start.8 = (bf16[128,1152]{1,0:T(8,128)(2,1)S(1)}, bf16[128,1152]{1,0:T(8,128)(2,1)S(1)}, u32[]{:S(2)}, u32[]{:S(2)}) collective-permute-start(bf16[128,1152]{1,0:T(8,128)(2,1)S(1)} %get-tuple-element.54), channel_id=1, source_target_pairs={{0,3},{1,2},{2,1},{3,0},{4,7},{5,6},{6,5},{7,4},{8,11},{9,10},{10,... | collective-permute-start | bytes 884744 | tf_op jit(solution)/shard_map/ppermute | solution.py:442
